TPU v7x, 32 devices: a whole 2x2x4 slice. The times are simulated.
32 devices in a mesh: dp: 8 (over y, x, core), mp: 4 (over z).
Axes of the slice: x: 2, y: 2, z: 4, core: 2. Of those that a mesh axis runs over, the one named last changes fastest.
Arguments:
- tokens: bfloat16 [10240, 768], P(('dp', 'mp')), may hold values from -6 to 6
- segment_ids: int32 [64, 160], P('dp'), may hold values from 0 to 3, as said below
- live_mask: int32 [64, 160], P('dp'), may hold values from 0 to 1, as said below
- query_weight: bfloat16 [768, 768], P(None, 'mp'), may hold values from -0.21875 to 0.21875
- key_weight: bfloat16 [768, 768], P(None, 'mp'), may hold values from -0.21875 to 0.21875
- value_weight: bfloat16 [768, 768], P(None, 'mp'), may hold values from -0.21875 to 0.21875
- query_bias: bfloat16 [768], P('mp'), may hold values from -3 to 3
- value_bias: bfloat16 [768], P('mp'), may hold values from -3 to 3
- output_weight: bfloat16 [768, 768], P('mp'), may hold values from -1.25 to 1.25
- output_bias: bfloat16 [768], replicated, may hold values from -3 to 3
- first_gain: bfloat16 [768], replicated, may hold values from 0.5 to 1.5
- first_shift: bfloat16 [768], replicated, may hold values from -3 to 3
- inner_weight: bfloat16 [768, 3072], P(None, 'mp'), may hold values from -0.21875 to 0.21875
- inner_bias: bfloat16 [3072], P('mp'), may hold values from -3 to 3
- outer_weight: bfloat16 [3072, 768], P('mp'), may hold values from -0.109375 to 0.109375
- outer_bias: bfloat16 [768], replicated, may hold values from -3 to 3
- second_gain: bfloat16 [768], replicated, may hold values from 0.5 to 1.5
- second_shift: bfloat16 [768], replicated, may hold values from -3 to 3
- cotangent: bfloat16 [10240, 768], P(('dp', 'mp')), may hold values from -6 to 6
Outputs:
- output: bfloat16 [10240, 768], P(('dp', 'mp'))
- input_grad: bfloat16 [10240, 768], P(('dp', 'mp'))
- query_weight_grad: float32 [768, 768], P(None, 'mp')
- key_weight_grad: float32 [768, 768], P(None, 'mp')
- value_weight_grad: float32 [768, 768], P(None, 'mp')
- query_bias_grad: float32 [768], P('mp')
- value_bias_grad: float32 [768], P('mp')
- output_weight_grad: float32 [768, 768], P('mp')
- output_bias_grad: float32 [768], replicated
- first_gain_grad: float32 [768], replicated
- first_shift_grad: float32 [768], replicated
- inner_weight_grad: float32 [768, 3072], P(None, 'mp')
- inner_bias_grad: float32 [3072], P('mp')
- outer_weight_grad: float32 [3072, 768], P('mp')
- outer_bias_grad: float32 [768], replicated
- second_gain_grad: float32 [768], replicated
- second_shift_grad: float32 [768], replicated
Inputs may be any that keep to these rules, and one draw needn't show every extreme that they name: `segment_ids`: each row packs one to four chains: ids never fall along a row, start at 0 and take every value up to the row's number of chains less one; padding after a row's live tokens keeps the last chain's id; every chain has 16 or more live tokens; row 0 holds four chains. `live_mask`: 1 on a row's leading live tokens, 0 on the padding after them, at most 40 padding tokens a row; row 0 has padding.
All inputs are finite; a program needn't handle non-finite values.
Results may differ from a plain program's by a relative error of at most 0.02.
Values may be sent and summed in bfloat16 or wider, within the bound.
A program may use at most 128 MiB of HBM per device.

v0:
```python
import math

import jax
import jax.numpy as jnp
from jax import lax
from jax.sharding import PartitionSpec as P

DH = 64
SEQ = 160


EPSILON = 1e-06
NEG_FILL = -1000000000.0
ROOT_HALF = 0.7071067811865476


def layer_norm(summed, gain_row, shift_row):
    centre_mean = jnp.mean(summed, -1, keepdims=True)
    centred = summed - centre_mean
    variance = jnp.mean(centred * centred, -1, keepdims=True)
    return centred * lax.rsqrt(variance + EPSILON) * gain_row + shift_row


def gelu_exact(values):
    return 0.5 * values * (1.0 + lax.erf(values * ROOT_HALF))


def column_product(left, right):
    return lax.dot_general(
        left, right, (((0,), (0,)), ((), ())), preferred_element_type=jnp.float32
    )


def right_transpose(left, right):
    return lax.dot_general(
        left, right, (((1,), (1,)), ((), ())), preferred_element_type=jnp.float32
    )


def per_device(
    tokens,
    segment_ids,
    live_mask,
    query_weight,
    key_weight,
    value_weight,
    query_bias,
    value_bias,
    output_weight,
    output_bias,
    first_gain,
    first_shift,
    inner_weight,
    inner_bias,
    outer_weight,
    outer_bias,
    second_gain,
    second_shift,
    cotangent,
):
    seq_rows = segment_ids.shape[0]
    heads_here = query_weight.shape[1] // DH
    block_rows = math.gcd(seq_rows, 4)
    blocks = seq_rows // block_rows
    score_scale = DH ** (-0.5)
    allowed = (segment_ids[:, :, None] == segment_ids[:, None, :]) & (live_mask[:, None, :] == 1)
    allowed_blk = allowed.reshape(blocks, block_rows, SEQ, SEQ)

    def split_heads(row_array):
        return row_array.reshape(blocks, block_rows, SEQ, heads_here, DH)

    def join_heads(block_array):
        return block_array.reshape(seq_rows * SEQ, heads_here * DH)

    group_tokens = lax.all_gather(tokens, "mp", axis=0, tiled=True)
    queries = (
        jnp.dot(group_tokens, query_weight, preferred_element_type=jnp.float32)
        + query_bias.astype(jnp.float32)
    ).astype(jnp.bfloat16)
    key_rows = jnp.dot(group_tokens, key_weight, preferred_element_type=jnp.float32).astype(
        jnp.bfloat16
    )
    value_rows = (
        jnp.dot(group_tokens, value_weight, preferred_element_type=jnp.float32)
        + value_bias.astype(jnp.float32)
    ).astype(jnp.bfloat16)

    def masked_scores(query_blk, key_blk, mask_blk):
        scores = (
            jnp.einsum("rqhd,rkhd->rhqk", query_blk, key_blk, preferred_element_type=jnp.float32)
            * score_scale
        )
        return jnp.where(mask_blk[:, None], scores, NEG_FILL)

    def forward_block(block_item):
        query_blk, key_blk, value_blk, mask_blk = block_item
        scores = masked_scores(query_blk, key_blk, mask_blk)
        row_max = jnp.max(scores, -1, keepdims=True)
        exponent = jnp.exp(scores - row_max)
        row_total = jnp.sum(exponent, -1, keepdims=True)
        prob_rows = (exponent / row_total).astype(jnp.bfloat16)
        context_blk = jnp.einsum(
            "rhqk,rkhd->rqhd", prob_rows, value_blk, preferred_element_type=jnp.float32
        )
        return (context_blk.astype(jnp.bfloat16), row_max + jnp.log(row_total))

    query_split = split_heads(queries)
    key_split = split_heads(key_rows)
    value_split = split_heads(value_rows)
    context_split, log_total = lax.map(
        forward_block, (query_split, key_split, value_split, allowed_blk)
    )
    context = join_heads(context_split)
    rows_blk = context
    attn_total = lax.psum_scatter(
        jnp.dot(rows_blk, output_weight, preferred_element_type=jnp.float32),
        "mp",
        scatter_dimension=0,
        tiled=True,
    )
    first_sum = attn_total + output_bias.astype(jnp.float32) + tokens.astype(jnp.float32)
    first_normed, first_pull = jax.vjp(
        layer_norm, first_sum, first_gain.astype(jnp.float32), first_shift.astype(jnp.float32)
    )
    normed_bf = first_normed.astype(jnp.bfloat16)
    group_normed = lax.all_gather(normed_bf, "mp", axis=0, tiled=True)
    inner_pre = jnp.dot(
        group_normed, inner_weight, preferred_element_type=jnp.float32
    ) + inner_bias.astype(jnp.float32)
    activated, gelu_pull = jax.vjp(gelu_exact, inner_pre)
    activated_bf = activated.astype(jnp.bfloat16)
    rows_blk = activated_bf
    ffn_total = lax.psum_scatter(
        jnp.dot(rows_blk, outer_weight, preferred_element_type=jnp.float32).astype(jnp.bfloat16),
        "mp",
        scatter_dimension=0,
        tiled=True,
    ).astype(jnp.float32)
    second_sum = ffn_total + outer_bias.astype(jnp.float32) + first_normed
    result, second_pull = jax.vjp(
        layer_norm, second_sum, second_gain.astype(jnp.float32), second_shift.astype(jnp.float32)
    )
    second_grad, second_gain_grad, second_shift_grad = second_pull(cotangent.astype(jnp.float32))
    outer_bias_grad = jnp.sum(second_grad, 0)
    tokens_back, normed_back = (
        lax.all_gather(tokens, "mp", axis=0, tiled=True),
        lax.all_gather(normed_bf, "mp", axis=0, tiled=True),
    )
    group_second = lax.all_gather(second_grad.astype(jnp.bfloat16), "mp", axis=0, tiled=True)
    outer_weight_grad = column_product(activated_bf, group_second)
    activated_grad = right_transpose(group_second, outer_weight)
    (inner_grad,) = gelu_pull(activated_grad)
    inner_bf = inner_grad.astype(jnp.bfloat16)
    inner_bias_grad = jnp.sum(inner_bf, 0, dtype=jnp.float32)
    inner_weight_grad = column_product(normed_back, inner_bf)
    rows_blk = inner_bf
    hidden_total = lax.psum_scatter(
        right_transpose(rows_blk, inner_weight).astype(jnp.bfloat16),
        "mp",
        scatter_dimension=0,
        tiled=True,
    ).astype(jnp.float32)
    first_grad, first_gain_grad, first_shift_grad = first_pull(hidden_total + second_grad)
    output_bias_grad = jnp.sum(first_grad, 0)
    group_first = lax.all_gather(first_grad.astype(jnp.bfloat16), "mp", axis=0, tiled=True)
    output_weight_grad = column_product(context, group_first)
    context_grad = right_transpose(group_first, output_weight).astype(jnp.bfloat16)

    def backward_block(block_item):
        query_blk, key_blk, value_blk, mask_blk, lse_blk, grad_blk = block_item
        scores = masked_scores(query_blk, key_blk, mask_blk)
        prob_rows = jnp.exp(scores - lse_blk)
        value_grad = jnp.einsum(
            "rhqk,rqhd->rkhd",
            prob_rows.astype(jnp.bfloat16),
            grad_blk,
            preferred_element_type=jnp.float32,
        )
        prob_grad = jnp.einsum(
            "rqhd,rkhd->rhqk", grad_blk, value_blk, preferred_element_type=jnp.float32
        )
        inner_sum = jnp.sum(prob_rows * prob_grad, -1, keepdims=True)
        score_grad = (prob_rows * (prob_grad - inner_sum)).astype(jnp.bfloat16)
        query_grad = (
            jnp.einsum("rhqk,rkhd->rqhd", score_grad, key_blk, preferred_element_type=jnp.float32)
            * score_scale
        )
        key_grad = (
            jnp.einsum("rhqk,rqhd->rkhd", score_grad, query_blk, preferred_element_type=jnp.float32)
            * score_scale
        )
        return (
            query_grad.astype(jnp.bfloat16),
            key_grad.astype(jnp.bfloat16),
            value_grad.astype(jnp.bfloat16),
        )

    query_split_grad, key_split_grad, value_split_grad = lax.map(
        backward_block,
        (query_split, key_split, value_split, allowed_blk, log_total, split_heads(context_grad)),
    )
    query_grad = join_heads(query_split_grad)
    key_grad = join_heads(key_split_grad)
    value_grad = join_heads(value_split_grad)
    query_weight_grad = column_product(tokens_back, query_grad)
    key_weight_grad = column_product(tokens_back, key_grad)
    value_weight_grad = column_product(tokens_back, value_grad)
    query_bias_grad = jnp.sum(query_grad, 0, dtype=jnp.float32)
    value_bias_grad = jnp.sum(value_grad, 0, dtype=jnp.float32)
    query_blk = query_grad
    key_blk = key_grad
    value_blk = value_grad
    input_total = lax.psum_scatter(
        (
            right_transpose(query_blk, query_weight)
            + right_transpose(key_blk, key_weight)
            + right_transpose(value_blk, value_weight)
        ).astype(jnp.bfloat16),
        "mp",
        scatter_dimension=0,
        tiled=True,
    ).astype(jnp.float32)
    input_grad = (input_total + first_grad).astype(jnp.bfloat16)
    (
        query_weight_grad,
        key_weight_grad,
        value_weight_grad,
        query_bias_grad,
        value_bias_grad,
        output_weight_grad,
        inner_weight_grad,
        inner_bias_grad,
        outer_weight_grad,
    ) = lax.psum(
        (
            query_weight_grad,
            key_weight_grad,
            value_weight_grad,
            query_bias_grad,
            value_bias_grad,
            output_weight_grad,
            inner_weight_grad,
            inner_bias_grad,
            outer_weight_grad,
        ),
        "dp",
    )
    (
        first_gain_grad,
        first_shift_grad,
        output_bias_grad,
        second_gain_grad,
        second_shift_grad,
        outer_bias_grad,
    ) = lax.psum(
        (
            first_gain_grad,
            first_shift_grad,
            output_bias_grad,
            second_gain_grad,
            second_shift_grad,
            outer_bias_grad,
        ),
        ("dp", "mp"),
    )
    return (
        result.astype(jnp.bfloat16),
        input_grad,
        query_weight_grad,
        key_weight_grad,
        value_weight_grad,
        query_bias_grad,
        value_bias_grad,
        output_weight_grad,
        output_bias_grad,
        first_gain_grad,
        first_shift_grad,
        inner_weight_grad,
        inner_bias_grad,
        outer_weight_grad,
        outer_bias_grad,
        second_gain_grad,
        second_shift_grad,
    )


def solution(mesh):
    in_specs = (
        P(("dp", "mp"), None),
        P("dp", None),
        P("dp", None),
        P(None, "mp"),
        P(None, "mp"),
        P(None, "mp"),
        P("mp"),
        P("mp"),
        P("mp", None),
        P(),
        P(),
        P(),
        P(None, "mp"),
        P("mp"),
        P("mp", None),
        P(),
        P(),
        P(),
        P(("dp", "mp"), None),
    )
    out_specs = (
        P(("dp", "mp"), None),
        P(("dp", "mp"), None),
        P(None, "mp"),
        P(None, "mp"),
        P(None, "mp"),
        P("mp"),
        P("mp"),
        P("mp", None),
        P(),
        P(),
        P(),
        P(None, "mp"),
        P("mp"),
        P("mp", None),
        P(),
        P(),
        P(),
    )
    return jax.shard_map(
        per_device, mesh=mesh, in_specs=in_specs, out_specs=out_specs, check_vma=False
    )
```

profile of v0, /device:TPU:0, one launch (start us, length us, event | category | flops | bytes accessed | tf_op | source)
XLA Modules:
  0.0 611.0 jit_solution(2858507210493650658)
XLA Ops:
  11.2 44.7 %all-gather.5.cloned.1.call-done = bf16[1280,768]{1,0:T(8,128)(2,1)} async-done(((bf16[320,768]{1,0:T(8,128)(2,1)}), bf16[1280,768]{1,0:T(8,128)(2,1)}) %all-gather.5.cloned.1.call-update) | async-done | bytes 1966096 | tf_op jit(solution)/shard_map/all_gather | solution.py:75
  55.9 2.4 fusion.39
  60.3 2.4 fusion.40
  63.7 2.4 convolution_convert_fusion.5
  70.2 7.1 %while.26 = (s32[]{:T(128)}, bf16[2,4,160,3,64]{2,1,0,4,3:T(4,128)(2,1)}, f32[2,4,3,160,1]{3,2,1,4,0:T(4,128)S(1)}, bf16[2,4,160,3,64]{2,4,3,1,0:T(8,128)(2,1)},...) while((s32[]{:T(128)}, ...), condition=%wide.region_3.4_spmd, body=%wide.region_0.3_spmd.sunk | while | flops 82450560 | bytes 13274817 | solution.py:110
  77.3 3.0 reshape.171
  80.3 3.6 fusion.53
  84.7 71.0 %reduce-scatter.5.cloned.1.call-done = f32[320,768]{1,0:T(8,128)} async-done(((f32[1280,768]{1,0:T(8,128)}), f32[320,768]{1,0:T(8,128)}) %reduce-scatter.5.cloned.1.call-update) | async-done | bytes 983056 | tf_op jit(solution)/shard_map/reduce_scatter | solution.py:115
  159.4 43.8 %all-gather.7.cloned.1.call-done = bf16[1280,768]{1,0:T(8,128)(2,1)} async-done(((bf16[320,768]{1,0:T(8,128)(2,1)}), bf16[1280,768]{1,0:T(8,128)(2,1)}) %all-gather.7.cloned.1.call-update) | async-done | bytes 1966096 | tf_op jit(solution)/shard_map/all_gather | solution.py:126
  203.3 5.6 multiply_convert_fusion.1
  210.3 3.0 convolution_convert_fusion.3
  214.0 39.7 %reduce-scatter.7.cloned.1.call-done = bf16[320,768]{1,0:T(8,128)(2,1)} async-done(((bf16[1280,768]{1,0:T(8,128)(2,1)}), bf16[320,768]{1,0:T(8,128)(2,1)}) %reduce-scatter.7.cloned.1.call-update) | async-done | bytes 491536 | tf_op jit(solution)/shard_map/reduce_scatter | solution.py:133
  259.5 42.9 %all-gather.9.cloned.1.call-done = bf16[1280,768]{1,0:T(8,128)(2,1)} async-done(((bf16[320,768]{1,0:T(8,128)(2,1)}), bf16[1280,768]{1,0:T(8,128)(2,1)}) %all-gather.9.cloned.1.call-update) | async-done | bytes 1966096 | tf_op jit(solution)/shard_map/all_gather | solution.py:149
  302.4 5.5 convert_reduce_fusion
  309.3 3.0 convolution_convert_fusion.2
  312.3 40.4 %reduce-scatter.9.cloned.1.call-done = bf16[320,768]{1,0:T(8,128)(2,1)} async-done(((bf16[1280,768]{1,0:T(8,128)(2,1)}), bf16[320,768]{1,0:T(8,128)(2,1)}) %reduce-scatter.9.cloned.1.call-update) | async-done | bytes 491536 | tf_op jit(solution)/shard_map/reduce_scatter | solution.py:157
  358.7 42.7 %all-gather.11.cloned.1.call-done = bf16[1280,768]{1,0:T(8,128)(2,1)} async-done(((bf16[320,768]{1,0:T(8,128)(2,1)}), bf16[1280,768]{1,0:T(8,128)(2,1)}) %all-gather.11.cloned.1.call-update) | async-done | bytes 1966096 | tf_op jit(solution)/shard_map/all_gather | solution.py:165
  406.6 16.8 %while.27 = (s32[]{:T(128)}, bf16[2,4,160,3,64]{2,4,3,1,0:T(8,128)(2,1)}, bf16[2,4,160,3,64]{2,1,0,4,3:T(4,128)(2,1)}, bf16[2,4,160,3,64]{2,4,3,1,0:T(8,128)(2,1...) while((s32[]{:T(128)}, ...), condition=%wide.region_17.18_spmd, body=%wide.region_15.17_spmd.sunk | while | flops 199985280 | bytes 28557624 | solution.py:198
  423.3 2.4 reshape.174
  434.3 5.4 fusion.57
  439.8 3.2 fusion.56
  449.0 41.4 %all-reduce = (f32[768]{0:T(1024)}, f32[768]{0:T(1024)}, f32[768]{0:T(1024)}, f32[768]{0:T(1024)}, f32[768]{0:T(1024)}, /*index=5*/f32[768]{0:T(1024)}) all-reduce(f32[768]{0:T(1024)S(1)} %get-tuple-element.219, f32[768]{0:T(1024)S(1)} %get-tuple-element.148, ...), channel_id=1, replica_groups=mesh['dp'=8,'mp'=4] {'dp','mp'}, use_global_device_ids=true, to_apply=%region_28.29 | all-reduce | flops 4608 | bytes 36864 | tf_op jit(solution)/shard_map/psum | solution.py:255
  490.9 15.2 %all-reduce.1 = (f32[192]{0:T(256)}, f32[192]{0:T(256)}, f32[768]{0:T(1024)}) all-reduce(f32[192]{0:T(256)S(1)} %reduce_sum.216, f32[192]{0:T(256)S(1)} %reduce_sum.218, f32[768]{0:T(1024)S(1)} %get-tuple-element.204), channel_id=1, replica_groups=mesh['dp'=8,'mp'=4] {'dp'}, use_global_device_ids=true, to_apply=%region_23.24 | all-reduce | flops 1152 | bytes 9216 | tf_op jit(solution)/shard_map/psum | solution.py:234
  508.1 86.2 %all-reduce.5.cloned.1.call-done = (f32[768,192]{0,1:T(8,128)}, f32[768,192]{0,1:T(8,128)}, f32[768,192]{0,1:T(8,128)}, f32[192,768]{1,0:T(8,128)}, f32[768,768]{1,0:T(8,128)}, /*index=5*/f32[768,768]{1,0:T(8,128)}) async-done(((f32[768,192]{0,1:T(8,128)}, f32[768,192]{0,1:T(8,128)}, f32[768,192]{0,1:T(8,128)}, f32[192,768]{1,0:T(8,128)}, f32[768,768]{1,0:T(8,128)}, /*index=5*/f32[768,768]{1,0:T(8,128)}), ...) | async-done | bytes 7077904 | tf_op jit(solution)/shard_map/psum | solution.py:234
  (235 shorter events, 86.2 us)
Async XLA Ops:
  7.2 196.1 %copy-start = (bf16[768,768]{1,0:T(8,128)(2,1)S(1)}, bf16[768,768]{1,0:T(8,128)(2,1)}, u32[]{:S(2)}) copy-start(bf16[768,768]{1,0:T(8,128)(2,1)} %param.35) | copy-start | bytes 3538948
  7.2 48.7 %all-gather.5.cloned.1.call-start = ((), (), s32[]{:S(2)}) async-start(), calls=%async_computation.4 | async-start | bytes 2457600 | tf_op jit(solution)/shard_map/all_gather | solution.py:75
  7.9 147.7 %reduce-scatter.5.cloned.1.call-start = ((), (), s32[]{:S(2)}) async-start(), calls=%async_computation.5 | async-start | bytes 4915200 | tf_op jit(solution)/shard_map/reduce_scatter | solution.py:115
  70.2 10.1 %copy-start.36 = (bf16[192,768]{1,0:T(8,128)(2,1)S(1)}, bf16[192,768]{1,0:T(8,128)(2,1)}, u32[]{:S(2)}) copy-start(bf16[192,768]{1,0:T(8,128)(2,1)} %param.31) | copy-start | bytes 884740
  84.0 119.3 %all-gather.7.cloned.1.call-start = ((), (), s32[]{:S(2)}) async-start(), calls=%async_computation.6 | async-start | bytes 2457600 | tf_op jit(solution)/shard_map/all_gather | solution.py:126
  159.2 94.5 %reduce-scatter.7.cloned.1.call-start = ((), (), s32[]{:S(2)}) async-start(), calls=%async_computation.7 | async-start | bytes 2457600 | tf_op jit(solution)/shard_map/reduce_scatter | solution.py:133
  203.3 7.0 %copy-start.49 = (bf16[768,768]{1,0:T(8,128)(2,1)S(1)}, bf16[768,768]{1,0:T(8,128)(2,1)}, u32[]{:S(2)}) copy-start(bf16[768,768]{1,0:T(8,128)(2,1)} %param.37) | copy-start | bytes 3538948
  213.3 89.1 %all-gather.9.cloned.1.call-start = ((), (), s32[]{:S(2)}) async-start(), calls=%async_computation.8 | async-start | bytes 2457600 | tf_op jit(solution)/shard_map/all_gather | solution.py:149
  259.5 93.3 %reduce-scatter.9.cloned.1.call-start = ((), (), s32[]{:S(2)}) async-start(), calls=%async_computation.9 | async-start | bytes 2457600 | tf_op jit(solution)/shard_map/reduce_scatter | solution.py:157
  312.3 40.5 %copy-start.3 = (f32[320,768]{1,0:T(8,128)S(1)}, f32[320,768]{1,0:T(8,128)}, u32[]{:S(2)}) copy-start(f32[320,768]{1,0:T(8,128)} %copy-done.2) | copy-start | bytes 2949124
  312.3 89.1 %all-gather.11.cloned.1.call-start = ((), (), s32[]{:S(2)}) async-start(), calls=%async_computation.10 | async-start | bytes 2457600 | tf_op jit(solution)/shard_map/all_gather | solution.py:165
  358.4 147.7 %reduce-scatter.11.cloned.1.call-start = ((), (), s32[]{:S(2)}) async-start(), calls=%async_computation.11 | async-start | bytes 2457600 | tf_op jit(solution)/shard_map/reduce_scatter | solution.py:213
  423.3 5.0 copy-start.16
  434.0 5.8 copy-start.28
  434.0 160.3 %all-reduce.5.cloned.1.call-start = ((), (), s32[]{:S(2)}) async-start(), calls=%async_computation.12 | async-start | bytes 14155776 | tf_op jit(solution)/shard_map/psum | solution.py:234
  434.3 5.5 copy-start.31
  439.8 3.2 copy-start.9
  448.9 41.5 %copy-start.17 = (bf16[2,4,160,3,64]{2,4,3,1,0:T(8,128)(2,1)S(1)}, bf16[2,4,160,3,64]{2,4,3,1,0:T(8,128)(2,1)}, u32[]{:S(2)}) copy-start(bf16[2,4,160,3,64]{2,4,3,1,0:T(8,128)(2,1)} %get-tuple-element.113) | copy-start | bytes 1474564
  448.9 41.5 %copy-start.20 = (bf16[2,4,160,3,64]{2,4,3,1,0:T(8,128)(2,1)S(1)}, bf16[2,4,160,3,64]{2,4,3,1,0:T(8,128)(2,1)}, u32[]{:S(2)}) copy-start(bf16[2,4,160,3,64]{2,4,3,1,0:T(8,128)(2,1)} %get-tuple-element.111) | copy-start | bytes 1474564
  449.0 57.2 %copy-start.8 = (f32[320,768]{1,0:T(8,128)S(1)}, f32[320,768]{1,0:T(8,128)}, u32[]{:S(2)}) copy-start(f32[320,768]{1,0:T(8,128)} %copy-done.7) | copy-start | bytes 2949124
  594.4 4.1 copy-start.35
  594.4 4.9 copy-start.34
  596.4 3.7 copy-start.26
  600.1 3.9 copy-start.1
  (44 other events, 59.1 us)
Sparse Core Ops, SparseCore 0:
  9.6 46.2 all-gather.4
  84.1 71.5 reduce-scatter.4
  159.3 43.8 all-gather.6
  213.4 40.2 reduce-scatter.6
  259.6 42.7 all-gather.8
  312.4 40.2 reduce-scatter.8
  358.5 42.7 all-gather.10
  434.1 40.9 reduce-scatter.10
  480.4 113.9 all-reduce.4
where the time goes:
time: 620 us; the launch traced here: 611 us
  waiting for transfers between devices  412 us (66%)
  matrix products  57.6 us (9%)
  blocking collectives  56.6 us (9%)
  local copies, waits for them, and re-layouts  49.6 us (8%)
  other arithmetic  19 us (3%)
  between operations  14.7 us (2%)
    psum x1, waiting for transfers between devices, per_device(): lax.psum((query_weight_grad, key_weight_grad, value_weight_grad, query_bi...  86.2 us
    reduce_scatter x1, waiting for transfers between devices, per_device(): lax.psum_scatter(jnp.dot(rows_blk, output_weight, preferred_element_type=...  71 us
    all_gather x1, waiting for transfers between devices, per_device(): group_tokens = lax.all_gather(tokens, 'mp', axis=0, tiled=True)  44.7 us
    all_gather x1, waiting for transfers between devices, per_device(): group_normed = lax.all_gather(normed_bf, 'mp', axis=0, tiled=True)  43.8 us
    all_gather x1, waiting for transfers between devices, per_device(): lax.all_gather(second_grad.astype(jnp.bfloat16), 'mp', axis=0, tiled=True)  42.9 us
    all_gather x1, waiting for transfers between devices, per_device(): lax.all_gather(first_grad.astype(jnp.bfloat16), 'mp', axis=0, tiled=True)  42.7 us
    psum x1, blocking collectives, per_device(): lax.psum((first_gain_grad, first_shift_grad, output_bias_grad, second_gai...  41.4 us
    reduce_scatter x1, waiting for transfers between devices, per_device(): lax.psum_scatter(right_transpose(rows_blk, inner_weight).astype(jnp.bfloa...  40.4 us
  transfers between devices with their start and end apart: 9, of which 8 were waited for; matrix products, arithmetic and copies ran while one was open for 3% of the time, Pallas kernels for 0%

commit v1 on v0

v1 whole, which is shorter than its diff:
```python
import functools

import jax
import jax.numpy as jnp
from jax import lax
from jax.experimental import pallas as pl
from jax.experimental.pallas import tpu as pltpu
from jax.sharding import PartitionSpec as P

DH = 64
EPSILON = 1e-06
NEG_FILL = -1000000000.0
ROOT_HALF = 0.7071067811865476
PDF_SCALE = 0.3989422804014327
BF = jnp.bfloat16
F32 = jnp.float32
MESH = pl.DeviceIdType.MESH

NN = (((1,), (0,)), ((), ()))
NT = (((1,), (1,)), ((), ()))
TN = (((0,), (0,)), ((), ()))

ATT, INN, OUT = 0, 1, 2
V_OB, V_G1, V_S1, V_EB, V_G2, V_S2 = 8, 9, 10, 11, 12, 13


def dot(left, right, dims):
    return lax.dot_general(left, right, dims, preferred_element_type=F32)


def layer_kernel(
    cfg,
    tok, cot, wq, wk, wv, wo, wi, wout, vin, seg, live,
    out_ref, dx_ref, grad_ref, vec_ref,
    wbuf, bias, xs, cots, qkv, ka, ks, prob, mask, acc, tmp, nh1, r1,
    nb, nhalf, af, asib, al, gp, g, sg, di, fg, fgf,
    gr, rf, rz1, rz2, rs, rx, vrecv,
    loc_sem, ag_s, ag_r, gr_s, gr_r, x_s, x_r, b_s, b_r, v_s, v_r, e_s, e_r,
):
    n_dp, d, seq, rows = cfg["dp"], cfg["d"], cfg["seq"], cfg["rows"]
    tl = seq * rows
    ml = d // 4
    hs = ml // DH
    half, qtr, eig = d // 2, d // 4, d // 8
    scale = DH ** (-0.5)
    bits = n_dp.bit_length() - 1
    dp, z = lax.axis_index("dp"), lax.axis_index("mp")
    c = dp % 2
    df = 2 + 2 * c
    ds_ = 6 - df
    f, s = (dp // df) % 2, (dp // ds_) % 2
    p_f, p_s, p_c = dp + df * (1 - 2 * f), dp + ds_ * (1 - 2 * s), dp + 1 - 2 * c
    z0, zh = z % 2, z // 2
    z1, z2, z3 = z + 1 - 2 * z0, z + 2 - 4 * zh, 3 - z
    h0 = pl.multiple_of(c * half, 128)
    ho = pl.multiple_of((1 - c) * half, 128)
    q0 = pl.multiple_of(c * half + f * qtr, 16)
    e0 = pl.multiple_of(c * half + f * qtr + s * eig, 16)
    qo = pl.multiple_of(c * half + (1 - f) * qtr, 16)
    eo = pl.multiple_of(c * half + f * qtr + (1 - s) * eig, 16)
    shard = (z, z1, z2, z3)

    def shard_of(k):
        k0, kh = k % 2, k // 2
        return z0 + k0 - 2 * z0 * k0 + 2 * (zh + kh - 2 * zh * kh)

    def remote(src, dst, ssem, rsem, dev):
        return pltpu.make_async_remote_copy(
            src_ref=src, dst_ref=dst, send_sem=ssem, recv_sem=rsem, device_id=dev, device_id_type=MESH
        )

    pending = []

    def send(make):
        remote(*make()).start()
        pending.append(make)

    loads = [
        pltpu.make_async_copy(tok, xs.at[pl.ds(0, rows)], loc_sem.at[0]),
        pltpu.make_async_copy(wo, wbuf.at[ATT, z, pl.ds(3 * ml, ml)], loc_sem.at[1]),
        pltpu.make_async_copy(wi, wbuf.at[INN, z], loc_sem.at[2]),
        pltpu.make_async_copy(wout, wbuf.at[OUT, z], loc_sem.at[3]),
        pltpu.make_async_copy(cot, cots, loc_sem.at[4]),
    ]
    for cp in loads:
        cp.start()
    barrier = pltpu.get_barrier_semaphore()
    extra = [dp + (1 << b) * (1 - 2 * ((dp // (1 << b)) % 2)) for b in range(3, bits)]
    greet = [(p_c, z), (p_f, z), (p_s, z), (dp, z1), (dp, z2), (dp, z3)] + [(e, z) for e in extra]
    for dev in greet:
        pl.semaphore_signal(barrier, inc=1, device_id=dev, device_id_type=MESH)
    for j, w_ref in enumerate((wq, wk, wv)):
        wbuf[ATT, z, pl.ds(j * ml, ml), :] = w_ref[...].T
    bias[z] = vin[...]
    loads[1].wait()
    pl.semaphore_wait(barrier, len(greet))

    wide = {ATT: False, INN: False, OUT: True}

    def own(piece, off, n):
        if piece == ATT:
            return wbuf.at[ATT, z, pl.ds(off, n)]
        return (wi, wout)[piece - 1].at[pl.ds(off, n)]

    def reg(piece, k, off, n):
        return wbuf.at[piece, shard[k], pl.ds(off, n)]

    def ag_send(piece, slot, where, dev, mine=False):
        def make():
            region = reg(piece, *where)
            src = own(piece, *where[1:]) if mine else region
            return src, region, ag_s.at[piece, slot], ag_r.at[piece, slot], dev

        send(make)

    def ag_wait(piece, slot, where):
        region = reg(piece, *where)
        remote(region, region, ag_s.at[piece, slot], ag_r.at[piece, slot], (dp, z1)).wait_recv()

    def first(piece):
        return (q0, qtr) if wide[piece] else (e0, eig)

    def a_z(piece):
        off, n = first(piece)
        ag_send(piece, 1, (0, off, n), (dp, z1), True)
        ag_send(piece, 0, (0, off, n), (dp, z2), True)

    def a_zf(piece):
        off, n = first(piece)
        ag_wait(piece, 0, (2, off, n))
        ag_send(piece, 2, (2, off, n), (dp, z1))

    def a_arrive(piece, k):
        off, n = first(piece)
        if k != 2:
            ag_wait(piece, {1: 1, 3: 2}[k], (k, off, n))

    def a_s(piece, k):
        a_arrive(piece, k)
        ag_send(piece, 2 + k, (k, e0, eig), (p_s, z))

    def a_f(piece, k):
        if wide[piece]:
            a_arrive(piece, k)
        else:
            ag_wait(piece, 2 + k, (k, eo, eig))
        ag_send(piece, 5 + k, (k, q0, qtr), (p_f, z))

    def a_c(piece, k):
        ag_wait(piece, 5 + k, (k, qo, qtr))
        ag_send(piece, 8 + k, (k, h0, half), (p_c, z))

    def a_done(piece, k):
        ag_wait(piece, 8 + k, (k, ho, half))

    X_TOK, X_N, X_G, X_FG, X_A, X_DI, X_KA = 0, 1, 2, 3, 4, 8, 12

    def core_send(slot, pair):
        send(lambda: (*pair(), x_s.at[slot], x_r.at[slot], (p_c, z)))

    def core_wait(slot, dst):
        remote(dst, dst, x_s.at[slot], x_r.at[slot], (p_c, z)).wait_recv()

    for j, zz in enumerate((z1, z2, z3)):
        send(lambda j=j, zz=zz: (vin, bias.at[z], b_s.at[j], b_r.at[j], (dp, zz)))
    a_z(ATT)
    a_z(INN)
    a_z(OUT)
    core_send(X_TOK, lambda: (tok, xs.at[pl.ds(rows, rows)]))

    for r in range(rows):
        seg_row = seg[pl.ds(z * rows + r, 1), :]
        live_row = live[pl.ds(z * rows + r, 1), :]
        code = jnp.where(live_row == 1, seg_row, -1)
        ids = lax.broadcasted_iota(jnp.int32, (8, seq), 0)
        key_hot = (jnp.broadcast_to(code, (8, seq)) == ids).astype(F32).astype(BF)
        query_hot = (jnp.broadcast_to(seg_row, (8, seq)) == ids).astype(F32).astype(BF)
        mask[r] = jnp.where(dot(key_hot, query_hot, TN) > 0.5, 0.0, NEG_FILL)
    acc[...] = jnp.zeros_like(acc)
    first_row = (lax.broadcasted_iota(jnp.int32, (8, seq), 0) == 0).astype(F32).astype(BF)
    loads[0].wait()

    def attend(t):
        def row(r, carry):
            x_row = xs[r]
            bias_rows = bias[t].astype(BF)[:, : 3 * ml]
            qkv[t, r] = (
                dot(wbuf[ATT, t, pl.ds(0, 3 * ml), :], x_row, NT) + dot(bias_rows, first_row, TN)
            ).astype(BF)
            for h in range(hs):
                query = qkv[t, r, pl.ds(h * DH, DH), :]
                key = qkv[t, r, pl.ds(ml + h * DH, DH), :]
                value = qkv[t, r, pl.ds(2 * ml + h * DH, DH), :]
                scores = dot(key, query, TN) * scale + mask[r]
                top = jnp.max(scores, 0, keepdims=True)
                exponent = jnp.exp(scores - top)
                total = jnp.sum(exponent, 0, keepdims=True)
                prob_t = (exponent * (1.0 / total)).astype(BF)
                prob[t, r, h] = prob_t
                ka[t, r, pl.ds(3 * ml + h * DH, DH), :] = dot(value, prob_t, NN).astype(BF)
            part = dot(ka[t, r, pl.ds(3 * ml, ml), :], wbuf[ATT, t, pl.ds(3 * ml, ml), :], TN)
            sl = pl.ds(pl.multiple_of(r * seq, 16), seq)
            acc[sl, :] = acc[sl, :] + part
            return carry

        lax.fori_loop(0, rows, row, 0)

    def attend_loop(i, carry):
        @pl.when(i == 1)
        def _():
            remote(vin, bias.at[z1], b_s.at[0], b_r.at[0], (dp, z1)).wait_recv()
            remote(vin, bias.at[z2], b_s.at[1], b_r.at[1], (dp, z2)).wait_recv()
            remote(vin, bias.at[z3], b_s.at[2], b_r.at[2], (dp, z3)).wait_recv()
            a_s(ATT, 1)
            a_zf(ATT)
            a_s(ATT, 2)
            a_f(ATT, 1)
            a_s(INN, 1)
            a_s(ATT, 3)
            a_f(ATT, 2)
            a_c(ATT, 1)
            a_zf(INN)
            a_s(INN, 2)
            a_done(ATT, 1)

        @pl.when(i == 2)
        def _():
            a_f(ATT, 3)
            a_c(ATT, 2)
            a_s(INN, 3)
            a_f(INN, 1)
            a_done(ATT, 2)

        @pl.when(i == 3)
        def _():
            a_c(ATT, 3)
            a_f(INN, 2)
            a_c(INN, 1)
            a_done(ATT, 3)

        attend(shard_of(i))
        return carry

    lax.fori_loop(0, 4, attend_loop, 0)

    rb = 32

    def norm_rows(summed):
        mean = jnp.mean(summed, -1, keepdims=True)
        centred = summed - mean
        variance = jnp.mean(centred * centred, -1, keepdims=True)
        rs_ = lax.rsqrt(variance + EPSILON)
        return centred * rs_, rs_

    def norm_back(grad, hat, rs_):
        return rs_ * (grad - jnp.mean(grad, -1, keepdims=True) - hat * jnp.mean(grad * hat, -1, keepdims=True))

    def vrow(j):
        return vin[pl.ds(j, 1), :]

    a_f(INN, 3)
    a_c(INN, 2)
    a_zf(OUT)
    a_f(OUT, 1)

    def norm1(j, carry):
        sl = pl.ds(pl.multiple_of(j * rb, 16), rb)
        per = seq // rb
        x_blk = xs[j // per, pl.ds(pl.multiple_of((j % per) * rb, 16), rb), :].astype(F32)
        hat, rs_ = norm_rows(acc[sl, :] + vrow(2) + x_blk)
        nh1[sl, :] = hat
        r1[sl, :] = jnp.broadcast_to(rs_, (rb, 128))
        nb[sl, :] = (hat * vrow(3) + vrow(4)).astype(BF)
        acc[sl, :] = jnp.zeros((rb, d), F32)
        return carry

    lax.fori_loop(0, tl // rb, norm1, 0)
    core_send(X_N, lambda: (nb.at[:, pl.ds(ho, half)], nhalf.at[pl.ds(tl, tl)]))
    nhalf[pl.ds(0, tl), :] = nb[:, pl.ds(h0, half)]

    loads[2].wait()

    def up(i, carry):
        @pl.when(i == 1)
        def _():
            a_done(INN, 1)
            a_f(OUT, 2)
            a_c(INN, 3)

        @pl.when(i == 2)
        def _():
            a_done(INN, 2)
            a_c(OUT, 1)

        @pl.when(i == 3)
        def _():
            a_done(INN, 3)
            a_c(OUT, 2)

        t = shard_of(i)
        tmp[...] = dot(nb[...], wbuf[INN, t], NN)
        b_row = bias[t, pl.ds(1, 1), :]

        def act(j, carry):
            sl = pl.ds(pl.multiple_of(j * rb, 16), rb)
            u = tmp[sl, :] + b_row
            cdf = 0.5 * (1.0 + lax.erf(u * ROOT_HALF))
            af[t, sl, :] = (u * cdf).astype(BF)
            gp[t, sl, :] = (cdf + u * (PDF_SCALE * jnp.exp(-0.5 * u * u))).astype(BF)
            return carry

        lax.fori_loop(0, tl // rb, act, 0)
        remote(af.at[t, :, pl.ds(ho, half)], asib.at[t], x_s.at[X_A + i], x_r.at[X_A + i], (p_c, z)).start()
        return carry

    lax.fori_loop(0, 4, up, 0)
    loads[3].wait()
    loads[4].wait()

    def down(i, carry):
        @pl.when(i == 1)
        def _():
            a_f(OUT, 3)
            a_done(OUT, 1)

        @pl.when(i == 2)
        def _():
            a_done(OUT, 2)
            a_c(OUT, 3)

        @pl.when(i == 3)
        def _():
            a_done(OUT, 3)

        t = shard_of(i)
        acc[...] += dot(af[t], wbuf[OUT, t], NN)
        return carry

    lax.fori_loop(0, 4, down, 0)

    vec_ref[...] = jnp.zeros_like(vec_ref)

    def add_vec(row, value):
        vec_ref[pl.ds(row, 1), :] = vec_ref[pl.ds(row, 1), :] + value

    def norm2(j, carry):
        sl = pl.ds(pl.multiple_of(j * rb, 16), rb)
        normed = nh1[sl, :] * vrow(3) + vrow(4)
        hat, rs_ = norm_rows(acc[sl, :] + vrow(5) + normed)
        out_ref[sl, :] = (hat * vrow(6) + vrow(7)).astype(BF)
        c_blk = cots[sl, :].astype(F32)
        back = norm_back(c_blk * vrow(6), hat, rs_)
        sg[sl, :] = back
        g[sl, :] = back.astype(BF)
        acc[sl, :] = jnp.zeros((rb, d), F32)
        add_vec(V_G2, jnp.sum(c_blk * hat, 0, keepdims=True))
        add_vec(V_S2, jnp.sum(c_blk, 0, keepdims=True))
        add_vec(V_EB, jnp.sum(back, 0, keepdims=True))
        return carry

    lax.fori_loop(0, tl // rb, norm2, 0)
    core_send(X_G, lambda: (g.at[pl.ds(0, tl)], g.at[pl.ds(tl, tl)]))

    fq = pl.multiple_of(f * qtr, 16)
    fo = pl.multiple_of((1 - f) * qtr, 16)
    sq = pl.multiple_of(f * qtr + s * eig, 16)
    so = pl.multiple_of(f * qtr + (1 - s) * eig, 16)

    def g_sem(piece, slot):
        return gr_s.at[piece, slot], gr_r.at[piece, slot]

    def g_send(piece, slot, pair, dev):
        send(lambda: (*pair(), *g_sem(piece, slot), dev))

    def g_wait(piece, slot, dst):
        remote(dst, dst, *g_sem(piece, slot), (dp, z1)).wait_recv()

    def add_into(dst, src, n):
        def blk(j, carry):
            sl = pl.ds(pl.multiple_of(j * 48, 16), 48)
            dst[sl, :] = (dst[sl, :].astype(F32) + src[sl, :].astype(F32)).astype(BF)
            return carry

        lax.fori_loop(0, n // 48, blk, 0)

    def fs_dynamic(piece, k):
        ssem, rsem = g_sem(piece, k)
        remote(gr.at[piece, k, pl.ds(fo, qtr)], rf.at[piece, k], ssem, rsem, (p_f, z)).start()

    def fr(piece, k):
        g_wait(piece, k, rf.at[piece, k])
        add_into(gr.at[piece, k, pl.ds(fq, qtr)], rf.at[piece, k], qtr)
        if k == 3:
            g_send(piece, 4, lambda: (gr.at[piece, 3, pl.ds(fq, qtr)], rz1.at[piece, 0]), (dp, z1))
        if k == 1:
            g_send(piece, 5, lambda: (gr.at[piece, 1, pl.ds(fq, qtr)], rz1.at[piece, 1]), (dp, z1))

    def z1r2(piece):
        g_wait(piece, 4, rz1.at[piece, 0])
        add_into(gr.at[piece, 2, pl.ds(fq, qtr)], rz1.at[piece, 0], qtr)
        g_send(piece, 6, lambda: (gr.at[piece, 2, pl.ds(fq, qtr)], rz2.at[piece]), (dp, z2))

    def z1r0(piece):
        g_wait(piece, 5, rz1.at[piece, 1])
        add_into(gr.at[piece, 0, pl.ds(fq, qtr)], rz1.at[piece, 1], qtr)

    def z2r(piece):
        g_wait(piece, 6, rz2.at[piece])
        add_into(gr.at[piece, 0, pl.ds(fq, qtr)], rz2.at[piece], qtr)
        g_send(piece, 7, lambda: (gr.at[piece, 0, pl.ds(so, eig)], rs.at[piece]), (p_s, z))

    def sr(piece):
        g_wait(piece, 7, rs.at[piece])
        mine = gr.at[piece, 0, pl.ds(sq, eig)]
        add_into(mine, rs.at[piece], eig)
        for j, partner in enumerate(extra):
            cp = remote(mine, rx.at[piece, j], e_s.at[piece, j], e_r.at[piece, j], (partner, z))
            cp.start()
            cp.wait()
            add_into(mine, rx.at[piece, j], eig)
        g_send(
            piece, 8, lambda: (gr.at[piece, 0, pl.ds(sq, eig)], grad_ref.at[piece, pl.ds(e0, eig)]), (p_s, z)
        )
        cp = pltpu.make_async_copy(mine, grad_ref.at[piece, pl.ds(e0, eig)], loc_sem.at[5 + piece])
        cp.start()
        return cp

    local_out = {}

    def sr_(piece):
        local_out[piece] = sr(piece)

    def s2r(piece):
        g_wait(piece, 8, grad_ref.at[piece, pl.ds(eo, eig)])
        local_out[piece].wait()
        g_send(piece, 9, lambda: (grad_ref.at[piece, pl.ds(q0, qtr)],) * 2, (p_f, z))

    def f2r(piece):
        g_wait(piece, 9, grad_ref.at[piece, pl.ds(qo, qtr)])
        g_send(piece, 10, lambda: (grad_ref.at[piece, pl.ds(h0, half)],) * 2, (p_c, z))

    def c2r(piece):
        g_wait(piece, 10, grad_ref.at[piece, pl.ds(ho, half)])

    def order(i):
        return 3 - 2 * (i % 2) - i // 2

    def ffn_back(i, carry):
        @pl.when(i < 4)
        def _():
            k = order(i)
            t = shard_of(k)
            tmp[...] = dot(g[pl.ds(0, tl), :], wbuf[OUT, t], NT)

            def act(j, carry):
                sl = pl.ds(pl.multiple_of(j * rb, 16), rb)
                blk = (tmp[sl, :] * gp[t, sl, :].astype(F32)).astype(BF)
                di[t, sl, :] = blk
                return carry + jnp.sum(blk.astype(F32), 0, keepdims=True)

            vec_ref[pl.ds(4 + t, 1), :] = lax.fori_loop(0, tl // rb, act, jnp.zeros((1, d), F32))
            remote(
                di.at[t, pl.ds(0, tl)], di.at[t, pl.ds(tl, tl)], x_s.at[X_DI + k], x_r.at[X_DI + k], (p_c, z)
            ).start()

            @pl.when(i == 0)
            def _():
                core_wait(X_G, g.at[pl.ds(tl, tl)])
                core_wait(X_N, nhalf.at[pl.ds(tl, tl)])

            core_wait(X_A + k, asib.at[t])
            al[pl.ds(0, tl), :] = af[t, :, pl.ds(h0, half)]
            al[pl.ds(tl, tl), :] = asib[t]
            gr[OUT, k] = dot(al[...], g[...], TN).astype(BF)
            fs_dynamic(OUT, k)
            acc[...] += dot(di[t, pl.ds(0, tl), :], wbuf[INN, t], NT)

        @pl.when(i == 2)
        def _():
            fr(OUT, 3)

        @pl.when(i == 4)
        def _():
            fr(OUT, 1)

        @pl.when(i > 0)
        def _():
            k = order(i - 1)
            t = shard_of(k)
            core_wait(X_DI + k, di.at[t, pl.ds(tl, tl)])
            gr[INN, k] = dot(nhalf[...], di[t], TN).astype(BF)
            fs_dynamic(INN, k)

        return carry

    lax.fori_loop(0, 5, ffn_back, 0)

    def norm1_back(j, carry):
        sl = pl.ds(pl.multiple_of(j * rb, 16), rb)
        per = seq // rb
        hat = nh1[sl, :]
        total = acc[sl, :] + sg[sl, :]
        back = norm_back(total * vrow(3), hat, r1[sl, 0:1])
        fgf[sl, :] = back
        fg[j // per, pl.ds(pl.multiple_of((j % per) * rb, 16), rb), :] = back.astype(BF)
        acc[sl, :] = jnp.zeros((rb, d), F32)
        add_vec(V_G1, jnp.sum(total * hat, 0, keepdims=True))
        add_vec(V_S1, jnp.sum(total, 0, keepdims=True))
        add_vec(V_OB, jnp.sum(back, 0, keepdims=True))
        return carry

    lax.fori_loop(0, tl // rb, norm1_back, 0)
    core_send(X_FG, lambda: (fg.at[pl.ds(0, rows)], fg.at[pl.ds(rows, rows)]))
    ones = jnp.ones((8, seq), BF)

    def attend_back(t):
        def row(r, carry):
            dctx = dot(wbuf[ATT, t, pl.ds(3 * ml, ml), :], fg[r], NT).astype(BF)
            for h in range(hs):
                query = qkv[t, r, pl.ds(h * DH, DH), :]
                key = qkv[t, r, pl.ds(ml + h * DH, DH), :]
                value = qkv[t, r, pl.ds(2 * ml + h * DH, DH), :]
                prob_t = prob[t, r, h]
                grad = dctx[h * DH : (h + 1) * DH]
                ka[t, r, pl.ds(2 * ml + h * DH, DH), :] = dot(grad, prob_t, NT).astype(BF)
                prob_grad = dot(value, grad, TN)
                wide_prob = prob_t.astype(F32)
                inner = jnp.sum(wide_prob * prob_grad, 0, keepdims=True)
                score_grad = (wide_prob * (prob_grad - inner)).astype(BF)
                ka[t, r, pl.ds(h * DH, DH), :] = (dot(key, score_grad, NN) * scale).astype(BF)
                ka[t, r, pl.ds(ml + h * DH, DH), :] = (dot(query, score_grad, NT) * scale).astype(BF)
            grads = ka[t, r, pl.ds(0, 3 * ml), :]
            vec_ref[pl.ds(t, 1), pl.ds(0, 3 * ml)] += dot(ones, grads, NT)[0:1]
            sl = pl.ds(pl.multiple_of(r * seq, 16), seq)
            acc[sl, :] = acc[sl, :] + dot(grads, wbuf[ATT, t, pl.ds(0, 3 * ml), :], TN)
            return carry

        lax.fori_loop(0, rows, row, 0)

    def att_back(i, carry):
        @pl.when(i < 4)
        def _():
            k = order(i)
            t = shard_of(k)
            attend_back(t)
            remote(
                ka.at[t, :, pl.ds(ho, half)], ks.at[t], x_s.at[X_KA + k], x_r.at[X_KA + k], (p_c, z)
            ).start()

        @pl.when(i == 0)
        def _():
            core_wait(X_TOK, xs.at[pl.ds(rows, rows)])
            core_wait(X_FG, fg.at[pl.ds(rows, rows)])
            fr(OUT, 2)
            fr(OUT, 0)

        @pl.when(i == 1)
        def _():
            z1r2(OUT)
            fr(INN, 3)

        @pl.when(i == 2)
        def _():
            z1r0(OUT)
            fr(INN, 1)

        @pl.when(i == 3)
        def _():
            z2r(OUT)
            fr(INN, 2)

        @pl.when(i == 4)
        def _():
            fr(INN, 0)
            z1r2(INN)

        @pl.when(i > 0)
        def _():
            k = order(i - 1)
            t = shard_of(k)
            core_wait(X_KA + k, ks.at[t])
            for j in range(2):
                rowsel = pl.ds(pl.multiple_of(h0 + j * ml, 16), ml)
                use = c * j
                total = jnp.zeros((ml, d), F32)
                for r in range(rows):
                    right_own = xs[r] if j == 0 else jnp.where(use == 1, fg[r], xs[r])
                    right_sib = xs[rows + r] if j == 0 else jnp.where(use == 1, fg[rows + r], xs[rows + r])
                    total += dot(ka[t, r, rowsel, :], right_own, NN)
                    total += dot(ks[t, r, pl.ds(j * ml, ml), :], right_sib, NN)
                gr[ATT, k, pl.ds(j * ml, ml), :] = total.astype(BF)
            fs_dynamic(ATT, k)

        return carry

    lax.fori_loop(0, 5, att_back, 0)

    def finish(j, carry):
        sl = pl.ds(pl.multiple_of(j * rb, 16), rb)
        dx_ref[sl, :] = (fgf[sl, :] + acc[sl, :]).astype(BF)
        return carry

    lax.fori_loop(0, tl // rb, finish, 0)

    partners = [(p_c, z), (p_f, z), (p_s, z)] + [(e, z) for e in extra] + [(dp, z1), (dp, z2)]

    def v_step(j):
        cp = remote(vec_ref, vrecv.at[j], v_s.at[j], v_r.at[j], partners[j])
        cp.start()
        return cp

    def v_end(cp, j):
        cp.wait()
        vec_ref[...] += vrecv[j]

    v0 = v_step(0)
    sr_(OUT)
    z1r0(INN)
    v_end(v0, 0)
    v1 = v_step(1)
    fr(ATT, 3)
    z2r(INN)
    fr(ATT, 1)
    s2r(OUT)
    v_end(v1, 1)
    v2 = v_step(2)
    fr(ATT, 2)
    sr_(INN)
    f2r(OUT)
    fr(ATT, 0)
    v_end(v2, 2)
    v3 = v_step(3)
    z1r2(ATT)
    s2r(INN)
    z1r0(ATT)
    v_end(v3, 3)
    v4 = v_step(4)
    f2r(INN)
    z2r(ATT)
    v_end(v4, 4)
    for j in range(5, len(partners)):
        v_end(v_step(j), j)
    sr_(ATT)
    s2r(ATT)
    f2r(ATT)
    c2r(OUT)
    c2r(INN)
    c2r(ATT)

    for make in pending:
        remote(*make()).wait_send()

    def sent(k, carry):
        t = shard_of(k)
        remote(af.at[t, :, pl.ds(ho, half)], asib.at[t], x_s.at[X_A + k], x_r.at[X_A + k], (p_c, z)).wait_send()
        remote(
            di.at[t, pl.ds(0, tl)], di.at[t, pl.ds(tl, tl)], x_s.at[X_DI + k], x_r.at[X_DI + k], (p_c, z)
        ).wait_send()
        remote(ka.at[t, :, pl.ds(ho, half)], ks.at[t], x_s.at[X_KA + k], x_r.at[X_KA + k], (p_c, z)).wait_send()
        for piece in range(3):
            ssem, rsem = g_sem(piece, k)
            remote(gr.at[piece, k, pl.ds(fo, qtr)], rf.at[piece, k], ssem, rsem, (p_f, z)).wait_send()
        return carry

    lax.fori_loop(0, 4, sent, 0)


def spread_kernel(
    ml, grads, vec, out_in, dx_in,
    out_ref, dx_ref, gq, gk, gv, go, gi, ge,
):
    out_ref[...] = out_in[...]
    dx_ref[...] = dx_in[...]
    for j, ref in enumerate((gq, gk, gv)):
        ref[...] = grads[0, pl.ds(j * ml, ml), :].astype(F32).T
    go[...] = grads[0, pl.ds(3 * ml, ml), :].astype(F32)
    gi[...] = grads[1].astype(F32)
    ge[...] = grads[2].astype(F32)


def per_device(
    n_dp,
    tokens, segment_ids, live_mask, query_weight, key_weight, value_weight, query_bias, value_bias,
    output_weight, output_bias, first_gain, first_shift, inner_weight, inner_bias, outer_weight,
    outer_bias, second_gain, second_shift, cotangent,
):
    tl, d = tokens.shape
    seq_rows, seq = segment_ids.shape
    rows = tl // seq
    ml = query_weight.shape[1]
    half, qtr, eig = d // 2, d // 4, d // 8
    bits = n_dp.bit_length() - 1
    n_extra = max(bits - 3, 1)
    n_vec = bits + 2
    zeros = jnp.zeros((ml,), F32)
    att_bias = jnp.concatenate([query_bias.astype(F32), zeros, value_bias.astype(F32), zeros])
    vin = jnp.stack(
        [att_bias]
        + [
            v.astype(F32)
            for v in (inner_bias, output_bias, first_gain, first_shift, outer_bias, second_gain, second_shift)
        ]
    )
    cfg = {"dp": n_dp, "d": d, "seq": seq, "rows": rows}
    vmem = pl.BlockSpec(memory_space=pltpu.VMEM)
    hbm = pl.BlockSpec(memory_space=pl.ANY)
    scratch = [
        pltpu.VMEM((3, 4, d, d), BF),
        pltpu.VMEM((4, 8, d), F32),
        pltpu.VMEM((2 * rows, seq, d), BF),
        pltpu.VMEM((tl, d), BF),
        pltpu.VMEM((4, rows, 3 * ml, seq), BF),
        pltpu.VMEM((4, rows, d, seq), BF),
        pltpu.VMEM((4, rows, half, seq), BF),
        pltpu.VMEM((4, rows, ml // DH, seq, seq), BF),
        pltpu.VMEM((rows, seq, seq), F32),
        pltpu.VMEM((tl, d), F32),
        pltpu.VMEM((tl, d), F32),
        pltpu.VMEM((tl, d), F32),
        pltpu.VMEM((tl, 128), F32),
        pltpu.VMEM((tl, d), BF),
        pltpu.VMEM((2 * tl, half), BF),
        pltpu.VMEM((4, tl, d), BF),
        pltpu.VMEM((4, tl, half), BF),
        pltpu.VMEM((2 * tl, half), BF),
        pltpu.VMEM((4, tl, d), BF),
        pltpu.VMEM((2 * tl, d), BF),
        pltpu.VMEM((tl, d), F32),
        pltpu.VMEM((4, 2 * tl, d), BF),
        pltpu.VMEM((2 * rows, seq, d), BF),
        pltpu.VMEM((tl, d), F32),
        pltpu.VMEM((3, 4, half, d), BF),
        pltpu.VMEM((3, 4, qtr, d), BF),
        pltpu.VMEM((3, 2, qtr, d), BF),
        pltpu.VMEM((3, qtr, d), BF),
        pltpu.VMEM((3, eig, d), BF),
        pltpu.VMEM((3, n_extra, eig, d), BF) if bits > 3 else pltpu.VMEM((1, 1, 16, 128), BF),
        pltpu.VMEM((n_vec, 16, d), F32),
        pltpu.SemaphoreType.DMA((8,)),
        pltpu.SemaphoreType.DMA((3, 12)),
        pltpu.SemaphoreType.DMA((3, 12)),
        pltpu.SemaphoreType.DMA((3, 11)),
        pltpu.SemaphoreType.DMA((3, 11)),
        pltpu.SemaphoreType.DMA((16,)),
        pltpu.SemaphoreType.DMA((16,)),
        pltpu.SemaphoreType.DMA((3,)),
        pltpu.SemaphoreType.DMA((3,)),
        pltpu.SemaphoreType.DMA((n_vec,)),
        pltpu.SemaphoreType.DMA((n_vec,)),
        pltpu.SemaphoreType.DMA((3, n_extra)),
        pltpu.SemaphoreType.DMA((3, n_extra)),
    ]
    out, dx, grads, vec = pl.pallas_call(
        functools.partial(layer_kernel, cfg),
        out_shape=(
            jax.ShapeDtypeStruct((tl, d), BF),
            jax.ShapeDtypeStruct((tl, d), BF),
            jax.ShapeDtypeStruct((3, d, d), BF),
            jax.ShapeDtypeStruct((16, d), F32),
        ),
        in_specs=[hbm, hbm, vmem, vmem, vmem, hbm, hbm, hbm, vmem, vmem, vmem],
        out_specs=(vmem, vmem, hbm, vmem),
        scratch_shapes=scratch,
        compiler_params=pltpu.CompilerParams(
            collective_id=0, has_side_effects=True, vmem_limit_bytes=62 * 1024 * 1024
        ),
        name="layer",
    )(
        tokens.reshape(rows, seq, d), cotangent, query_weight, key_weight, value_weight, output_weight,
        inner_weight, outer_weight, vin, segment_ids, live_mask,
    )
    ff = inner_weight.shape[1]
    out, dx, gq, gk, gv, go, gi, ge = pl.pallas_call(
        functools.partial(spread_kernel, ml),
        out_shape=(
            jax.ShapeDtypeStruct((tl, d), BF),
            jax.ShapeDtypeStruct((tl, d), BF),
            jax.ShapeDtypeStruct((d, ml), F32),
            jax.ShapeDtypeStruct((d, ml), F32),
            jax.ShapeDtypeStruct((d, ml), F32),
            jax.ShapeDtypeStruct((ml, d), F32),
            jax.ShapeDtypeStruct((d, ff), F32),
            jax.ShapeDtypeStruct((ff, d), F32),
        ),
        in_specs=[vmem] * 4,
        out_specs=(vmem,) * 8,
        compiler_params=pltpu.CompilerParams(vmem_limit_bytes=40 * 1024 * 1024),
        name="spread",
    )(grads, vec, out, dx)
    z = lax.axis_index("mp")
    att_row = lax.dynamic_slice(vec, (z, 0), (1, d))[0]
    inner_row = lax.dynamic_slice(vec, (4 + z, 0), (1, d))[0]
    return (
        out, dx, gq, gk, gv, att_row[:ml], att_row[2 * ml : 3 * ml], go, vec[V_OB], vec[V_G1], vec[V_S1],
        gi, inner_row, ge, vec[V_EB], vec[V_G2], vec[V_S2],
    )


def solution(mesh):
    tok, shared = P(("dp", "mp"), None), P()
    cols, rows, vec = P(None, "mp"), P("mp", None), P("mp")
    in_specs = (
        tok, P("dp", None), P("dp", None), cols, cols, cols, vec, vec, rows, shared, shared, shared,
        cols, vec, rows, shared, shared, shared, tok,
    )
    out_specs = (
        tok, tok, cols, cols, cols, vec, vec, rows, shared, shared, shared, cols, vec, rows,
        shared, shared, shared,
    )
    return jax.shard_map(
        functools.partial(per_device, mesh.shape["dp"]),
        mesh=mesh,
        in_specs=in_specs,
        out_specs=out_specs,
        check_vma=False,
    )
```

time: 620 us -> 205 us (0.33); the launches traced: 611 us -> 204 us
  waiting for transfers between devices: 412 us -> 0 us
  Pallas kernels: 0 us -> 180 us
  matrix products: 57.6 us -> 0 us
  blocking collectives: 56.6 us -> 0 us
  local copies, waits for them, and re-layouts: 49.6 us -> 22.2 us
  other arithmetic: 19 us -> 1.39 us
  between operations: 14.7 us -> 0.68 us
    pallas_call x0 -> x2, Pallas kernels: none -> 180 us  [the longest x1 177 us: per_device(): pl.pallas_call(functools.partial(layer_kernel, cfg), out_shape=(jax.Shape...]
    all_gather x4 -> x0, waiting for transfers between devices: 174 us -> none  [the longest x1 44.7 us: per_device(): group_tokens = lax.all_gather(tokens, 'mp', axis=0, tiled=True)]
    reduce_scatter x4 -> x0, waiting for transfers between devices: 151 us -> none  [the longest x1 71 us: per_device(): lax.psum_scatter(jnp.dot(rows_blk, output_weight, preferred_element_type=...]
    psum x1 -> x0, waiting for transfers between devices: 86.2 us -> none  [per_device(): lax.psum((query_weight_grad, key_weight_grad, value_weight_grad, query_bi...]
    dot_general x32 -> x0, matrix products: 57.6 us -> none  [the longest x6 14.5 us: right_transpose(): lax.dot_general(left, right, (((1,), (1,)), ((), ())), preferred_element_...]
    psum x2 -> x0, blocking collectives: 56.6 us -> none  [the longest x1 41.4 us: per_device(): lax.psum((first_gain_grad, first_shift_grad, output_bias_grad, second_gai...]
    while x41 -> x0, local copies, waits for them, and re-layouts: 13.3 us -> none
    reshape x8 -> x0, local copies, waits for them, and re-layouts: 12.2 us -> none  [the longest x4 6.97 us: join_heads(): return block_array.reshape(seq_rows * SEQ, heads_here * DH)]
  transfers between devices with their start and end apart: 9 -> 0, of which waited for: 8 -> 0; matrix products, arithmetic and copies ran while one was open for 3% -> 0% of each run, Pallas kernels for 0% -> 0%
where the time goes in v1:
time: 205 us; the launch traced here: 204 us
  Pallas kernels  180 us (88%)
  local copies, waits for them, and re-layouts  22.2 us (11%)
    pallas_call x1, Pallas kernels, per_device(): pl.pallas_call(functools.partial(layer_kernel, cfg), out_shape=(jax.Shape...  177 us
    unnamed x14, local copies, waits for them, and re-layouts  13.7 us
    another operation x9, local copies, waits for them, and re-layouts, per_device(): jnp.stack([att_bias] + [v.astype(F32) for v in (inner_bias, output_bias,...  5.45 us

profile of v1, /device:TPU:0, one launch (start us, length us, event | category | flops | bytes accessed | tf_op | source)
XLA Modules:
  0.0 203.9 jit_solution(10179553798805686938)
XLA Ops:
  0.7 1.9 copy.36.wq
  2.5 1.9 copy.37.wk
  4.4 1.9 copy.38.wv
  6.3 0.7 convert_element_type.5
  6.9 0.7 convert_element_type.4
  7.7 0.7 reshape.40
  8.4 0.7 reshape.41
  9.1 0.7 reshape.42
  9.8 0.7 reshape.43
  10.4 0.7 reshape.44
  11.1 0.7 reshape.45
  11.8 0.7 reshape.46
  12.5 0.6 stack.63.vin
  13.1 176.5 %layer.1 = (bf16[320,768]{1,0:T(8,128)(2,1)}, bf16[320,768]{1,0:T(8,128)(2,1)}, bf16[3,768,768]{2,1,0:T(8,128)(2,1)}, f32[16,768]{1,0:T(8,128)}) custom-call(bf16[2,160,768]{2,1,0:T(8,128)(2,1)} %bitcast.3, bf16[320,768]{1,0:T(8,128)(2,1)} %cot.1, bf16[768,192]{1,0:T(8,128)(2,1)} %copy.36.wq, bf16[768,192]{1,0:T(8,128)(2,1)} %copy.37.wk, ...), custom_call_target="tpu_custom_call" | custom-call | tf_op jit(solution)/shard_map/layer/pallas_call | solution.py:753
  189.7 2.0 copy-done
  191.7 1.0 copy-done.1
  192.7 1.0 copy-done.2
  193.7 0.8 copy-done.3
  194.5 3.0 %spread.1 = (bf16[320,768]{1,0:T(8,128)(2,1)}, bf16[320,768]{1,0:T(8,128)(2,1)}, f32[768,192]{1,0:T(8,128)S(1)}, f32[768,192]{1,0:T(8,128)S(1)}, f32[768,192]{1,...) custom-call(bf16[3,768,768]{2,1,0:T(8,128)(2,1)S(1)} %copy-done, ...), custom_call_target="tpu_custom_call" | custom-call | tf_op jit(solution)/shard_map/spread/pallas_call | solution.py:773
  197.6 1.1 copy.39
  198.6 1.1 copy.40
  199.7 1.1 copy.41
  200.8 1.4 fusion
  202.1 1.8 slice_reduce_fusion
  (7 shorter events, 0.1 us)
Async XLA Ops:
  189.6 2.0 copy-start
  191.7 1.0 copy-start.1
  192.7 1.0 copy-start.2
  193.7 0.8 copy-start.3

commit v2 on v1

--- a/solution.py
+++ b/solution.py
@@ -30,11 +30,11 @@
 
 def layer_kernel(
     cfg,
-    tok, cot, wq, wk, wv, wo, wi, wout, vin, seg, live,
+    tok, cot, wq, wk, wv, wo, wi, wout, bq, bv, bi, bo, g1, s1, be, g2, s2, seg, live,
     out_ref, dx_ref, grad_ref, vec_ref,
     wbuf, bias, xs, cots, qkv, ka, ks, prob, mask, acc, tmp, nh1, r1,
     nb, nhalf, af, asib, al, gp, g, sg, di, fg, fgf,
-    gr, rf, rz1, rz2, rs, rx, vrecv,
+    gr, rf, rz1, rz2, rs, rx, vrecv, vin,
     loc_sem, ag_s, ag_r, gr_s, gr_r, x_s, x_r, b_s, b_r, v_s, v_r, e_s, e_r,
 ):
     n_dp, d, seq, rows = cfg["dp"], cfg["d"], cfg["seq"], cfg["rows"]
@@ -81,6 +81,9 @@
         pltpu.make_async_copy(wi, wbuf.at[INN, z], loc_sem.at[2]),
         pltpu.make_async_copy(wout, wbuf.at[OUT, z], loc_sem.at[3]),
         pltpu.make_async_copy(cot, cots, loc_sem.at[4]),
+    ] + [
+        pltpu.make_async_copy(ref, wbuf.at[ATT, z, pl.ds(j * ml, ml)], loc_sem.at[8 + j])
+        for j, ref in enumerate((wq, wk, wv))
     ]
     for cp in loads:
         cp.start()
@@ -89,10 +92,14 @@
     greet = [(p_c, z), (p_f, z), (p_s, z), (dp, z1), (dp, z2), (dp, z3)] + [(e, z) for e in extra]
     for dev in greet:
         pl.semaphore_signal(barrier, inc=1, device_id=dev, device_id_type=MESH)
-    for j, w_ref in enumerate((wq, wk, wv)):
-        wbuf[ATT, z, pl.ds(j * ml, ml), :] = w_ref[...].T
+    vin[...] = jnp.zeros_like(vin)
+    vin[pl.ds(0, 1), pl.ds(0, ml)] = bq[...].astype(F32).reshape(1, ml)
+    vin[pl.ds(0, 1), pl.ds(2 * ml, ml)] = bv[...].astype(F32).reshape(1, ml)
+    for j, ref in enumerate((bi, bo, g1, s1, be, g2, s2)):
+        vin[pl.ds(j + 1, 1), :] = ref[...].astype(F32).reshape(1, d)
     bias[z] = vin[...]
-    loads[1].wait()
+    for j in (1, 5, 6, 7):
+        loads[j].wait()
     pl.semaphore_wait(barrier, len(greet))
 
     wide = {ATT: False, INN: False, OUT: True}
@@ -667,15 +674,46 @@
 
 def spread_kernel(
     ml, grads, vec, out_in, dx_in,
-    out_ref, dx_ref, gq, gk, gv, go, gi, ge,
+    out_ref, dx_ref, gq, gk, gv, go, gi, ge, bq, bv, bo, g1, s1, bi, be, g2, s2,
+    grads_v, vec_v, att_v, big_v, io_v, sem,
 ):
-    out_ref[...] = out_in[...]
-    dx_ref[...] = dx_in[...]
-    for j, ref in enumerate((gq, gk, gv)):
-        ref[...] = grads[0, pl.ds(j * ml, ml), :].astype(F32).T
-    go[...] = grads[0, pl.ds(3 * ml, ml), :].astype(F32)
-    gi[...] = grads[1].astype(F32)
-    ge[...] = grads[2].astype(F32)
+    z = lax.axis_index("mp")
+    moves = [
+        pltpu.make_async_copy(grads.at[1], grads_v.at[1], sem.at[0]),
+        pltpu.make_async_copy(grads.at[2], grads_v.at[2], sem.at[1]),
+        pltpu.make_async_copy(grads.at[0], grads_v.at[0], sem.at[2]),
+        pltpu.make_async_copy(vec, vec_v, sem.at[3]),
+        pltpu.make_async_copy(out_in, io_v.at[0], sem.at[4]),
+        pltpu.make_async_copy(dx_in, io_v.at[1], sem.at[5]),
+    ]
+    for cp in moves:
+        cp.start()
+    outs = []
+    for j, ref in enumerate((gi, ge)):
+        moves[j].wait()
+        big_v[j] = grads_v[j + 1].astype(F32)
+        cp = pltpu.make_async_copy(big_v.at[j], ref, sem.at[6 + j])
+        cp.start()
+        outs.append(cp)
+    moves[2].wait()
+    att_v[...] = grads_v[0].astype(F32)
+    for j, ref in enumerate((gq, gk, gv, go)):
+        cp = pltpu.make_async_copy(att_v.at[pl.ds(j * ml, ml)], ref, sem.at[8 + j])
+        cp.start()
+        outs.append(cp)
+    for j, ref in enumerate((out_ref, dx_ref)):
+        moves[4 + j].wait()
+        cp = pltpu.make_async_copy(io_v.at[j], ref, sem.at[12 + j])
+        cp.start()
+        outs.append(cp)
+    moves[3].wait()
+    bq[...] = vec_v[pl.ds(z, 1), pl.ds(0, ml)].reshape(ml)
+    bv[...] = vec_v[pl.ds(z, 1), pl.ds(2 * ml, ml)].reshape(ml)
+    bi[...] = vec_v[pl.ds(4 + z, 1), :].reshape(4 * ml)
+    for row, ref in ((V_OB, bo), (V_G1, g1), (V_S1, s1), (V_EB, be), (V_G2, g2), (V_S2, s2)):
+        ref[...] = vec_v[pl.ds(row, 1), :].reshape(4 * ml)
+    for cp in outs:
+        cp.wait()
 
 
 def per_device(
@@ -692,15 +730,6 @@
     bits = n_dp.bit_length() - 1
     n_extra = max(bits - 3, 1)
     n_vec = bits + 2
-    zeros = jnp.zeros((ml,), F32)
-    att_bias = jnp.concatenate([query_bias.astype(F32), zeros, value_bias.astype(F32), zeros])
-    vin = jnp.stack(
-        [att_bias]
-        + [
-            v.astype(F32)
-            for v in (inner_bias, output_bias, first_gain, first_shift, outer_bias, second_gain, second_shift)
-        ]
-    )
     cfg = {"dp": n_dp, "d": d, "seq": seq, "rows": rows}
     vmem = pl.BlockSpec(memory_space=pltpu.VMEM)
     hbm = pl.BlockSpec(memory_space=pl.ANY)
@@ -736,7 +765,8 @@
         pltpu.VMEM((3, eig, d), BF),
         pltpu.VMEM((3, n_extra, eig, d), BF) if bits > 3 else pltpu.VMEM((1, 1, 16, 128), BF),
         pltpu.VMEM((n_vec, 16, d), F32),
-        pltpu.SemaphoreType.DMA((8,)),
+        pltpu.VMEM((8, d), F32),
+        pltpu.SemaphoreType.DMA((11,)),
         pltpu.SemaphoreType.DMA((3, 12)),
         pltpu.SemaphoreType.DMA((3, 12)),
         pltpu.SemaphoreType.DMA((3, 11)),
@@ -758,7 +788,7 @@
             jax.ShapeDtypeStruct((3, d, d), BF),
             jax.ShapeDtypeStruct((16, d), F32),
         ),
-        in_specs=[hbm, hbm, vmem, vmem, vmem, hbm, hbm, hbm, vmem, vmem, vmem],
+        in_specs=[hbm] * 8 + [vmem] * 11,
         out_specs=(vmem, vmem, hbm, vmem),
         scratch_shapes=scratch,
         compiler_params=pltpu.CompilerParams(
@@ -766,34 +796,35 @@
         ),
         name="layer",
     )(
-        tokens.reshape(rows, seq, d), cotangent, query_weight, key_weight, value_weight, output_weight,
-        inner_weight, outer_weight, vin, segment_ids, live_mask,
+        tokens.reshape(rows, seq, d), cotangent, query_weight.T, key_weight.T, value_weight.T, output_weight,
+        inner_weight, outer_weight, query_bias, value_bias, inner_bias, output_bias, first_gain, first_shift,
+        outer_bias, second_gain, second_shift, segment_ids, live_mask,
     )
     ff = inner_weight.shape[1]
-    out, dx, gq, gk, gv, go, gi, ge = pl.pallas_call(
+    out, dx, gq, gk, gv, go, gi, ge, bq, bv, bo, g1, s1, bi, be, g2, s2 = pl.pallas_call(
         functools.partial(spread_kernel, ml),
-        out_shape=(
-            jax.ShapeDtypeStruct((tl, d), BF),
-            jax.ShapeDtypeStruct((tl, d), BF),
-            jax.ShapeDtypeStruct((d, ml), F32),
-            jax.ShapeDtypeStruct((d, ml), F32),
-            jax.ShapeDtypeStruct((d, ml), F32),
-            jax.ShapeDtypeStruct((ml, d), F32),
-            jax.ShapeDtypeStruct((d, ff), F32),
-            jax.ShapeDtypeStruct((ff, d), F32),
+        out_shape=tuple(
+            jax.ShapeDtypeStruct(shape, dtype)
+            for shape, dtype in [((tl, d), BF)] * 2
+            + [((ml, d), F32)] * 4
+            + [((d, ff), F32), ((ff, d), F32)]
+            + [((ml,), F32)] * 2
+            + [((d,), F32)] * 7
         ),
-        in_specs=[vmem] * 4,
-        out_specs=(vmem,) * 8,
-        compiler_params=pltpu.CompilerParams(vmem_limit_bytes=40 * 1024 * 1024),
+        in_specs=[hbm] * 4,
+        out_specs=(hbm,) * 8 + (vmem,) * 9,
+        scratch_shapes=[
+            pltpu.VMEM((3, d, d), BF),
+            pltpu.VMEM((16, d), F32),
+            pltpu.VMEM((d, d), F32),
+            pltpu.VMEM((2, d, d), F32),
+            pltpu.VMEM((2, tl, d), BF),
+            pltpu.SemaphoreType.DMA((14,)),
+        ],
+        compiler_params=pltpu.CompilerParams(vmem_limit_bytes=60 * 1024 * 1024),
         name="spread",
     )(grads, vec, out, dx)
-    z = lax.axis_index("mp")
-    att_row = lax.dynamic_slice(vec, (z, 0), (1, d))[0]
-    inner_row = lax.dynamic_slice(vec, (4 + z, 0), (1, d))[0]
-    return (
-        out, dx, gq, gk, gv, att_row[:ml], att_row[2 * ml : 3 * ml], go, vec[V_OB], vec[V_G1], vec[V_S1],
-        gi, inner_row, ge, vec[V_EB], vec[V_G2], vec[V_S2],
-    )
+    return out, dx, gq.T, gk.T, gv.T, bq, bv, go, bo, g1, s1, gi, bi, ge, be, g2, s2
 
 
 def solution(mesh):

time: 205 us -> 187 us (0.912)
  local copies, waits for them, and re-layouts: 22.2 us -> 0 us
  Pallas kernels: 180 us -> 186 us
    unnamed x14 -> x0, local copies, waits for them, and re-layouts: 13.7 us -> none
    another operation x9 -> x0, local copies, waits for them, and re-layouts: 5.45 us -> none  [per_device(): jnp.stack([att_bias] + [v.astype(F32) for v in (inner_bias, output_bias,...]
    pallas_call x1, Pallas kernels: 177 us -> 180 us  [per_device(): pl.pallas_call(functools.partial(layer_kernel, cfg), out_shape=(jax.Shape...]
    slice x2 -> x0, local copies, waits for them, and re-layouts: 3.11 us -> none  [the longest x1 1.75 us: per_device(): vec[V_S2]]
    pallas_call x1, Pallas kernels: 3.05 us -> 5.36 us  [per_device(): pl.pallas_call(functools.partial(spread_kernel, ml), out_shape=tuple((jax...]
where the time goes in v2:
time: 187 us
  Pallas kernels  186 us (99%)
    pallas_call x1, Pallas kernels, per_device(): pl.pallas_call(functools.partial(layer_kernel, cfg), out_shape=(jax.Shape...  180 us
    pallas_call x1, Pallas kernels, per_device(): pl.pallas_call(functools.partial(spread_kernel, ml), out_shape=tuple((jax...  5.36 us

profile of v2, /device:TPU:0, one launch (start us, length us, event | category | flops | bytes accessed | tf_op | source)
XLA Modules:
  0.0 186.5 jit_solution(14308371073827171197)
XLA Ops:
  0.7 180.5 %layer.1 = (bf16[320,768]{1,0:T(8,128)(2,1)}, bf16[320,768]{1,0:T(8,128)(2,1)}, bf16[3,768,768]{2,1,0:T(8,128)(2,1)}, f32[16,768]{1,0:T(8,128)}) custom-call(bf16[2,160,768]{2,1,0:T(8,128)(2,1)} %bitcast.7, bf16[320,768]{1,0:T(8,128)(2,1)} %cot.1, bf16[192,768]{1,0:T(8,128)(2,1)} %bitcast.8, bf16[192,768]{1,0:T(8,128)(2,1)} %bitcast.9, ...), custom_call_target="tpu_custom_call" | custom-call | tf_op jit(solution)/shard_map/layer/pallas_call | solution.py:783
  181.2 5.4 %spread.1 = (bf16[320,768]{1,0:T(8,128)(2,1)}, bf16[320,768]{1,0:T(8,128)(2,1)}, f32[192,768]{1,0:T(8,128)}, f32[192,768]{1,0:T(8,128)}, f32[192,768]{1,0:T(8,12...) custom-call(bf16[3,768,768]{2,1,0:T(8,128)(2,1)} %get-tuple-element., ...), custom_call_target="tpu_custom_call" | custom-call | tf_op jit(solution)/shard_map/spread/pallas_call | solution.py:804

commit v3 on v2

--- a/solution.py
+++ b/solution.py
@@ -21,6 +21,68 @@
 TN = (((0,), (0,)), ((), ()))
 
 ATT, INN, OUT = 0, 1, 2
+WIDE = (False, False, True)
+CHAIN = ("FS12", "F12S", "F12S")
+PLAN = {
+    "x0": {
+        0: (("az2", 0, 0), ("az1", 0, 0),),
+    },
+    "att": {
+        0: (("zf", 0, 0), ("s", 0, 2),),
+        1: (("s", 0, 1), ("az1", 1, 0), ("f", 0, 2), ("az2", 1, 0),),
+        2: (("f", 0, 1), ("az1", 2, 0), ("s", 1, 1), ("f", 1, 1), ("s", 0, 3), ("c", 0, 1), ("d", 0, 1), ("zf", 1, 0), ("c", 0, 2), ("s", 1, 2), ("az2", 2, 0), ("d", 0, 2), ("f", 2, 1),),
+        3: (("f", 0, 3), ("c", 1, 1), ("f", 1, 2),),
+        4: (("d", 1, 1),),
+        5: (("s", 1, 3), ("c", 2, 1),),
+        6: (("c", 0, 3), ("zf", 2, 0), ("c", 1, 2), ("d", 0, 3), ("f", 2, 2),),
+        7: (("f", 1, 3),),
+    },
+    "n1": {
+    },
+    "up": {
+        0: (("d", 2, 1), ("f", 2, 3),),
+        2: (("c", 1, 3), ("d", 1, 2), ("c", 2, 2),),
+        3: (("c", 2, 3), ("d", 1, 3),),
+    },
+    "dn": {
+        1: (("d", 2, 2),),
+        3: (("d", 2, 3),),
+    },
+    "l2": {
+    },
+    "da": {
+    },
+    "gwo": {
+        2: (("gFr", 2, 3), ("g1s", 2, 3), ("gFs", 1, 3),),
+    },
+    "dn2": {
+        0: (("gFs", 2, 3),),
+        1: (("gFs", 2, 1),),
+        3: (("gFr", 2, 1),),
+    },
+    "gwi": {
+        1: (("gFs", 2, 2),),
+        2: (("g1s", 2, 1),),
+        3: (("gFs", 1, 2),),
+    },
+    "l1b": {
+        0: (("gFs", 1, 0),),
+    },
+    "ab": {
+        0: (("gFr", 1, 3), ("gFr", 2, 2), ("g1s", 1, 3), ("gFs", 2, 0), ("g1r", 2, 2), ("g2s", 2, 2), ("gFs", 1, 1),),
+        4: (("gFs", 0, 3),),
+        6: (("gFs", 0, 1), ("gFr", 1, 1), ("gFr", 2, 0), ("g1s", 1, 1), ("gFr", 1, 2),),
+        7: (("g1r", 1, 2), ("gFr", 0, 3), ("g1r", 2, 0), ("gSs", 0, 3), ("g2s", 1, 2), ("g2r", 2, 0), ("gSs", 2, 0),),
+    },
+    "gwa": {
+        3: (("gFr", 0, 1), ("gFs", 0, 2), ("gSs", 0, 1),),
+    },
+    "fin": {
+    },
+    "end": {
+        0: (("gSr", 2, 0), ("vs", 0, 0), ("gSr", 0, 3), ("vr", 0, 0), ("gFr", 1, 0), ("gS2s", 2, 0), ("gFr", 0, 2), ("vs", 1, 0), ("gFs", 0, 0), ("gSs", 0, 2), ("g1s", 0, 3), ("g1r", 1, 0), ("vr", 1, 0), ("g2r", 1, 0), ("gS2r", 2, 0), ("gSr", 0, 2), ("gSs", 1, 0), ("g1r", 0, 2), ("gFr", 0, 0), ("gSr", 0, 1), ("g2s", 0, 2), ("gSs", 0, 0), ("g1s", 0, 1), ("vs", 2, 0), ("gSr", 1, 0), ("gF2r", 2, 0), ("gS2s", 1, 0), ("gSr", 0, 0), ("g1r", 0, 0), ("g2r", 0, 0), ("gS2s", 0, 0), ("gS2r", 1, 0), ("gC2r", 2, 0), ("gS2r", 0, 0), ("vr", 2, 0), ("vs", 3, 0), ("vr", 3, 0), ("gF2r", 1, 0), ("vs", 4, 0), ("gF2r", 0, 0), ("vr", 4, 0), ("gC2r", 0, 0), ("gC2r", 1, 0),),
+    },
+}
 V_OB, V_G1, V_S1, V_EB, V_G2, V_S2 = 8, 9, 10, 11, 12, 13
 
 
@@ -34,7 +96,7 @@
     out_ref, dx_ref, grad_ref, vec_ref,
     wbuf, bias, xs, cots, qkv, ka, ks, prob, mask, acc, tmp, nh1, r1,
     nb, nhalf, af, asib, al, gp, g, sg, di, fg, fgf,
-    gr, rf, rz1, rz2, rs, rx, vrecv, vin,
+    gr, rf, rz, rs, rx, vrecv, vin,
     loc_sem, ag_s, ag_r, gr_s, gr_r, x_s, x_r, b_s, b_r, v_s, v_r, e_s, e_r,
 ):
     n_dp, d, seq, rows = cfg["dp"], cfg["d"], cfg["seq"], cfg["rows"]
@@ -102,8 +164,6 @@
         loads[j].wait()
     pl.semaphore_wait(barrier, len(greet))
 
-    wide = {ATT: False, INN: False, OUT: True}
-
     def own(piece, off, n):
         if piece == ATT:
             return wbuf.at[ATT, z, pl.ds(off, n)]
@@ -125,29 +185,28 @@
         remote(region, region, ag_s.at[piece, slot], ag_r.at[piece, slot], (dp, z1)).wait_recv()
 
     def first(piece):
-        return (q0, qtr) if wide[piece] else (e0, eig)
-
-    def a_z(piece):
-        off, n = first(piece)
-        ag_send(piece, 1, (0, off, n), (dp, z1), True)
-        ag_send(piece, 0, (0, off, n), (dp, z2), True)
-
-    def a_zf(piece):
-        off, n = first(piece)
-        ag_wait(piece, 0, (2, off, n))
-        ag_send(piece, 2, (2, off, n), (dp, z1))
+        return (q0, qtr) if WIDE[piece] else (e0, eig)
+
+    def a_z1(piece, _):
+        ag_send(piece, 1, (0, *first(piece)), (dp, z1), True)
+
+    def a_z2(piece, _):
+        ag_send(piece, 0, (0, *first(piece)), (dp, z2), True)
+
+    def a_zf(piece, _):
+        ag_wait(piece, 0, (2, *first(piece)))
+        ag_send(piece, 2, (2, *first(piece)), (dp, z1))
 
     def a_arrive(piece, k):
-        off, n = first(piece)
         if k != 2:
-            ag_wait(piece, {1: 1, 3: 2}[k], (k, off, n))
+            ag_wait(piece, {1: 1, 3: 2}[k], (k, *first(piece)))
 
     def a_s(piece, k):
         a_arrive(piece, k)
         ag_send(piece, 2 + k, (k, e0, eig), (p_s, z))
 
     def a_f(piece, k):
-        if wide[piece]:
+        if WIDE[piece]:
             a_arrive(piece, k)
         else:
             ag_wait(piece, 2 + k, (k, eo, eig))
@@ -157,7 +216,7 @@
         ag_wait(piece, 5 + k, (k, qo, qtr))
         ag_send(piece, 8 + k, (k, h0, half), (p_c, z))
 
-    def a_done(piece, k):
+    def a_d(piece, k):
         ag_wait(piece, 8 + k, (k, ho, half))
 
     X_TOK, X_N, X_G, X_FG, X_A, X_DI, X_KA = 0, 1, 2, 3, 4, 8, 12
@@ -168,11 +227,130 @@
     def core_wait(slot, dst):
         remote(dst, dst, x_s.at[slot], x_r.at[slot], (p_c, z)).wait_recv()
 
+    fq = pl.multiple_of(f * qtr, 16)
+    fo = pl.multiple_of((1 - f) * qtr, 16)
+    sq = pl.multiple_of(f * qtr + s * eig, 16)
+    so = pl.multiple_of(f * qtr + (1 - s) * eig, 16)
+
+    def g_sem(piece, slot):
+        return gr_s.at[piece, slot], gr_r.at[piece, slot]
+
+    def g_send(piece, slot, pair, dev):
+        send(lambda: (*pair(), *g_sem(piece, slot), dev))
+
+    def g_wait(piece, slot, dst):
+        remote(dst, dst, *g_sem(piece, slot), (dp, z1)).wait_recv()
+
+    def add_into(dst, src, n):
+        def blk(j, carry):
+            sl = pl.ds(pl.multiple_of(j * 48, 16), 48)
+            dst[sl, :] = (dst[sl, :].astype(F32) + src[sl, :].astype(F32)).astype(BF)
+            return carry
+
+        lax.fori_loop(0, n // 48, blk, 0)
+
+    def part(piece, stage):
+        chain = CHAIN[piece]
+        return (sq, eig) if chain.index("S") < chain.index(stage) else (fq, qtr)
+
+    def g_fs(piece, k):
+        g_send(piece, k, lambda: (gr.at[piece, k, pl.ds(fo, qtr)], rf.at[piece, k]), (p_f, z))
+
+    def g_fr(piece, k):
+        g_wait(piece, k, rf.at[piece, k])
+        add_into(gr.at[piece, k, pl.ds(fq, qtr)], rf.at[piece, k], qtr)
+
+    def g_ss(piece, k):
+        g_send(piece, 4 + k, lambda: (gr.at[piece, k, pl.ds(so, eig)], rs.at[piece, k]), (p_s, z))
+
+    def g_sr(piece, k):
+        g_wait(piece, 4 + k, rs.at[piece, k])
+        add_into(gr.at[piece, k, pl.ds(sq, eig)], rs.at[piece, k], eig)
+
+    def g_1s(piece, k):
+        off, n = part(piece, "1")
+        slot = 0 if k == 3 else 1
+        g_send(
+            piece, 8 + slot, lambda: (gr.at[piece, k, pl.ds(off, n)], rz.at[piece, slot, pl.ds(0, n)]), (dp, z1)
+        )
+
+    def g_zr(piece, k, slot, stage):
+        off, n = part(piece, stage)
+        g_wait(piece, 8 + slot, rz.at[piece, slot, pl.ds(0, n)])
+        add_into(gr.at[piece, k, pl.ds(off, n)], rz.at[piece, slot, pl.ds(0, n)], n)
+
+    def g_1r(piece, k):
+        g_zr(piece, k, 0 if k == 2 else 1, "1")
+
+    def g_2s(piece, k):
+        off, n = part(piece, "2")
+        g_send(piece, 10, lambda: (gr.at[piece, 2, pl.ds(off, n)], rz.at[piece, 2, pl.ds(0, n)]), (dp, z2))
+
+    def g_2r(piece, k):
+        g_zr(piece, 0, 2, "2")
+
+    def local_out(piece):
+        return pltpu.make_async_copy(
+            gr.at[piece, 0, pl.ds(sq, eig)], grad_ref.at[piece, pl.ds(e0, eig)], loc_sem.at[5 + piece]
+        )
+
+    def g_s2s(piece, _):
+        for j, partner in enumerate(extra):
+            cp = remote(
+                gr.at[piece, 0, pl.ds(sq, eig)], rx.at[piece, j], e_s.at[piece, j], e_r.at[piece, j], (partner, z)
+            )
+            cp.start()
+            cp.wait()
+            add_into(gr.at[piece, 0, pl.ds(sq, eig)], rx.at[piece, j], eig)
+        g_send(
+            piece, 11, lambda: (gr.at[piece, 0, pl.ds(sq, eig)], grad_ref.at[piece, pl.ds(e0, eig)]), (p_s, z)
+        )
+        local_out(piece).start()
+
+    def g_s2r(piece, _):
+        g_wait(piece, 11, grad_ref.at[piece, pl.ds(eo, eig)])
+        local_out(piece).wait()
+        g_send(piece, 12, lambda: (grad_ref.at[piece, pl.ds(q0, qtr)],) * 2, (p_f, z))
+
+    def g_f2r(piece, _):
+        g_wait(piece, 12, grad_ref.at[piece, pl.ds(qo, qtr)])
+        g_send(piece, 13, lambda: (grad_ref.at[piece, pl.ds(h0, half)],) * 2, (p_c, z))
+
+    def g_c2r(piece, _):
+        g_wait(piece, 13, grad_ref.at[piece, pl.ds(ho, half)])
+
+    partners = [(p_c, z), (p_f, z), (p_s, z), (dp, z1), (dp, z2)] + [(e, z) for e in extra]
+
+    def v_copy(j):
+        return remote(vec_ref, vrecv.at[j], v_s.at[j], v_r.at[j], partners[j])
+
+    def v_send(j, _):
+        v_copy(j).start()
+
+    def v_recv(j, _):
+        v_copy(j).wait()
+        vec_ref[...] += vrecv[j]
+
+    events = {
+        "az1": a_z1, "az2": a_z2, "zf": a_zf, "s": a_s, "f": a_f, "c": a_c, "d": a_d,
+        "gFs": g_fs, "gFr": g_fr, "gSs": g_ss, "gSr": g_sr, "g1s": g_1s, "g1r": g_1r, "g2s": g_2s, "g2r": g_2r,
+        "gS2s": g_s2s, "gS2r": g_s2r, "gF2r": g_f2r, "gC2r": g_c2r, "vs": v_send, "vr": v_recv,
+    }
+
+    def do(listed):
+        for kind, piece, k in listed:
+            events[kind](piece, k)
+
+    def at(place, index):
+        for n, listed in PLAN.get(place, {}).items():
+            pl.when(index == n)(functools.partial(do, listed))
+
+    def once(place):
+        do(PLAN.get(place, {}).get(0, ()))
+
     for j, zz in enumerate((z1, z2, z3)):
         send(lambda j=j, zz=zz: (vin, bias.at[z], b_s.at[j], b_r.at[j], (dp, zz)))
-    a_z(ATT)
-    a_z(INN)
-    a_z(OUT)
+    once("x0")
     core_send(X_TOK, lambda: (tok, xs.at[pl.ds(rows, rows)]))
 
     for r in range(rows):
@@ -187,8 +365,17 @@
     first_row = (lax.broadcasted_iota(jnp.int32, (8, seq), 0) == 0).astype(F32).astype(BF)
     loads[0].wait()
 
-    def attend(t):
-        def row(r, carry):
+    def attend(i, carry):
+        t = shard_of(i)
+
+        def row(r, inner_carry):
+            at("att", i * rows + r)
+
+            @pl.when((i == 1) & (r == 0))
+            def _():
+                for j, zz in enumerate((z1, z2, z3)):
+                    remote(vin, bias.at[zz], b_s.at[j], b_r.at[j], (dp, zz)).wait_recv()
+
             x_row = xs[r]
             bias_rows = bias[t].astype(BF)[:, : 3 * ml]
             qkv[t, r] = (
@@ -205,50 +392,15 @@
                 prob_t = (exponent * (1.0 / total)).astype(BF)
                 prob[t, r, h] = prob_t
                 ka[t, r, pl.ds(3 * ml + h * DH, DH), :] = dot(value, prob_t, NN).astype(BF)
-            part = dot(ka[t, r, pl.ds(3 * ml, ml), :], wbuf[ATT, t, pl.ds(3 * ml, ml), :], TN)
+            part_sum = dot(ka[t, r, pl.ds(3 * ml, ml), :], wbuf[ATT, t, pl.ds(3 * ml, ml), :], TN)
             sl = pl.ds(pl.multiple_of(r * seq, 16), seq)
-            acc[sl, :] = acc[sl, :] + part
-            return carry
+            acc[sl, :] = acc[sl, :] + part_sum
+            return inner_carry
 
         lax.fori_loop(0, rows, row, 0)
-
-    def attend_loop(i, carry):
-        @pl.when(i == 1)
-        def _():
-            remote(vin, bias.at[z1], b_s.at[0], b_r.at[0], (dp, z1)).wait_recv()
-            remote(vin, bias.at[z2], b_s.at[1], b_r.at[1], (dp, z2)).wait_recv()
-            remote(vin, bias.at[z3], b_s.at[2], b_r.at[2], (dp, z3)).wait_recv()
-            a_s(ATT, 1)
-            a_zf(ATT)
-            a_s(ATT, 2)
-            a_f(ATT, 1)
-            a_s(INN, 1)
-            a_s(ATT, 3)
-            a_f(ATT, 2)
-            a_c(ATT, 1)
-            a_zf(INN)
-            a_s(INN, 2)
-            a_done(ATT, 1)
-
-        @pl.when(i == 2)
-        def _():
-            a_f(ATT, 3)
-            a_c(ATT, 2)
-            a_s(INN, 3)
-            a_f(INN, 1)
-            a_done(ATT, 2)
-
-        @pl.when(i == 3)
-        def _():
-            a_c(ATT, 3)
-            a_f(INN, 2)
-            a_c(INN, 1)
-            a_done(ATT, 3)
-
-        attend(shard_of(i))
-        return carry
-
-    lax.fori_loop(0, 4, attend_loop, 0)
+        return carry
+
+    lax.fori_loop(0, 4, attend, 0)
 
     rb = 32
 
@@ -265,10 +417,7 @@
     def vrow(j):
         return vin[pl.ds(j, 1), :]
 
-    a_f(INN, 3)
-    a_c(INN, 2)
-    a_zf(OUT)
-    a_f(OUT, 1)
+    once("n1")
 
     def norm1(j, carry):
         sl = pl.ds(pl.multiple_of(j * rb, 16), rb)
@@ -288,22 +437,7 @@
     loads[2].wait()
 
     def up(i, carry):
-        @pl.when(i == 1)
-        def _():
-            a_done(INN, 1)
-            a_f(OUT, 2)
-            a_c(INN, 3)
-
-        @pl.when(i == 2)
-        def _():
-            a_done(INN, 2)
-            a_c(OUT, 1)
-
-        @pl.when(i == 3)
-        def _():
-            a_done(INN, 3)
-            a_c(OUT, 2)
-
+        at("up", i)
         t = shard_of(i)
         tmp[...] = dot(nb[...], wbuf[INN, t], NN)
         b_row = bias[t, pl.ds(1, 1), :]
@@ -325,26 +459,14 @@
     loads[4].wait()
 
     def down(i, carry):
-        @pl.when(i == 1)
-        def _():
-            a_f(OUT, 3)
-            a_done(OUT, 1)
-
-        @pl.when(i == 2)
-        def _():
-            a_done(OUT, 2)
-            a_c(OUT, 3)
-
-        @pl.when(i == 3)
-        def _():
-            a_done(OUT, 3)
-
+        at("dn", i)
         t = shard_of(i)
         acc[...] += dot(af[t], wbuf[OUT, t], NN)
         return carry
 
     lax.fori_loop(0, 4, down, 0)
 
+    once("l2")
     vec_ref[...] = jnp.zeros_like(vec_ref)
 
     def add_vec(row, value):
@@ -368,107 +490,28 @@
     lax.fori_loop(0, tl // rb, norm2, 0)
     core_send(X_G, lambda: (g.at[pl.ds(0, tl)], g.at[pl.ds(tl, tl)]))
 
-    fq = pl.multiple_of(f * qtr, 16)
-    fo = pl.multiple_of((1 - f) * qtr, 16)
-    sq = pl.multiple_of(f * qtr + s * eig, 16)
-    so = pl.multiple_of(f * qtr + (1 - s) * eig, 16)
-
-    def g_sem(piece, slot):
-        return gr_s.at[piece, slot], gr_r.at[piece, slot]
-
-    def g_send(piece, slot, pair, dev):
-        send(lambda: (*pair(), *g_sem(piece, slot), dev))
-
-    def g_wait(piece, slot, dst):
-        remote(dst, dst, *g_sem(piece, slot), (dp, z1)).wait_recv()
-
-    def add_into(dst, src, n):
-        def blk(j, carry):
-            sl = pl.ds(pl.multiple_of(j * 48, 16), 48)
-            dst[sl, :] = (dst[sl, :].astype(F32) + src[sl, :].astype(F32)).astype(BF)
-            return carry
-
-        lax.fori_loop(0, n // 48, blk, 0)
-
-    def fs_dynamic(piece, k):
-        ssem, rsem = g_sem(piece, k)
-        remote(gr.at[piece, k, pl.ds(fo, qtr)], rf.at[piece, k], ssem, rsem, (p_f, z)).start()
-
-    def fr(piece, k):
-        g_wait(piece, k, rf.at[piece, k])
-        add_into(gr.at[piece, k, pl.ds(fq, qtr)], rf.at[piece, k], qtr)
-        if k == 3:
-            g_send(piece, 4, lambda: (gr.at[piece, 3, pl.ds(fq, qtr)], rz1.at[piece, 0]), (dp, z1))
-        if k == 1:
-            g_send(piece, 5, lambda: (gr.at[piece, 1, pl.ds(fq, qtr)], rz1.at[piece, 1]), (dp, z1))
-
-    def z1r2(piece):
-        g_wait(piece, 4, rz1.at[piece, 0])
-        add_into(gr.at[piece, 2, pl.ds(fq, qtr)], rz1.at[piece, 0], qtr)
-        g_send(piece, 6, lambda: (gr.at[piece, 2, pl.ds(fq, qtr)], rz2.at[piece]), (dp, z2))
-
-    def z1r0(piece):
-        g_wait(piece, 5, rz1.at[piece, 1])
-        add_into(gr.at[piece, 0, pl.ds(fq, qtr)], rz1.at[piece, 1], qtr)
-
-    def z2r(piece):
-        g_wait(piece, 6, rz2.at[piece])
-        add_into(gr.at[piece, 0, pl.ds(fq, qtr)], rz2.at[piece], qtr)
-        g_send(piece, 7, lambda: (gr.at[piece, 0, pl.ds(so, eig)], rs.at[piece]), (p_s, z))
-
-    def sr(piece):
-        g_wait(piece, 7, rs.at[piece])
-        mine = gr.at[piece, 0, pl.ds(sq, eig)]
-        add_into(mine, rs.at[piece], eig)
-        for j, partner in enumerate(extra):
-            cp = remote(mine, rx.at[piece, j], e_s.at[piece, j], e_r.at[piece, j], (partner, z))
-            cp.start()
-            cp.wait()
-            add_into(mine, rx.at[piece, j], eig)
-        g_send(
-            piece, 8, lambda: (gr.at[piece, 0, pl.ds(sq, eig)], grad_ref.at[piece, pl.ds(e0, eig)]), (p_s, z)
-        )
-        cp = pltpu.make_async_copy(mine, grad_ref.at[piece, pl.ds(e0, eig)], loc_sem.at[5 + piece])
-        cp.start()
-        return cp
-
-    local_out = {}
-
-    def sr_(piece):
-        local_out[piece] = sr(piece)
-
-    def s2r(piece):
-        g_wait(piece, 8, grad_ref.at[piece, pl.ds(eo, eig)])
-        local_out[piece].wait()
-        g_send(piece, 9, lambda: (grad_ref.at[piece, pl.ds(q0, qtr)],) * 2, (p_f, z))
-
-    def f2r(piece):
-        g_wait(piece, 9, grad_ref.at[piece, pl.ds(qo, qtr)])
-        g_send(piece, 10, lambda: (grad_ref.at[piece, pl.ds(h0, half)],) * 2, (p_c, z))
-
-    def c2r(piece):
-        g_wait(piece, 10, grad_ref.at[piece, pl.ds(ho, half)])
-
     def order(i):
         return 3 - 2 * (i % 2) - i // 2
 
     def ffn_back(i, carry):
         @pl.when(i < 4)
         def _():
+            at("da", i)
             k = order(i)
             t = shard_of(k)
             tmp[...] = dot(g[pl.ds(0, tl), :], wbuf[OUT, t], NT)
 
-            def act(j, carry):
+            def act(j, total):
                 sl = pl.ds(pl.multiple_of(j * rb, 16), rb)
                 blk = (tmp[sl, :] * gp[t, sl, :].astype(F32)).astype(BF)
                 di[t, sl, :] = blk
-                return carry + jnp.sum(blk.astype(F32), 0, keepdims=True)
+                return total + jnp.sum(blk.astype(F32), 0, keepdims=True)
 
             vec_ref[pl.ds(4 + t, 1), :] = lax.fori_loop(0, tl // rb, act, jnp.zeros((1, d), F32))
             remote(
                 di.at[t, pl.ds(0, tl)], di.at[t, pl.ds(tl, tl)], x_s.at[X_DI + k], x_r.at[X_DI + k], (p_c, z)
             ).start()
+            at("gwo", i)
 
             @pl.when(i == 0)
             def _():
@@ -479,28 +522,21 @@
             al[pl.ds(0, tl), :] = af[t, :, pl.ds(h0, half)]
             al[pl.ds(tl, tl), :] = asib[t]
             gr[OUT, k] = dot(al[...], g[...], TN).astype(BF)
-            fs_dynamic(OUT, k)
+            at("dn2", i)
             acc[...] += dot(di[t, pl.ds(0, tl), :], wbuf[INN, t], NT)
-
-        @pl.when(i == 2)
-        def _():
-            fr(OUT, 3)
-
-        @pl.when(i == 4)
-        def _():
-            fr(OUT, 1)
 
         @pl.when(i > 0)
         def _():
+            at("gwi", i - 1)
             k = order(i - 1)
             t = shard_of(k)
             core_wait(X_DI + k, di.at[t, pl.ds(tl, tl)])
             gr[INN, k] = dot(nhalf[...], di[t], TN).astype(BF)
-            fs_dynamic(INN, k)
 
         return carry
 
     lax.fori_loop(0, 5, ffn_back, 0)
+    once("l1b")
 
     def norm1_back(j, carry):
         sl = pl.ds(pl.multiple_of(j * rb, 16), rb)
@@ -520,36 +556,35 @@
     core_send(X_FG, lambda: (fg.at[pl.ds(0, rows)], fg.at[pl.ds(rows, rows)]))
     ones = jnp.ones((8, seq), BF)
 
-    def attend_back(t):
-        def row(r, carry):
-            dctx = dot(wbuf[ATT, t, pl.ds(3 * ml, ml), :], fg[r], NT).astype(BF)
-            for h in range(hs):
-                query = qkv[t, r, pl.ds(h * DH, DH), :]
-                key = qkv[t, r, pl.ds(ml + h * DH, DH), :]
-                value = qkv[t, r, pl.ds(2 * ml + h * DH, DH), :]
-                prob_t = prob[t, r, h]
-                grad = dctx[h * DH : (h + 1) * DH]
-                ka[t, r, pl.ds(2 * ml + h * DH, DH), :] = dot(grad, prob_t, NT).astype(BF)
-                prob_grad = dot(value, grad, TN)
-                wide_prob = prob_t.astype(F32)
-                inner = jnp.sum(wide_prob * prob_grad, 0, keepdims=True)
-                score_grad = (wide_prob * (prob_grad - inner)).astype(BF)
-                ka[t, r, pl.ds(h * DH, DH), :] = (dot(key, score_grad, NN) * scale).astype(BF)
-                ka[t, r, pl.ds(ml + h * DH, DH), :] = (dot(query, score_grad, NT) * scale).astype(BF)
-            grads = ka[t, r, pl.ds(0, 3 * ml), :]
-            vec_ref[pl.ds(t, 1), pl.ds(0, 3 * ml)] += dot(ones, grads, NT)[0:1]
-            sl = pl.ds(pl.multiple_of(r * seq, 16), seq)
-            acc[sl, :] = acc[sl, :] + dot(grads, wbuf[ATT, t, pl.ds(0, 3 * ml), :], TN)
-            return carry
-
-        lax.fori_loop(0, rows, row, 0)
-
     def att_back(i, carry):
         @pl.when(i < 4)
         def _():
             k = order(i)
             t = shard_of(k)
-            attend_back(t)
+
+            def row(r, inner_carry):
+                at("ab", i * rows + r)
+                dctx = dot(wbuf[ATT, t, pl.ds(3 * ml, ml), :], fg[r], NT).astype(BF)
+                for h in range(hs):
+                    query = qkv[t, r, pl.ds(h * DH, DH), :]
+                    key = qkv[t, r, pl.ds(ml + h * DH, DH), :]
+                    value = qkv[t, r, pl.ds(2 * ml + h * DH, DH), :]
+                    prob_t = prob[t, r, h]
+                    grad = dctx[h * DH : (h + 1) * DH]
+                    ka[t, r, pl.ds(2 * ml + h * DH, DH), :] = dot(grad, prob_t, NT).astype(BF)
+                    prob_grad = dot(value, grad, TN)
+                    wide_prob = prob_t.astype(F32)
+                    inner = jnp.sum(wide_prob * prob_grad, 0, keepdims=True)
+                    score_grad = (wide_prob * (prob_grad - inner)).astype(BF)
+                    ka[t, r, pl.ds(h * DH, DH), :] = (dot(key, score_grad, NN) * scale).astype(BF)
+                    ka[t, r, pl.ds(ml + h * DH, DH), :] = (dot(query, score_grad, NT) * scale).astype(BF)
+                grads = ka[t, r, pl.ds(0, 3 * ml), :]
+                vec_ref[pl.ds(t, 1), pl.ds(0, 3 * ml)] += dot(ones, grads, NT)[0:1]
+                sl = pl.ds(pl.multiple_of(r * seq, 16), seq)
+                acc[sl, :] = acc[sl, :] + dot(grads, wbuf[ATT, t, pl.ds(0, 3 * ml), :], TN)
+                return inner_carry
+
+            lax.fori_loop(0, rows, row, 0)
             remote(
                 ka.at[t, :, pl.ds(ho, half)], ks.at[t], x_s.at[X_KA + k], x_r.at[X_KA + k], (p_c, z)
             ).start()
@@ -558,31 +593,10 @@
         def _():
             core_wait(X_TOK, xs.at[pl.ds(rows, rows)])
             core_wait(X_FG, fg.at[pl.ds(rows, rows)])
-            fr(OUT, 2)
-            fr(OUT, 0)
-
-        @pl.when(i == 1)
-        def _():
-            z1r2(OUT)
-            fr(INN, 3)
-
-        @pl.when(i == 2)
-        def _():
-            z1r0(OUT)
-            fr(INN, 1)
-
-        @pl.when(i == 3)
-        def _():
-            z2r(OUT)
-            fr(INN, 2)
-
-        @pl.when(i == 4)
-        def _():
-            fr(INN, 0)
-            z1r2(INN)
 
         @pl.when(i > 0)
         def _():
+            at("gwa", i - 1)
             k = order(i - 1)
             t = shard_of(k)
             core_wait(X_KA + k, ks.at[t])
@@ -596,11 +610,11 @@
                     total += dot(ka[t, r, rowsel, :], right_own, NN)
                     total += dot(ks[t, r, pl.ds(j * ml, ml), :], right_sib, NN)
                 gr[ATT, k, pl.ds(j * ml, ml), :] = total.astype(BF)
-            fs_dynamic(ATT, k)
 
         return carry
 
     lax.fori_loop(0, 5, att_back, 0)
+    once("fin")
 
     def finish(j, carry):
         sl = pl.ds(pl.multiple_of(j * rb, 16), rb)
@@ -609,50 +623,10 @@
 
     lax.fori_loop(0, tl // rb, finish, 0)
 
-    partners = [(p_c, z), (p_f, z), (p_s, z)] + [(e, z) for e in extra] + [(dp, z1), (dp, z2)]
-
-    def v_step(j):
-        cp = remote(vec_ref, vrecv.at[j], v_s.at[j], v_r.at[j], partners[j])
-        cp.start()
-        return cp
-
-    def v_end(cp, j):
-        cp.wait()
-        vec_ref[...] += vrecv[j]
-
-    v0 = v_step(0)
-    sr_(OUT)
-    z1r0(INN)
-    v_end(v0, 0)
-    v1 = v_step(1)
-    fr(ATT, 3)
-    z2r(INN)
-    fr(ATT, 1)
-    s2r(OUT)
-    v_end(v1, 1)
-    v2 = v_step(2)
-    fr(ATT, 2)
-    sr_(INN)
-    f2r(OUT)
-    fr(ATT, 0)
-    v_end(v2, 2)
-    v3 = v_step(3)
-    z1r2(ATT)
-    s2r(INN)
-    z1r0(ATT)
-    v_end(v3, 3)
-    v4 = v_step(4)
-    f2r(INN)
-    z2r(ATT)
-    v_end(v4, 4)
+    once("end")
     for j in range(5, len(partners)):
-        v_end(v_step(j), j)
-    sr_(ATT)
-    s2r(ATT)
-    f2r(ATT)
-    c2r(OUT)
-    c2r(INN)
-    c2r(ATT)
+        v_send(j, 0)
+        v_recv(j, 0)
 
     for make in pending:
         remote(*make()).wait_send()
@@ -664,9 +638,6 @@
             di.at[t, pl.ds(0, tl)], di.at[t, pl.ds(tl, tl)], x_s.at[X_DI + k], x_r.at[X_DI + k], (p_c, z)
         ).wait_send()
         remote(ka.at[t, :, pl.ds(ho, half)], ks.at[t], x_s.at[X_KA + k], x_r.at[X_KA + k], (p_c, z)).wait_send()
-        for piece in range(3):
-            ssem, rsem = g_sem(piece, k)
-            remote(gr.at[piece, k, pl.ds(fo, qtr)], rf.at[piece, k], ssem, rsem, (p_f, z)).wait_send()
         return carry
 
     lax.fori_loop(0, 4, sent, 0)
@@ -760,17 +731,16 @@
         pltpu.VMEM((tl, d), F32),
         pltpu.VMEM((3, 4, half, d), BF),
         pltpu.VMEM((3, 4, qtr, d), BF),
-        pltpu.VMEM((3, 2, qtr, d), BF),
-        pltpu.VMEM((3, qtr, d), BF),
-        pltpu.VMEM((3, eig, d), BF),
+        pltpu.VMEM((3, 3, qtr, d), BF),
+        pltpu.VMEM((3, 4, eig, d), BF),
         pltpu.VMEM((3, n_extra, eig, d), BF) if bits > 3 else pltpu.VMEM((1, 1, 16, 128), BF),
         pltpu.VMEM((n_vec, 16, d), F32),
         pltpu.VMEM((8, d), F32),
         pltpu.SemaphoreType.DMA((11,)),
         pltpu.SemaphoreType.DMA((3, 12)),
         pltpu.SemaphoreType.DMA((3, 12)),
-        pltpu.SemaphoreType.DMA((3, 11)),
-        pltpu.SemaphoreType.DMA((3, 11)),
+        pltpu.SemaphoreType.DMA((3, 14)),
+        pltpu.SemaphoreType.DMA((3, 14)),
         pltpu.SemaphoreType.DMA((16,)),
         pltpu.SemaphoreType.DMA((16,)),
         pltpu.SemaphoreType.DMA((3,)),

time: 187 us -> 157 us (0.84)
  Pallas kernels: 186 us -> 156 us
    pallas_call x1, Pallas kernels: 180 us -> 151 us  [per_device(): pl.pallas_call(functools.partial(layer_kernel, cfg), out_shape=(jax.Shape...]
where the time goes in v3:
time: 157 us
  Pallas kernels  156 us (99%)
    pallas_call x1, Pallas kernels, per_device(): pl.pallas_call(functools.partial(layer_kernel, cfg), out_shape=(jax.Shape...  151 us
    pallas_call x1, Pallas kernels, per_device(): pl.pallas_call(functools.partial(spread_kernel, ml), out_shape=tuple((jax...  5.36 us

profile of v3, /device:TPU:0, one launch (start us, length us, event | category | flops | bytes accessed | tf_op | source)
XLA Modules:
  0.0 156.9 jit_solution(15087595135464659483)
XLA Ops:
  0.7 150.9 %layer.1 = (bf16[320,768]{1,0:T(8,128)(2,1)}, bf16[320,768]{1,0:T(8,128)(2,1)}, bf16[3,768,768]{2,1,0:T(8,128)(2,1)}, f32[16,768]{1,0:T(8,128)}) custom-call(bf16[2,160,768]{2,1,0:T(8,128)(2,1)} %bitcast.7, bf16[320,768]{1,0:T(8,128)(2,1)} %cot.1, bf16[192,768]{1,0:T(8,128)(2,1)} %bitcast.8, bf16[192,768]{1,0:T(8,128)(2,1)} %bitcast.9, ...), custom_call_target="tpu_custom_call" | custom-call | tf_op jit(solution)/shard_map/layer/pallas_call | solution.py:753
  151.5 5.4 %spread.1 = (bf16[320,768]{1,0:T(8,128)(2,1)}, bf16[320,768]{1,0:T(8,128)(2,1)}, f32[192,768]{1,0:T(8,128)}, f32[192,768]{1,0:T(8,128)}, f32[192,768]{1,0:T(8,12...) custom-call(bf16[3,768,768]{2,1,0:T(8,128)(2,1)} %get-tuple-element., ...), custom_call_target="tpu_custom_call" | custom-call | tf_op jit(solution)/shard_map/spread/pallas_call | solution.py:774

commit v4 on v3

--- a/solution.py
+++ b/solution.py
@@ -21,66 +21,88 @@
 TN = (((0,), (0,)), ((), ()))
 
 ATT, INN, OUT = 0, 1, 2
-WIDE = (False, False, True)
-CHAIN = ("FS12", "F12S", "F12S")
+GATHERED = (
+    (0, 0, 384, False),
+    (0, 384, 384, False),
+    (1, 0, 384, False),
+    (1, 384, 384, True),
+    (2, 0, 384, False),
+    (2, 384, 384, True),
+)
+SUMMED = (
+    (0, 0, 192, "FS12"),
+    (0, 192, 192, "FS12"),
+    (1, 0, 192, "F12S"),
+    (1, 192, 192, "F12S"),
+    (2, 0, 192, "F12S"),
+    (2, 192, 192, "F12S"),
+)
 PLAN = {
     "x0": {
-        0: (("az2", 0, 0), ("az1", 0, 0),),
+        0: (("az1", 0, 0), ("az2", 0, 0), ("az1", 1, 0), ("az2", 1, 0), ("s", 0, 1), ("zf", 0, 0), ("s", 0, 2), ("s", 1, 1), ("az2", 2, 0), ("az1", 2, 0), ("f", 0, 1), ("zf", 1, 0), ("f", 1, 1),),
     },
     "att": {
-        0: (("zf", 0, 0), ("s", 0, 2),),
-        1: (("s", 0, 1), ("az1", 1, 0), ("f", 0, 2), ("az2", 1, 0),),
-        2: (("f", 0, 1), ("az1", 2, 0), ("s", 1, 1), ("f", 1, 1), ("s", 0, 3), ("c", 0, 1), ("d", 0, 1), ("zf", 1, 0), ("c", 0, 2), ("s", 1, 2), ("az2", 2, 0), ("d", 0, 2), ("f", 2, 1),),
-        3: (("f", 0, 3), ("c", 1, 1), ("f", 1, 2),),
-        4: (("d", 1, 1),),
-        5: (("s", 1, 3), ("c", 2, 1),),
-        6: (("c", 0, 3), ("zf", 2, 0), ("c", 1, 2), ("d", 0, 3), ("f", 2, 2),),
-        7: (("f", 1, 3),),
+        0: (("s", 1, 2), ("az1", 3, 0), ("c", 0, 1), ("f", 0, 2), ("az2", 3, 0),),
+        1: (("s", 2, 1), ("f", 1, 2), ("c", 1, 1), ("zf", 2, 0), ("s", 2, 2), ("s", 0, 3), ("az2", 4, 0), ("az1", 4, 0), ("c", 0, 2),),
+        2: (("f", 2, 1), ("d", 1, 1), ("d", 0, 1),),
+        3: (("f", 3, 1), ("f", 0, 3), ("d", 0, 2), ("s", 1, 3), ("az2", 5, 0), ("az1", 5, 0), ("f", 1, 3), ("s", 4, 1), ("c", 1, 2), ("zf", 4, 0), ("s", 2, 3), ("zf", 3, 0), ("f", 2, 2),),
+        4: (("d", 1, 2), ("s", 4, 2), ("c", 0, 3), ("f", 3, 2),),
+        5: (("f", 4, 1), ("f", 5, 1), ("d", 0, 3), ("c", 1, 3), ("f", 2, 3), ("zf", 5, 0), ("c", 2, 2), ("f", 5, 2),),
+        6: (("c", 2, 1), ("c", 4, 1), ("c", 3, 1), ("c", 3, 2), ("d", 1, 3), ("s", 4, 3), ("f", 3, 3), ("c", 5, 1),),
+        7: (("f", 4, 2), ("d", 3, 1), ("d", 2, 1), ("d", 3, 2), ("c", 2, 3),),
     },
     "n1": {
+        0: (("f", 4, 3), ("c", 5, 2), ("c", 3, 3), ("d", 2, 3), ("d", 2, 2), ("f", 5, 3),),
     },
     "up": {
-        0: (("d", 2, 1), ("f", 2, 3),),
-        2: (("c", 1, 3), ("d", 1, 2), ("c", 2, 2),),
-        3: (("c", 2, 3), ("d", 1, 3),),
+        2: (("c", 4, 2),),
+        3: (("d", 3, 3), ("c", 4, 3),),
     },
     "dn": {
-        1: (("d", 2, 2),),
-        3: (("d", 2, 3),),
+        1: (("d", 5, 1), ("d", 4, 2), ("d", 4, 1), ("c", 5, 3),),
+        2: (("d", 5, 2),),
+        3: (("d", 4, 3), ("d", 5, 3),),
     },
     "l2": {
     },
     "da": {
+        2: (("gFr", 5, 3), ("gFs", 2, 3), ("g1s", 5, 3), ("gFs", 4, 1),),
     },
     "gwo": {
-        2: (("gFr", 2, 3), ("g1s", 2, 3), ("gFs", 1, 3),),
+        3: (("g1s", 5, 1),),
     },
     "dn2": {
-        0: (("gFs", 2, 3),),
-        1: (("gFs", 2, 1),),
-        3: (("gFr", 2, 1),),
+        0: (("gFs", 5, 3), ("gFs", 4, 3),),
+        1: (("gFs", 5, 1),),
+        3: (("gFs", 2, 1),),
     },
     "gwi": {
+        1: (("gFr", 4, 3), ("gFs", 4, 2), ("g1s", 4, 3), ("gFs", 3, 3), ("gFr", 5, 1), ("gFs", 5, 2),),
+        3: (("gFs", 3, 2), ("gFs", 4, 0),),
+    },
+    "l1b": {
+        0: (("gFr", 4, 1), ("gFr", 4, 2),),
+    },
+    "ab": {
+        0: (("g1r", 4, 2), ("gFs", 5, 0), ("g1s", 4, 1),),
         1: (("gFs", 2, 2),),
-        2: (("g1s", 2, 1),),
-        3: (("gFs", 1, 2),),
-    },
-    "l1b": {
-        0: (("gFs", 1, 0),),
-    },
-    "ab": {
-        0: (("gFr", 1, 3), ("gFr", 2, 2), ("g1s", 1, 3), ("gFs", 2, 0), ("g1r", 2, 2), ("g2s", 2, 2), ("gFs", 1, 1),),
-        4: (("gFs", 0, 3),),
-        6: (("gFs", 0, 1), ("gFr", 1, 1), ("gFr", 2, 0), ("g1s", 1, 1), ("gFr", 1, 2),),
-        7: (("g1r", 1, 2), ("gFr", 0, 3), ("g1r", 2, 0), ("gSs", 0, 3), ("g2s", 1, 2), ("g2r", 2, 0), ("gSs", 2, 0),),
+        2: (("gFs", 2, 0), ("gFs", 3, 0), ("g2s", 4, 2),),
+        3: (("gFr", 2, 3), ("gFr", 2, 1), ("gFr", 5, 2), ("gFr", 3, 3), ("g1s", 2, 3),),
+        4: (("gFr", 4, 0),),
+        5: (("g1s", 3, 3), ("gFs", 0, 3), ("g1r", 5, 2), ("gFr", 5, 0), ("g1r", 4, 0), ("gFs", 1, 3),),
+        6: (("g2s", 5, 2),),
+        7: (("gFs", 0, 1), ("g2r", 4, 0), ("gSs", 4, 0),),
     },
     "gwa": {
-        3: (("gFr", 0, 1), ("gFs", 0, 2), ("gSs", 0, 1),),
+        0: (("gFs", 3, 1),),
+        2: (("gFr", 3, 2), ("gFr", 3, 1), ("gFr", 0, 3), ("gFs", 1, 1), ("gFr", 2, 2), ("g1s", 2, 1), ("gFr", 3, 0), ("gFr", 1, 3),),
+        3: (("gFs", 1, 2), ("g1r", 2, 2), ("gFr", 0, 1), ("gSr", 4, 0), ("gSs", 1, 3), ("g2s", 2, 2), ("gSs", 0, 1),),
     },
     "fin": {
+        0: (("g1s", 3, 1), ("gFr", 2, 0), ("gFs", 1, 0),),
     },
     "end": {
-        0: (("gSr", 2, 0), ("vs", 0, 0), ("gSr", 0, 3), ("vr", 0, 0), ("gFr", 1, 0), ("gS2s", 2, 0), ("gFr", 0, 2), ("vs", 1, 0), ("gFs", 0, 0), ("gSs", 0, 2), ("g1s", 0, 3), ("g1r", 1, 0), ("vr", 1, 0), ("g2r", 1, 0), ("gS2r", 2, 0), ("gSr", 0, 2), ("gSs", 1, 0), ("g1r", 0, 2), ("gFr", 0, 0), ("gSr", 0, 1), ("g2s", 0, 2), ("gSs", 0, 0), ("g1s", 0, 1), ("vs", 2, 0), ("gSr", 1, 0), ("gF2r", 2, 0), ("gS2s", 1, 0), ("gSr", 0, 0), ("g1r", 0, 0), ("g2r", 0, 0), ("gS2s", 0, 0), ("gS2r", 1, 0), ("gC2r", 2, 0), ("gS2r", 0, 0), ("vr", 2, 0), ("vs", 3, 0), ("vr", 3, 0), ("gF2r", 1, 0), ("vs", 4, 0), ("gF2r", 0, 0), ("vr", 4, 0), ("gC2r", 0, 0), ("gC2r", 1, 0),),
+        0: (("g1r", 3, 2), ("gFs", 0, 2), ("gFs", 0, 0), ("g2s", 3, 2), ("gSs", 0, 3), ("gSr", 0, 1), ("g1r", 2, 0), ("gFr", 1, 2), ("gSs", 1, 2), ("gSr", 1, 3), ("gFr", 0, 2), ("g1r", 5, 0), ("vs", 0, 0), ("gSs", 0, 2), ("vr", 0, 0), ("gS2s", 4, 0), ("g2r", 5, 0), ("gSr", 0, 3), ("vs", 1, 0), ("g1s", 0, 3), ("g2r", 2, 0), ("g1r", 3, 0), ("gFr", 1, 1), ("gFr", 1, 0), ("gFr", 0, 0), ("gSs", 1, 1), ("g1s", 1, 3), ("gSs", 5, 0), ("gSr", 0, 2), ("gSs", 2, 0), ("vr", 1, 0), ("gS2r", 4, 0), ("gSr", 5, 0), ("gSs", 1, 0), ("gSr", 1, 1), ("gS2s", 5, 0), ("g1r", 0, 2), ("gSs", 0, 0), ("gSr", 1, 2), ("g2s", 0, 2), ("g1s", 1, 1), ("g2r", 3, 0), ("g1r", 1, 2), ("gSs", 3, 0), ("gSr", 2, 0), ("gS2r", 5, 0), ("g1s", 0, 1), ("gSr", 1, 0), ("gS2s", 2, 0), ("vs", 2, 0), ("g2s", 1, 2), ("gSr", 0, 0), ("gSr", 3, 0), ("gS2s", 3, 0), ("g1r", 1, 0), ("gS2r", 2, 0), ("g1r", 0, 0), ("g2r", 0, 0), ("gF2r", 4, 0), ("gS2s", 0, 0), ("vr", 2, 0), ("g2r", 1, 0), ("gS2s", 1, 0), ("vs", 3, 0), ("gS2r", 3, 0), ("gS2r", 0, 0), ("gS2r", 1, 0), ("vr", 3, 0), ("gC2r", 4, 0), ("gF2r", 5, 0), ("gF2r", 2, 0), ("vs", 4, 0), ("gC2r", 2, 0), ("gF2r", 0, 0), ("vr", 4, 0), ("gF2r", 3, 0), ("gC2r", 0, 0), ("gF2r", 1, 0), ("gC2r", 5, 0), ("gC2r", 1, 0), ("gC2r", 3, 0),),
     },
 }
 V_OB, V_G1, V_S1, V_EB, V_G2, V_S2 = 8, 9, 10, 11, 12, 13
@@ -90,14 +112,24 @@
     return lax.dot_general(left, right, dims, preferred_element_type=F32)
 
 
+def depth_at(p, stage):
+    done = SUMMED[p][3].split(stage)[0]
+    return ("F" in done) + ("S" in done)
+
+
+def z_rows(p, slot):
+    sizes = {(q, t): SUMMED[q][2] >> depth_at(q, "2" if t == 2 else "1") for q in range(len(SUMMED)) for t in range(3)}
+    return sum(n for key, n in sizes.items() if key < (p, slot)), sizes[p, slot]
+
+
 def layer_kernel(
     cfg,
-    tok, cot, wq, wk, wv, wo, wi, wout, bq, bv, bi, bo, g1, s1, be, g2, s2, seg, live,
-    out_ref, dx_ref, grad_ref, vec_ref,
+    tok, cot, wq, wk, wv, wo, wi, wout, bq, bv, bi, bo, g1, s1, be, g2, s2, seg_in, live_in,
+    out_hbm, dx_hbm, grad_ref, vec_hbm,
     wbuf, bias, xs, cots, qkv, ka, ks, prob, mask, acc, tmp, nh1, r1,
-    nb, nhalf, af, asib, al, gp, g, sg, di, fg, fgf,
+    nb, nhalf, af, asib, al, gp, g, sg, di, fg, whole,
     gr, rf, rz, rs, rx, vrecv, vin,
-    loc_sem, ag_s, ag_r, gr_s, gr_r, x_s, x_r, b_s, b_r, v_s, v_r, e_s, e_r,
+    dx_ref, vec_ref, seg, live, *rest,
 ):
     n_dp, d, seq, rows = cfg["dp"], cfg["d"], cfg["seq"], cfg["rows"]
     tl = seq * rows
@@ -116,10 +148,39 @@
     z1, z2, z3 = z + 1 - 2 * z0, z + 2 - 4 * zh, 3 - z
     h0 = pl.multiple_of(c * half, 128)
     ho = pl.multiple_of((1 - c) * half, 128)
-    q0 = pl.multiple_of(c * half + f * qtr, 16)
-    e0 = pl.multiple_of(c * half + f * qtr + s * eig, 16)
-    qo = pl.multiple_of(c * half + (1 - f) * qtr, 16)
-    eo = pl.multiple_of(c * half + f * qtr + (1 - s) * eig, 16)
+
+    def sub(base, n, depth, other=False):
+        off = base
+        for level, bit in enumerate((c, f, s)[:depth]):
+            n //= 2
+            off = off + n * (1 - bit if other and level == depth - 1 else bit)
+        return (pl.multiple_of(off, 16) if depth else off), n
+
+    def cut(base, n, depth, other=False):
+        off = base
+        for level, bit in enumerate((f, s)[:depth]):
+            n //= 2
+            off = off + n * (1 - bit if other and level == depth - 1 else bit)
+        return (pl.multiple_of(off, 16) if depth else off), n
+
+    gathered = {}
+    for a, (piece, base, n, wide) in enumerate(GATHERED):
+        for depth in (1, 2, 3):
+            for other in (False, True):
+                gathered[a, depth, other] = sub(base, n, depth, other)
+    summed = {}
+    for p, (piece, base, n, chain) in enumerate(SUMMED):
+        for depth in (0, 1, 2):
+            for other in (False, True):
+                summed[p, depth, other] = cut(base, n, depth, other)
+
+    finals = {}
+    for p, (piece, base, n, chain) in enumerate(SUMMED):
+        for depth in (0, 1, 2):
+            for other in (False, True):
+                off, m = summed[p, depth, other]
+                finals[p, depth, other] = (pl.multiple_of(c * half + off, 16), m)
+        finals[p, "core", True] = (pl.multiple_of((1 - c) * half + base, 16), n)
     shard = (z, z1, z2, z3)
 
     def shard_of(k):
@@ -137,31 +198,35 @@
         remote(*make()).start()
         pending.append(make)
 
-    loads = [
-        pltpu.make_async_copy(tok, xs.at[pl.ds(0, rows)], loc_sem.at[0]),
-        pltpu.make_async_copy(wo, wbuf.at[ATT, z, pl.ds(3 * ml, ml)], loc_sem.at[1]),
-        pltpu.make_async_copy(wi, wbuf.at[INN, z], loc_sem.at[2]),
-        pltpu.make_async_copy(wout, wbuf.at[OUT, z], loc_sem.at[3]),
-        pltpu.make_async_copy(cot, cots, loc_sem.at[4]),
-    ] + [
-        pltpu.make_async_copy(ref, wbuf.at[ATT, z, pl.ds(j * ml, ml)], loc_sem.at[8 + j])
-        for j, ref in enumerate((wq, wk, wv))
-    ]
-    for cp in loads:
-        cp.start()
+    small = rest[:9]
+    loc_sem, ag_s, ag_r, gr_s, gr_r, x_s, x_r, b_s, b_r, v_s, v_r, e_s, e_r, out_sem = rest[9:]
     barrier = pltpu.get_barrier_semaphore()
     extra = [dp + (1 << b) * (1 - 2 * ((dp // (1 << b)) % 2)) for b in range(3, bits)]
     greet = [(p_c, z), (p_f, z), (p_s, z), (dp, z1), (dp, z2), (dp, z3)] + [(e, z) for e in extra]
     for dev in greet:
         pl.semaphore_signal(barrier, inc=1, device_id=dev, device_id_type=MESH)
-    vin[...] = jnp.zeros_like(vin)
-    vin[pl.ds(0, 1), pl.ds(0, ml)] = bq[...].astype(F32).reshape(1, ml)
-    vin[pl.ds(0, 1), pl.ds(2 * ml, ml)] = bv[...].astype(F32).reshape(1, ml)
-    for j, ref in enumerate((bi, bo, g1, s1, be, g2, s2)):
-        vin[pl.ds(j + 1, 1), :] = ref[...].astype(F32).reshape(1, d)
-    bias[z] = vin[...]
-    for j in (1, 5, 6, 7):
-        loads[j].wait()
+    att_loads = [
+        pltpu.make_async_copy(ref, wbuf.at[ATT, z, pl.ds(j * ml, ml)], loc_sem.at[j])
+        for j, ref in enumerate((wq, wk, wv, wo))
+    ]
+    vec_loads = [
+        pltpu.make_async_copy(ref, dst, loc_sem.at[4 + j])
+        for j, (ref, dst) in enumerate(zip((bq, bv, bi, bo, g1, s1, be, g2, s2), small))
+    ]
+    seg_loads = [
+        pltpu.make_async_copy(seg_in, seg, loc_sem.at[13]),
+        pltpu.make_async_copy(live_in, live, loc_sem.at[14]),
+        pltpu.make_async_copy(tok, xs.at[pl.ds(0, rows)], loc_sem.at[15]),
+    ]
+    late_loads = [
+        pltpu.make_async_copy(wi, wbuf.at[INN, z], loc_sem.at[16]),
+        pltpu.make_async_copy(wout, wbuf.at[OUT, z], loc_sem.at[17]),
+        pltpu.make_async_copy(cot, cots, loc_sem.at[18]),
+    ]
+    for cp in att_loads + vec_loads + seg_loads + late_loads:
+        cp.start()
+    for cp in att_loads:
+        cp.wait()
     pl.semaphore_wait(barrier, len(greet))
 
     def own(piece, off, n):
@@ -172,52 +237,53 @@
     def reg(piece, k, off, n):
         return wbuf.at[piece, shard[k], pl.ds(off, n)]
 
-    def ag_send(piece, slot, where, dev, mine=False):
+    def ag_send(a, slot, k, rows_of, dev, mine=False):
+        piece = GATHERED[a][0]
+
         def make():
-            region = reg(piece, *where)
-            src = own(piece, *where[1:]) if mine else region
-            return src, region, ag_s.at[piece, slot], ag_r.at[piece, slot], dev
+            region = reg(piece, k, *rows_of)
+            return own(piece, *rows_of) if mine else region, region, ag_s.at[a, slot], ag_r.at[a, slot], dev
 
         send(make)
 
-    def ag_wait(piece, slot, where):
-        region = reg(piece, *where)
-        remote(region, region, ag_s.at[piece, slot], ag_r.at[piece, slot], (dp, z1)).wait_recv()
-
-    def first(piece):
-        return (q0, qtr) if WIDE[piece] else (e0, eig)
-
-    def a_z1(piece, _):
-        ag_send(piece, 1, (0, *first(piece)), (dp, z1), True)
-
-    def a_z2(piece, _):
-        ag_send(piece, 0, (0, *first(piece)), (dp, z2), True)
-
-    def a_zf(piece, _):
-        ag_wait(piece, 0, (2, *first(piece)))
-        ag_send(piece, 2, (2, *first(piece)), (dp, z1))
-
-    def a_arrive(piece, k):
+    def ag_wait(a, slot, k, rows_of):
+        region = reg(GATHERED[a][0], k, *rows_of)
+        remote(region, region, ag_s.at[a, slot], ag_r.at[a, slot], (dp, z1)).wait_recv()
+
+    def first(a):
+        return gathered[a, 2 if GATHERED[a][3] else 3, False]
+
+    def a_z1(a, _):
+        ag_send(a, 1, 0, first(a), (dp, z1), True)
+
+    def a_z2(a, _):
+        ag_send(a, 0, 0, first(a), (dp, z2), True)
+
+    def a_zf(a, _):
+        ag_wait(a, 0, 2, first(a))
+        ag_send(a, 2, 2, first(a), (dp, z1))
+
+    def a_arrive(a, k):
         if k != 2:
-            ag_wait(piece, {1: 1, 3: 2}[k], (k, *first(piece)))
-
-    def a_s(piece, k):
-        a_arrive(piece, k)
-        ag_send(piece, 2 + k, (k, e0, eig), (p_s, z))
-
-    def a_f(piece, k):
-        if WIDE[piece]:
-            a_arrive(piece, k)
+            ag_wait(a, {1: 1, 3: 2}[k], k, first(a))
+
+    def a_s(a, k):
+        a_arrive(a, k)
+        ag_send(a, 2 + k, k, gathered[a, 3, False], (p_s, z))
+
+    def a_f(a, k):
+        if GATHERED[a][3]:
+            a_arrive(a, k)
         else:
-            ag_wait(piece, 2 + k, (k, eo, eig))
-        ag_send(piece, 5 + k, (k, q0, qtr), (p_f, z))
-
-    def a_c(piece, k):
-        ag_wait(piece, 5 + k, (k, qo, qtr))
-        ag_send(piece, 8 + k, (k, h0, half), (p_c, z))
-
-    def a_d(piece, k):
-        ag_wait(piece, 8 + k, (k, ho, half))
+            ag_wait(a, 2 + k, k, gathered[a, 3, True])
+        ag_send(a, 5 + k, k, gathered[a, 2, False], (p_f, z))
+
+    def a_c(a, k):
+        ag_wait(a, 5 + k, k, gathered[a, 2, True])
+        ag_send(a, 8 + k, k, gathered[a, 1, False], (p_c, z))
+
+    def a_d(a, k):
+        ag_wait(a, 8 + k, k, gathered[a, 1, True])
 
     X_TOK, X_N, X_G, X_FG, X_A, X_DI, X_KA = 0, 1, 2, 3, 4, 8, 12
 
@@ -227,19 +293,14 @@
     def core_wait(slot, dst):
         remote(dst, dst, x_s.at[slot], x_r.at[slot], (p_c, z)).wait_recv()
 
-    fq = pl.multiple_of(f * qtr, 16)
-    fo = pl.multiple_of((1 - f) * qtr, 16)
-    sq = pl.multiple_of(f * qtr + s * eig, 16)
-    so = pl.multiple_of(f * qtr + (1 - s) * eig, 16)
-
-    def g_sem(piece, slot):
-        return gr_s.at[piece, slot], gr_r.at[piece, slot]
-
-    def g_send(piece, slot, pair, dev):
-        send(lambda: (*pair(), *g_sem(piece, slot), dev))
-
-    def g_wait(piece, slot, dst):
-        remote(dst, dst, *g_sem(piece, slot), (dp, z1)).wait_recv()
+    def g_sem(p, slot):
+        return gr_s.at[p, slot], gr_r.at[p, slot]
+
+    def g_send(p, slot, pair, dev):
+        send(lambda: (*pair(), *g_sem(p, slot), dev))
+
+    def g_wait(p, slot, dst):
+        remote(dst, dst, *g_sem(p, slot), (dp, z1)).wait_recv()
 
     def add_into(dst, src, n):
         def blk(j, carry):
@@ -249,75 +310,93 @@
 
         lax.fori_loop(0, n // 48, blk, 0)
 
-    def part(piece, stage):
-        chain = CHAIN[piece]
-        return (sq, eig) if chain.index("S") < chain.index(stage) else (fq, qtr)
-
-    def g_fs(piece, k):
-        g_send(piece, k, lambda: (gr.at[piece, k, pl.ds(fo, qtr)], rf.at[piece, k]), (p_f, z))
-
-    def g_fr(piece, k):
-        g_wait(piece, k, rf.at[piece, k])
-        add_into(gr.at[piece, k, pl.ds(fq, qtr)], rf.at[piece, k], qtr)
-
-    def g_ss(piece, k):
-        g_send(piece, 4 + k, lambda: (gr.at[piece, k, pl.ds(so, eig)], rs.at[piece, k]), (p_s, z))
-
-    def g_sr(piece, k):
-        g_wait(piece, 4 + k, rs.at[piece, k])
-        add_into(gr.at[piece, k, pl.ds(sq, eig)], rs.at[piece, k], eig)
-
-    def g_1s(piece, k):
-        off, n = part(piece, "1")
+    def chunk(p, k, depth, other=False):
+        off, n = summed[p, depth, other]
+        return gr.at[SUMMED[p][0], k, pl.ds(off, n)]
+
+    def final(p, depth, other=False):
+        off, n = finals[p, depth, other]
+        return whole.at[SUMMED[p][0], pl.ds(off, n)]
+
+    def f_slot(p, k):
+        piece, base, n, _ = SUMMED[p]
+        return rf.at[piece, k, pl.ds(base // 2, n // 2)]
+
+    def s_slot(p, k):
+        piece, base, n, _ = SUMMED[p]
+        return rs.at[piece, k, pl.ds(base // 4, n // 4)]
+
+    def z_slot(p, slot):
+        return rz.at[pl.ds(*z_rows(p, slot))]
+
+    def g_fs(p, k):
+        g_send(p, k, lambda: (chunk(p, k, 1, True), f_slot(p, k)), (p_f, z))
+
+    def g_fr(p, k):
+        g_wait(p, k, f_slot(p, k))
+        add_into(chunk(p, k, 1), f_slot(p, k), SUMMED[p][2] // 2)
+
+    def g_ss(p, k):
+        g_send(p, 4 + k, lambda: (chunk(p, k, 2, True), s_slot(p, k)), (p_s, z))
+
+    def g_sr(p, k):
+        g_wait(p, 4 + k, s_slot(p, k))
+        add_into(chunk(p, k, 2), s_slot(p, k), SUMMED[p][2] // 4)
+
+    def g_1s(p, k):
         slot = 0 if k == 3 else 1
-        g_send(
-            piece, 8 + slot, lambda: (gr.at[piece, k, pl.ds(off, n)], rz.at[piece, slot, pl.ds(0, n)]), (dp, z1)
-        )
-
-    def g_zr(piece, k, slot, stage):
-        off, n = part(piece, stage)
-        g_wait(piece, 8 + slot, rz.at[piece, slot, pl.ds(0, n)])
-        add_into(gr.at[piece, k, pl.ds(off, n)], rz.at[piece, slot, pl.ds(0, n)], n)
-
-    def g_1r(piece, k):
-        g_zr(piece, k, 0 if k == 2 else 1, "1")
-
-    def g_2s(piece, k):
-        off, n = part(piece, "2")
-        g_send(piece, 10, lambda: (gr.at[piece, 2, pl.ds(off, n)], rz.at[piece, 2, pl.ds(0, n)]), (dp, z2))
-
-    def g_2r(piece, k):
-        g_zr(piece, 0, 2, "2")
-
-    def local_out(piece):
-        return pltpu.make_async_copy(
-            gr.at[piece, 0, pl.ds(sq, eig)], grad_ref.at[piece, pl.ds(e0, eig)], loc_sem.at[5 + piece]
-        )
-
-    def g_s2s(piece, _):
+        g_send(p, 8 + slot, lambda: (chunk(p, k, depth_at(p, "1")), z_slot(p, slot)), (dp, z1))
+
+    def g_1r(p, k):
+        slot = 0 if k == 2 else 1
+        g_wait(p, 8 + slot, z_slot(p, slot))
+        depth = depth_at(p, "1")
+        add_into(chunk(p, k, depth), z_slot(p, slot), SUMMED[p][2] >> depth)
+
+    def g_2s(p, k):
+        g_send(p, 10, lambda: (chunk(p, 2, depth_at(p, "2")), z_slot(p, 2)), (dp, z2))
+
+    def g_2r(p, k):
+        g_wait(p, 10, z_slot(p, 2))
+        depth = depth_at(p, "2")
+        add_into(chunk(p, 0, depth), z_slot(p, 2), SUMMED[p][2] >> depth)
+
+    def write_out(p):
+        piece, base, n, _ = SUMMED[p]
+        return [
+            pltpu.make_async_copy(
+                whole.at[piece, pl.ds(side * half + base, n)],
+                grad_ref.at[piece, pl.ds(side * half + base, n)],
+                out_sem.at[p, side],
+            )
+            for side in range(2)
+        ]
+
+    def g_s2s(p, _):
+        piece, base, n, _ = SUMMED[p]
         for j, partner in enumerate(extra):
-            cp = remote(
-                gr.at[piece, 0, pl.ds(sq, eig)], rx.at[piece, j], e_s.at[piece, j], e_r.at[piece, j], (partner, z)
-            )
+            slot = rx.at[piece, j, pl.ds(base // 4, n // 4)]
+            cp = remote(chunk(p, 0, 2), slot, e_s.at[p, j], e_r.at[p, j], (partner, z))
             cp.start()
             cp.wait()
-            add_into(gr.at[piece, 0, pl.ds(sq, eig)], rx.at[piece, j], eig)
-        g_send(
-            piece, 11, lambda: (gr.at[piece, 0, pl.ds(sq, eig)], grad_ref.at[piece, pl.ds(e0, eig)]), (p_s, z)
-        )
-        local_out(piece).start()
-
-    def g_s2r(piece, _):
-        g_wait(piece, 11, grad_ref.at[piece, pl.ds(eo, eig)])
-        local_out(piece).wait()
-        g_send(piece, 12, lambda: (grad_ref.at[piece, pl.ds(q0, qtr)],) * 2, (p_f, z))
-
-    def g_f2r(piece, _):
-        g_wait(piece, 12, grad_ref.at[piece, pl.ds(qo, qtr)])
-        g_send(piece, 13, lambda: (grad_ref.at[piece, pl.ds(h0, half)],) * 2, (p_c, z))
-
-    def g_c2r(piece, _):
-        g_wait(piece, 13, grad_ref.at[piece, pl.ds(ho, half)])
+            add_into(chunk(p, 0, 2), slot, n // 4)
+        mine, target = chunk(p, 0, 2), final(p, 2)
+        for lo in range(0, n // 4, 48):
+            target[pl.ds(lo, 48), :] = mine[pl.ds(lo, 48), :]
+        g_send(p, 11, lambda: (final(p, 2),) * 2, (p_s, z))
+
+    def g_s2r(p, _):
+        g_wait(p, 11, final(p, 2, True))
+        g_send(p, 12, lambda: (final(p, 1),) * 2, (p_f, z))
+
+    def g_f2r(p, _):
+        g_wait(p, 12, final(p, 1, True))
+        g_send(p, 13, lambda: (final(p, 0),) * 2, (p_c, z))
+
+    def g_c2r(p, _):
+        g_wait(p, 13, final(p, "core", True))
+        for cp in write_out(p):
+            cp.start()
 
     partners = [(p_c, z), (p_f, z), (p_s, z), (dp, z1), (dp, z2)] + [(e, z) for e in extra]
 
@@ -348,10 +427,20 @@
     def once(place):
         do(PLAN.get(place, {}).get(0, ()))
 
+    once("x0")
+    for cp in vec_loads:
+        cp.wait()
+    vin[...] = jnp.zeros_like(vin)
+    vin[pl.ds(0, 1), pl.ds(0, ml)] = small[0][...].astype(F32).reshape(1, ml)
+    vin[pl.ds(0, 1), pl.ds(2 * ml, ml)] = small[1][...].astype(F32).reshape(1, ml)
+    for j, ref in enumerate(small[2:]):
+        vin[pl.ds(j + 1, 1), :] = ref[...].astype(F32).reshape(1, d)
+    bias[z] = vin[...]
     for j, zz in enumerate((z1, z2, z3)):
         send(lambda j=j, zz=zz: (vin, bias.at[z], b_s.at[j], b_r.at[j], (dp, zz)))
-    once("x0")
     core_send(X_TOK, lambda: (tok, xs.at[pl.ds(rows, rows)]))
+    for cp in seg_loads:
+        cp.wait()
 
     for r in range(rows):
         seg_row = seg[pl.ds(z * rows + r, 1), :]
@@ -363,7 +452,6 @@
         mask[r] = jnp.where(dot(key_hot, query_hot, TN) > 0.5, 0.0, NEG_FILL)
     acc[...] = jnp.zeros_like(acc)
     first_row = (lax.broadcasted_iota(jnp.int32, (8, seq), 0) == 0).astype(F32).astype(BF)
-    loads[0].wait()
 
     def attend(i, carry):
         t = shard_of(i)
@@ -402,7 +490,7 @@
 
     lax.fori_loop(0, 4, attend, 0)
 
-    rb = 32
+    rb = seq
 
     def norm_rows(summed):
         mean = jnp.mean(summed, -1, keepdims=True)
@@ -434,7 +522,7 @@
     core_send(X_N, lambda: (nb.at[:, pl.ds(ho, half)], nhalf.at[pl.ds(tl, tl)]))
     nhalf[pl.ds(0, tl), :] = nb[:, pl.ds(h0, half)]
 
-    loads[2].wait()
+    late_loads[0].wait()
 
     def up(i, carry):
         at("up", i)
@@ -455,8 +543,8 @@
         return carry
 
     lax.fori_loop(0, 4, up, 0)
-    loads[3].wait()
-    loads[4].wait()
+    late_loads[1].wait()
+    late_loads[2].wait()
 
     def down(i, carry):
         at("dn", i)
@@ -476,8 +564,8 @@
         sl = pl.ds(pl.multiple_of(j * rb, 16), rb)
         normed = nh1[sl, :] * vrow(3) + vrow(4)
         hat, rs_ = norm_rows(acc[sl, :] + vrow(5) + normed)
-        out_ref[sl, :] = (hat * vrow(6) + vrow(7)).astype(BF)
         c_blk = cots[sl, :].astype(F32)
+        cots[sl, :] = (hat * vrow(6) + vrow(7)).astype(BF)
         back = norm_back(c_blk * vrow(6), hat, rs_)
         sg[sl, :] = back
         g[sl, :] = back.astype(BF)
@@ -488,6 +576,7 @@
         return carry
 
     lax.fori_loop(0, tl // rb, norm2, 0)
+    out_copy = pltpu.make_async_copy(cots, out_hbm, loc_sem.at[19])
     core_send(X_G, lambda: (g.at[pl.ds(0, tl)], g.at[pl.ds(tl, tl)]))
 
     def order(i):
@@ -535,6 +624,7 @@
 
         return carry
 
+    out_copy.start()
     lax.fori_loop(0, 5, ffn_back, 0)
     once("l1b")
 
@@ -544,7 +634,7 @@
         hat = nh1[sl, :]
         total = acc[sl, :] + sg[sl, :]
         back = norm_back(total * vrow(3), hat, r1[sl, 0:1])
-        fgf[sl, :] = back
+        sg[sl, :] = back
         fg[j // per, pl.ds(pl.multiple_of((j % per) * rb, 16), rb), :] = back.astype(BF)
         acc[sl, :] = jnp.zeros((rb, d), F32)
         add_vec(V_G1, jnp.sum(total * hat, 0, keepdims=True))
@@ -618,15 +708,20 @@
 
     def finish(j, carry):
         sl = pl.ds(pl.multiple_of(j * rb, 16), rb)
-        dx_ref[sl, :] = (fgf[sl, :] + acc[sl, :]).astype(BF)
+        dx_ref[sl, :] = (sg[sl, :] + acc[sl, :]).astype(BF)
         return carry
 
     lax.fori_loop(0, tl // rb, finish, 0)
+
+    dx_copy = pltpu.make_async_copy(dx_ref, dx_hbm, loc_sem.at[20])
+    dx_copy.start()
 
     once("end")
     for j in range(5, len(partners)):
         v_send(j, 0)
         v_recv(j, 0)
+    vec_copy = pltpu.make_async_copy(vec_ref, vec_hbm, loc_sem.at[21])
+    vec_copy.start()
 
     for make in pending:
         remote(*make()).wait_send()
@@ -641,48 +736,57 @@
         return carry
 
     lax.fori_loop(0, 4, sent, 0)
+    for p in range(len(SUMMED)):
+        for cp in write_out(p):
+            cp.wait()
+    out_copy.wait()
+    dx_copy.wait()
+    vec_copy.wait()
 
 
 def spread_kernel(
     ml, grads, vec, out_in, dx_in,
     out_ref, dx_ref, gq, gk, gv, go, gi, ge, bq, bv, bo, g1, s1, bi, be, g2, s2,
-    grads_v, vec_v, att_v, big_v, io_v, sem,
+    grads_v, vec_v, wide_v, io_v, in_sem, out_sem,
 ):
     z = lax.axis_index("mp")
+    n = 2 * ml
+    steps = [(piece, lo, [(ref, lo, n)]) for piece, ref in ((1, gi), (2, ge)) for lo in (0, n)]
+    steps += [(0, 0, [(gq, 0, ml), (gk, 0, ml)]), (0, n, [(gv, 0, ml), (go, 0, ml)])]
     moves = [
-        pltpu.make_async_copy(grads.at[1], grads_v.at[1], sem.at[0]),
-        pltpu.make_async_copy(grads.at[2], grads_v.at[2], sem.at[1]),
-        pltpu.make_async_copy(grads.at[0], grads_v.at[0], sem.at[2]),
-        pltpu.make_async_copy(vec, vec_v, sem.at[3]),
-        pltpu.make_async_copy(out_in, io_v.at[0], sem.at[4]),
-        pltpu.make_async_copy(dx_in, io_v.at[1], sem.at[5]),
+        pltpu.make_async_copy(grads.at[piece, pl.ds(lo, n)], grads_v.at[piece, pl.ds(lo, n)], in_sem.at[j])
+        for j, (piece, lo, _) in enumerate(steps)
     ]
-    for cp in moves:
+    ins = [
+        pltpu.make_async_copy(vec, vec_v, in_sem.at[6]),
+        pltpu.make_async_copy(out_in, io_v.at[0], in_sem.at[7]),
+        pltpu.make_async_copy(dx_in, io_v.at[1], in_sem.at[8]),
+    ]
+    for cp in moves + ins:
         cp.start()
     outs = []
-    for j, ref in enumerate((gi, ge)):
-        moves[j].wait()
-        big_v[j] = grads_v[j + 1].astype(F32)
-        cp = pltpu.make_async_copy(big_v.at[j], ref, sem.at[6 + j])
+
+    def put(src, dst):
+        cp = pltpu.make_async_copy(src, dst, out_sem.at[len(outs)])
         cp.start()
         outs.append(cp)
-    moves[2].wait()
-    att_v[...] = grads_v[0].astype(F32)
-    for j, ref in enumerate((gq, gk, gv, go)):
-        cp = pltpu.make_async_copy(att_v.at[pl.ds(j * ml, ml)], ref, sem.at[8 + j])
-        cp.start()
-        outs.append(cp)
-    for j, ref in enumerate((out_ref, dx_ref)):
-        moves[4 + j].wait()
-        cp = pltpu.make_async_copy(io_v.at[j], ref, sem.at[12 + j])
-        cp.start()
-        outs.append(cp)
-    moves[3].wait()
+
+    for j, (piece, lo, refs) in enumerate(steps):
+        moves[j].wait()
+        wide_v[piece, pl.ds(lo, n), :] = grads_v[piece, pl.ds(lo, n), :].astype(F32)
+        at = lo
+        for ref, row, m in refs:
+            put(wide_v.at[piece, pl.ds(at, m)], ref.at[pl.ds(row, m)])
+            at += m
+    ins[0].wait()
     bq[...] = vec_v[pl.ds(z, 1), pl.ds(0, ml)].reshape(ml)
     bv[...] = vec_v[pl.ds(z, 1), pl.ds(2 * ml, ml)].reshape(ml)
     bi[...] = vec_v[pl.ds(4 + z, 1), :].reshape(4 * ml)
     for row, ref in ((V_OB, bo), (V_G1, g1), (V_S1, s1), (V_EB, be), (V_G2, g2), (V_S2, s2)):
         ref[...] = vec_v[pl.ds(row, 1), :].reshape(4 * ml)
+    for j, ref in enumerate((out_ref, dx_ref)):
+        ins[1 + j].wait()
+        put(io_v.at[j], ref)
     for cp in outs:
         cp.wait()
 
@@ -697,6 +801,7 @@
     seq_rows, seq = segment_ids.shape
     rows = tl // seq
     ml = query_weight.shape[1]
+    ff = inner_weight.shape[1]
     half, qtr, eig = d // 2, d // 4, d // 8
     bits = n_dp.bit_length() - 1
     n_extra = max(bits - 3, 1)
@@ -728,27 +833,24 @@
         pltpu.VMEM((tl, d), F32),
         pltpu.VMEM((4, 2 * tl, d), BF),
         pltpu.VMEM((2 * rows, seq, d), BF),
-        pltpu.VMEM((tl, d), F32),
+        pltpu.VMEM((3, d, d), BF),
         pltpu.VMEM((3, 4, half, d), BF),
         pltpu.VMEM((3, 4, qtr, d), BF),
-        pltpu.VMEM((3, 3, qtr, d), BF),
+        pltpu.VMEM((sum(z_rows(len(SUMMED) - 1, 2)), d), BF),
         pltpu.VMEM((3, 4, eig, d), BF),
         pltpu.VMEM((3, n_extra, eig, d), BF) if bits > 3 else pltpu.VMEM((1, 1, 16, 128), BF),
         pltpu.VMEM((n_vec, 16, d), F32),
         pltpu.VMEM((8, d), F32),
-        pltpu.SemaphoreType.DMA((11,)),
-        pltpu.SemaphoreType.DMA((3, 12)),
-        pltpu.SemaphoreType.DMA((3, 12)),
-        pltpu.SemaphoreType.DMA((3, 14)),
-        pltpu.SemaphoreType.DMA((3, 14)),
-        pltpu.SemaphoreType.DMA((16,)),
-        pltpu.SemaphoreType.DMA((16,)),
-        pltpu.SemaphoreType.DMA((3,)),
-        pltpu.SemaphoreType.DMA((3,)),
-        pltpu.SemaphoreType.DMA((n_vec,)),
-        pltpu.SemaphoreType.DMA((n_vec,)),
-        pltpu.SemaphoreType.DMA((3, n_extra)),
-        pltpu.SemaphoreType.DMA((3, n_extra)),
+        pltpu.VMEM((tl, d), BF),
+        pltpu.VMEM((16, d), F32),
+        pltpu.VMEM((seq_rows, seq), jnp.int32),
+        pltpu.VMEM((seq_rows, seq), jnp.int32),
+    ]
+    scratch += [pltpu.VMEM((n,), BF) for n in (ml, ml, ff, d, d, d, d, d, d)]
+    scratch += [
+        pltpu.SemaphoreType.DMA(shape)
+        for shape in [(24,)] + [(len(GATHERED), 12)] * 2 + [(len(SUMMED), 14)] * 2 + [(16,)] * 2 + [(3,)] * 2
+        + [(n_vec,)] * 2 + [(len(SUMMED), n_extra)] * 2 + [(len(SUMMED), 2)]
     ]
     out, dx, grads, vec = pl.pallas_call(
         functools.partial(layer_kernel, cfg),
@@ -758,8 +860,8 @@
             jax.ShapeDtypeStruct((3, d, d), BF),
             jax.ShapeDtypeStruct((16, d), F32),
         ),
-        in_specs=[hbm] * 8 + [vmem] * 11,
-        out_specs=(vmem, vmem, hbm, vmem),
+        in_specs=[hbm] * 19,
+        out_specs=(hbm,) * 4,
         scratch_shapes=scratch,
         compiler_params=pltpu.CompilerParams(
             collective_id=0, has_side_effects=True, vmem_limit_bytes=62 * 1024 * 1024
@@ -770,7 +872,6 @@
         inner_weight, outer_weight, query_bias, value_bias, inner_bias, output_bias, first_gain, first_shift,
         outer_bias, second_gain, second_shift, segment_ids, live_mask,
     )
-    ff = inner_weight.shape[1]
     out, dx, gq, gk, gv, go, gi, ge, bq, bv, bo, g1, s1, bi, be, g2, s2 = pl.pallas_call(
         functools.partial(spread_kernel, ml),
         out_shape=tuple(
@@ -786,10 +887,10 @@
         scratch_shapes=[
             pltpu.VMEM((3, d, d), BF),
             pltpu.VMEM((16, d), F32),
-            pltpu.VMEM((d, d), F32),
-            pltpu.VMEM((2, d, d), F32),
+            pltpu.VMEM((3, d, d), F32),
             pltpu.VMEM((2, tl, d), BF),
-            pltpu.SemaphoreType.DMA((14,)),
+            pltpu.SemaphoreType.DMA((9,)),
+            pltpu.SemaphoreType.DMA((10,)),
         ],
         compiler_params=pltpu.CompilerParams(vmem_limit_bytes=60 * 1024 * 1024),
         name="spread",

time: 157 us -> 142 us (0.904)
  Pallas kernels: 156 us -> 141 us
    pallas_call x1, Pallas kernels: 151 us -> 136 us  [per_device(): pl.pallas_call(functools.partial(layer_kernel, cfg), out_shape=(jax.Shape...]
where the time goes in v4:
time: 142 us
  Pallas kernels  141 us (99%)
    pallas_call x1, Pallas kernels, per_device(): pl.pallas_call(functools.partial(layer_kernel, cfg), out_shape=(jax.Shape...  136 us
    pallas_call x1, Pallas kernels, per_device(): pl.pallas_call(functools.partial(spread_kernel, ml), out_shape=tuple((jax...  5.12 us

profile of v4, /device:TPU:0, one launch (start us, length us, event | category | flops | bytes accessed | tf_op | source)
XLA Modules:
  0.0 141.9 jit_solution(4217197783308653308)
XLA Ops:
  0.7 136.1 %layer.1 = (bf16[320,768]{1,0:T(8,128)(2,1)}, bf16[320,768]{1,0:T(8,128)(2,1)}, bf16[3,768,768]{2,1,0:T(8,128)(2,1)}, f32[16,768]{1,0:T(8,128)}) custom-call(bf16[2,160,768]{2,1,0:T(8,128)(2,1)} %bitcast.7, bf16[320,768]{1,0:T(8,128)(2,1)} %cot.1, bf16[192,768]{1,0:T(8,128)(2,1)} %bitcast.8, bf16[192,768]{1,0:T(8,128)(2,1)} %bitcast.9, ...), custom_call_target="tpu_custom_call" | custom-call | tf_op jit(solution)/shard_map/layer/pallas_call | solution.py:855
  136.8 5.1 %spread.1 = (bf16[320,768]{1,0:T(8,128)(2,1)}, bf16[320,768]{1,0:T(8,128)(2,1)}, f32[192,768]{1,0:T(8,128)}, f32[192,768]{1,0:T(8,128)}, f32[192,768]{1,0:T(8,12...) custom-call(bf16[3,768,768]{2,1,0:T(8,128)(2,1)} %get-tuple-element., ...), custom_call_target="tpu_custom_call" | custom-call | tf_op jit(solution)/shard_map/spread/pallas_call | solution.py:875

commit v5 on v4

--- a/solution.py
+++ b/solution.py
@@ -15,6 +15,7 @@
 BF = jnp.bfloat16
 F32 = jnp.float32
 MESH = pl.DeviceIdType.MESH
+LIMIT = 59 * 1024 * 1024
 
 NN = (((1,), (0,)), ((), ()))
 NT = (((1,), (1,)), ((), ()))
@@ -22,87 +23,90 @@
 
 ATT, INN, OUT = 0, 1, 2
 GATHERED = (
-    (0, 0, 384, False),
-    (0, 384, 384, False),
-    (1, 0, 384, False),
-    (1, 384, 384, True),
-    (2, 0, 384, False),
-    (2, 384, 384, True),
+    (0, 0, 384, 3),
+    (0, 384, 384, 3),
+    (1, 0, 384, 3),
+    (1, 384, 384, 2),
+    (2, 0, 384, 3),
+    (2, 384, 256, 2),
+    (2, 640, 128, 1),
 )
 SUMMED = (
     (0, 0, 192, "FS12"),
-    (0, 192, 192, "FS12"),
+    (0, 192, 128, "FSZd"),
+    (0, 320, 64, "FSZd"),
     (1, 0, 192, "F12S"),
     (1, 192, 192, "F12S"),
-    (2, 0, 192, "F12S"),
+    (2, 0, 192, "1F2S"),
     (2, 192, 192, "F12S"),
 )
 PLAN = {
     "x0": {
-        0: (("az1", 0, 0), ("az2", 0, 0), ("az1", 1, 0), ("az2", 1, 0), ("s", 0, 1), ("zf", 0, 0), ("s", 0, 2), ("s", 1, 1), ("az2", 2, 0), ("az1", 2, 0), ("f", 0, 1), ("zf", 1, 0), ("f", 1, 1),),
+        0: (("az1", 0, 0), ("az1", 1, 0), ("s", 0, 1), ("az2", 1, 0), ("az1", 4, 0), ("az2", 0, 0), ("az1", 2, 0), ("s", 1, 1), ("f", 0, 1), ("s", 4, 1), ("f", 1, 1), ("az2", 4, 0), ("zf", 0, 0), ("az2", 2, 0), ("zf", 1, 0), ("s", 0, 2), ("s", 1, 2),),
     },
     "att": {
-        0: (("s", 1, 2), ("az1", 3, 0), ("c", 0, 1), ("f", 0, 2), ("az2", 3, 0),),
-        1: (("s", 2, 1), ("f", 1, 2), ("c", 1, 1), ("zf", 2, 0), ("s", 2, 2), ("s", 0, 3), ("az2", 4, 0), ("az1", 4, 0), ("c", 0, 2),),
-        2: (("f", 2, 1), ("d", 1, 1), ("d", 0, 1),),
-        3: (("f", 3, 1), ("f", 0, 3), ("d", 0, 2), ("s", 1, 3), ("az2", 5, 0), ("az1", 5, 0), ("f", 1, 3), ("s", 4, 1), ("c", 1, 2), ("zf", 4, 0), ("s", 2, 3), ("zf", 3, 0), ("f", 2, 2),),
-        4: (("d", 1, 2), ("s", 4, 2), ("c", 0, 3), ("f", 3, 2),),
-        5: (("f", 4, 1), ("f", 5, 1), ("d", 0, 3), ("c", 1, 3), ("f", 2, 3), ("zf", 5, 0), ("c", 2, 2), ("f", 5, 2),),
-        6: (("c", 2, 1), ("c", 4, 1), ("c", 3, 1), ("c", 3, 2), ("d", 1, 3), ("s", 4, 3), ("f", 3, 3), ("c", 5, 1),),
-        7: (("f", 4, 2), ("d", 3, 1), ("d", 2, 1), ("d", 3, 2), ("c", 2, 3),),
+        0: (("f", 4, 1), ("s", 2, 1),),
+        1: (("f", 1, 2), ("az1", 5, 0), ("s", 0, 3), ("s", 1, 3), ("f", 0, 2), ("az2", 3, 0), ("c", 1, 1), ("zf", 4, 0), ("s", 4, 2), ("d", 1, 1), ("c", 4, 1), ("c", 0, 1), ("zf", 2, 0), ("f", 2, 1),),
+        2: (("s", 2, 2), ("f", 1, 3), ("d", 0, 1), ("f", 0, 3), ("az2", 5, 0),),
+        3: (("c", 1, 2), ("c", 2, 1), ("c", 0, 2), ("az1", 3, 0), ("zf", 3, 0), ("f", 3, 2), ("s", 2, 3), ("az2", 6, 0), ("d", 4, 1),),
+        4: (("f", 2, 2), ("s", 4, 3), ("d", 1, 2), ("d", 0, 2), ("f", 4, 2), ("c", 1, 3),),
+        5: (("zf", 5, 0), ("c", 0, 3), ("d", 1, 3), ("f", 2, 3),),
+        6: (("f", 3, 1), ("d", 0, 3),),
+        7: (("f", 3, 3), ("c", 2, 2), ("c", 3, 2), ("f", 5, 1), ("az1", 6, 0), ("f", 5, 2),),
     },
     "n1": {
-        0: (("f", 4, 3), ("c", 5, 2), ("c", 3, 3), ("d", 2, 3), ("d", 2, 2), ("f", 5, 3),),
+        0: (("d", 2, 1), ("f", 4, 3), ("c", 3, 1), ("c", 2, 3), ("c", 4, 2),),
     },
     "up": {
-        2: (("c", 4, 2),),
-        3: (("d", 3, 3), ("c", 4, 3),),
+        0: (("zf", 6, 0), ("d", 3, 2),),
+        1: (("c", 6, 2), ("d", 3, 1), ("d", 2, 2), ("f", 5, 3), ("c", 3, 3),),
+        2: (("c", 5, 1),),
+        3: (("c", 6, 1), ("d", 3, 3), ("c", 5, 2), ("d", 2, 3), ("d", 4, 2),),
     },
     "dn": {
-        1: (("d", 5, 1), ("d", 4, 2), ("d", 4, 1), ("c", 5, 3),),
+        0: (("c", 4, 3),),
+        1: (("d", 5, 1), ("d", 6, 1), ("d", 6, 2), ("c", 6, 3), ("c", 5, 3),),
         2: (("d", 5, 2),),
-        3: (("d", 4, 3), ("d", 5, 3),),
+        3: (("d", 6, 3), ("d", 5, 3), ("d", 4, 3),),
     },
     "l2": {
     },
     "da": {
-        2: (("gFr", 5, 3), ("gFs", 2, 3), ("g1s", 5, 3), ("gFs", 4, 1),),
+        2: (("gFs", 4, 3), ("gFr", 6, 3), ("gFs", 3, 3),),
+        3: (("gFs", 3, 1),),
     },
     "gwo": {
-        3: (("g1s", 5, 1),),
+        2: (("g1s", 6, 3),),
+        3: (("gFs", 4, 1),),
     },
     "dn2": {
-        0: (("gFs", 5, 3), ("gFs", 4, 3),),
-        1: (("gFs", 5, 1),),
-        3: (("gFs", 2, 1),),
+        0: (("gFs", 6, 3), ("g1s", 5, 3),),
+        1: (("gFs", 6, 1),),
+        2: (("gFs", 6, 2),),
     },
     "gwi": {
-        1: (("gFr", 4, 3), ("gFs", 4, 2), ("g1s", 4, 3), ("gFs", 3, 3), ("gFr", 5, 1), ("gFs", 5, 2),),
-        3: (("gFs", 3, 2), ("gFs", 4, 0),),
+        1: (("g1s", 5, 1),),
+        2: (("gFr", 6, 1),),
+        3: (("g1s", 6, 1), ("gFr", 4, 3), ("gFs", 6, 0), ("g1r", 5, 2), ("gFr", 6, 2),),
     },
     "l1b": {
-        0: (("gFr", 4, 1), ("gFr", 4, 2),),
+        0: (("gFs", 4, 2), ("g1r", 6, 2), ("gFs", 3, 0),),
     },
     "ab": {
-        0: (("g1r", 4, 2), ("gFs", 5, 0), ("g1s", 4, 1),),
-        1: (("gFs", 2, 2),),
-        2: (("gFs", 2, 0), ("gFs", 3, 0), ("g2s", 4, 2),),
-        3: (("gFr", 2, 3), ("gFr", 2, 1), ("gFr", 5, 2), ("gFr", 3, 3), ("g1s", 2, 3),),
-        4: (("gFr", 4, 0),),
-        5: (("g1s", 3, 3), ("gFs", 0, 3), ("g1r", 5, 2), ("gFr", 5, 0), ("g1r", 4, 0), ("gFs", 1, 3),),
-        6: (("g2s", 5, 2),),
-        7: (("gFs", 0, 1), ("g2r", 4, 0), ("gSs", 4, 0),),
+        1: (("gFr", 3, 3), ("gFs", 5, 2),),
+        2: (("gFs", 3, 2), ("g2s", 6, 2), ("gFs", 4, 0),),
+        4: (("gFs", 0, 3), ("g1s", 3, 3), ("gFs", 1, 3), ("g1r", 5, 0), ("gFs", 2, 3), ("g1s", 4, 3), ("gFs", 5, 0),),
+        6: (("gFs", 0, 1), ("gFs", 1, 1), ("gFr", 5, 2), ("g2s", 5, 2), ("gFr", 6, 0),),
+        7: (("gFr", 0, 3), ("gFr", 4, 1), ("g1r", 6, 0), ("gFs", 2, 1), ("gFr", 2, 3), ("gFr", 1, 3), ("gSs", 1, 3), ("g1s", 4, 1), ("gSs", 0, 3), ("g2r", 6, 0), ("gSs", 6, 0),),
     },
     "gwa": {
-        0: (("gFs", 3, 1),),
-        2: (("gFr", 3, 2), ("gFr", 3, 1), ("gFr", 0, 3), ("gFs", 1, 1), ("gFr", 2, 2), ("g1s", 2, 1), ("gFr", 3, 0), ("gFr", 1, 3),),
-        3: (("gFs", 1, 2), ("g1r", 2, 2), ("gFr", 0, 1), ("gSr", 4, 0), ("gSs", 1, 3), ("g2s", 2, 2), ("gSs", 0, 1),),
+        2: (("gFr", 0, 1), ("gFr", 3, 1), ("gFr", 4, 2), ("gSs", 0, 1),),
+        3: (("gSs", 2, 3), ("gFs", 1, 2), ("g1r", 4, 2), ("g2s", 4, 2), ("gFr", 1, 1), ("gFs", 0, 2), ("gFs", 2, 2),),
     },
     "fin": {
-        0: (("g1s", 3, 1), ("gFr", 2, 0), ("gFs", 1, 0),),
     },
     "end": {
-        0: (("g1r", 3, 2), ("gFs", 0, 2), ("gFs", 0, 0), ("g2s", 3, 2), ("gSs", 0, 3), ("gSr", 0, 1), ("g1r", 2, 0), ("gFr", 1, 2), ("gSs", 1, 2), ("gSr", 1, 3), ("gFr", 0, 2), ("g1r", 5, 0), ("vs", 0, 0), ("gSs", 0, 2), ("vr", 0, 0), ("gS2s", 4, 0), ("g2r", 5, 0), ("gSr", 0, 3), ("vs", 1, 0), ("g1s", 0, 3), ("g2r", 2, 0), ("g1r", 3, 0), ("gFr", 1, 1), ("gFr", 1, 0), ("gFr", 0, 0), ("gSs", 1, 1), ("g1s", 1, 3), ("gSs", 5, 0), ("gSr", 0, 2), ("gSs", 2, 0), ("vr", 1, 0), ("gS2r", 4, 0), ("gSr", 5, 0), ("gSs", 1, 0), ("gSr", 1, 1), ("gS2s", 5, 0), ("g1r", 0, 2), ("gSs", 0, 0), ("gSr", 1, 2), ("g2s", 0, 2), ("g1s", 1, 1), ("g2r", 3, 0), ("g1r", 1, 2), ("gSs", 3, 0), ("gSr", 2, 0), ("gS2r", 5, 0), ("g1s", 0, 1), ("gSr", 1, 0), ("gS2s", 2, 0), ("vs", 2, 0), ("g2s", 1, 2), ("gSr", 0, 0), ("gSr", 3, 0), ("gS2s", 3, 0), ("g1r", 1, 0), ("gS2r", 2, 0), ("g1r", 0, 0), ("g2r", 0, 0), ("gF2r", 4, 0), ("gS2s", 0, 0), ("vr", 2, 0), ("g2r", 1, 0), ("gS2s", 1, 0), ("vs", 3, 0), ("gS2r", 3, 0), ("gS2r", 0, 0), ("gS2r", 1, 0), ("vr", 3, 0), ("gC2r", 4, 0), ("gF2r", 5, 0), ("gF2r", 2, 0), ("vs", 4, 0), ("gC2r", 2, 0), ("gF2r", 0, 0), ("vr", 4, 0), ("gF2r", 3, 0), ("gC2r", 0, 0), ("gF2r", 1, 0), ("gC2r", 5, 0), ("gC2r", 1, 0), ("gC2r", 3, 0),),
+        0: (("gFs", 2, 0), ("g1s", 3, 1), ("gFr", 4, 0), ("gFr", 3, 2), ("gSs", 1, 1), ("gFr", 1, 2), ("gFr", 5, 0), ("g2r", 5, 0), ("gSr", 6, 0), ("g1r", 3, 2), ("gSs", 5, 0), ("gSs", 1, 2), ("gFs", 1, 0), ("gFr", 2, 2), ("g2s", 3, 2), ("gFr", 3, 0), ("gSr", 1, 3), ("gFr", 0, 2), ("gSr", 0, 1), ("gFr", 2, 1), ("gFs", 0, 0), ("gSr", 0, 3), ("g1s", 0, 3), ("vs", 0, 0), ("vr", 0, 0), ("gS2s", 6, 0), ("vs", 1, 0), ("gSs", 2, 1), ("gSr", 5, 0), ("gSr", 1, 2), ("gS2s", 5, 0), ("gSr", 1, 1), ("gFr", 1, 0), ("gSs", 2, 2), ("g1r", 4, 0), ("gSr", 2, 3), ("gSs", 0, 2), ("gZs", 1, 2), ("g1s", 0, 1), ("g2r", 4, 0), ("gFr", 0, 0), ("gSs", 4, 0), ("g1r", 3, 0), ("gSs", 1, 0), ("gSs", 0, 0), ("gFr", 2, 0), ("gS2r", 5, 0), ("g2r", 3, 0), ("gSr", 0, 2), ("gSs", 3, 0), ("g1r", 0, 2), ("vr", 1, 0), ("vs", 2, 0), ("g2s", 0, 2), ("gSr", 2, 1), ("gZs", 1, 1), ("gSr", 4, 0), ("gS2s", 4, 0), ("gSr", 0, 0), ("gZs", 2, 1), ("gS2r", 6, 0), ("gSr", 3, 0), ("gS2s", 3, 0), ("gZs", 1, 3), ("g1r", 0, 0), ("gSs", 2, 0), ("gS2r", 4, 0), ("gSr", 1, 0), ("g2r", 0, 0), ("gZr", 1, 1), ("gZr", 1, 2), ("gS2s", 0, 0), ("gF2r", 5, 0), ("gSr", 2, 2), ("gZs", 2, 3), ("gS2r", 3, 0), ("gSr", 2, 0), ("gZr", 1, 3), ("vr", 2, 0), ("gC2r", 5, 0), ("gZs", 2, 2), ("vs", 3, 0), ("gZr", 2, 1), ("gS2s", 1, 0), ("gS2r", 0, 0), ("gF2r", 3, 0), ("vr", 3, 0), ("gF2r", 4, 0), ("gZr", 2, 2), ("gZr", 2, 3), ("gS2s", 2, 0), ("vs", 4, 0), ("gF2r", 6, 0), ("gd2Fr", 1, 0), ("gC2r", 6, 0), ("gd2Sr", 1, 0), ("gF2r", 1, 0), ("gF2r", 0, 0), ("gd2Fr", 2, 0), ("gC2r", 4, 0), ("gd2Sr", 2, 0), ("gF2r", 2, 0), ("gC2r", 0, 0), ("vr", 4, 0), ("gC2r", 3, 0), ("gC2r", 1, 0), ("gC2r", 2, 0),),
     },
 }
 V_OB, V_G1, V_S1, V_EB, V_G2, V_S2 = 8, 9, 10, 11, 12, 13
@@ -118,18 +122,21 @@
 
 
 def z_rows(p, slot):
-    sizes = {(q, t): SUMMED[q][2] >> depth_at(q, "2" if t == 2 else "1") for q in range(len(SUMMED)) for t in range(3)}
+    sizes = {}
+    for q, (_, _, n, chain) in enumerate(SUMMED):
+        for t in range(3):
+            sizes[q, t] = n >> depth_at(q, "Z" if "Z" in chain else "112"[t])
     return sum(n for key, n in sizes.items() if key < (p, slot)), sizes[p, slot]
 
 
 def layer_kernel(
     cfg,
     tok, cot, wq, wk, wv, wo, wi, wout, bq, bv, bi, bo, g1, s1, be, g2, s2, seg_in, live_in,
-    out_hbm, dx_hbm, grad_ref, vec_hbm,
+    out_ref, dx_ref, whole, vec_ref,
     wbuf, bias, xs, cots, qkv, ka, ks, prob, mask, acc, tmp, nh1, r1,
-    nb, nhalf, af, asib, al, gp, g, sg, di, fg, whole,
+    nb, nhalf, af, asib, al, gp, g, sg, di, fg,
     gr, rf, rz, rs, rx, vrecv, vin,
-    dx_ref, vec_ref, seg, live, *rest,
+    seg, live, *rest,
 ):
     n_dp, d, seq, rows = cfg["dp"], cfg["d"], cfg["seq"], cfg["rows"]
     tl = seq * rows
@@ -143,6 +150,7 @@
     df = 2 + 2 * c
     ds_ = 6 - df
     f, s = (dp // df) % 2, (dp // ds_) % 2
+    p_x = dp + df * (1 - 2 * f) + ds_ * (1 - 2 * s)
     p_f, p_s, p_c = dp + df * (1 - 2 * f), dp + ds_ * (1 - 2 * s), dp + 1 - 2 * c
     z0, zh = z % 2, z // 2
     z1, z2, z3 = z + 1 - 2 * z0, z + 2 - 4 * zh, 3 - z
@@ -164,7 +172,7 @@
         return (pl.multiple_of(off, 16) if depth else off), n
 
     gathered = {}
-    for a, (piece, base, n, wide) in enumerate(GATHERED):
+    for a, (piece, base, n, cuts) in enumerate(GATHERED):
         for depth in (1, 2, 3):
             for other in (False, True):
                 gathered[a, depth, other] = sub(base, n, depth, other)
@@ -199,10 +207,10 @@
         pending.append(make)
 
     small = rest[:9]
-    loc_sem, ag_s, ag_r, gr_s, gr_r, x_s, x_r, b_s, b_r, v_s, v_r, e_s, e_r, out_sem = rest[9:]
+    loc_sem, ag_s, ag_r, gr_s, gr_r, x_s, x_r, b_s, b_r, v_s, v_r, e_s, e_r = rest[9:]
     barrier = pltpu.get_barrier_semaphore()
     extra = [dp + (1 << b) * (1 - 2 * ((dp // (1 << b)) % 2)) for b in range(3, bits)]
-    greet = [(p_c, z), (p_f, z), (p_s, z), (dp, z1), (dp, z2), (dp, z3)] + [(e, z) for e in extra]
+    greet = [(p_c, z), (p_f, z), (p_s, z), (p_x, z), (dp, z1), (dp, z2), (dp, z3)] + [(e, z) for e in extra]
     for dev in greet:
         pl.semaphore_signal(barrier, inc=1, device_id=dev, device_id_type=MESH)
     att_loads = [
@@ -251,7 +259,7 @@
         remote(region, region, ag_s.at[a, slot], ag_r.at[a, slot], (dp, z1)).wait_recv()
 
     def first(a):
-        return gathered[a, 2 if GATHERED[a][3] else 3, False]
+        return gathered[a, GATHERED[a][3], False]
 
     def a_z1(a, _):
         ag_send(a, 1, 0, first(a), (dp, z1), True)
@@ -272,20 +280,23 @@
         ag_send(a, 2 + k, k, gathered[a, 3, False], (p_s, z))
 
     def a_f(a, k):
-        if GATHERED[a][3]:
+        if GATHERED[a][3] < 3:
             a_arrive(a, k)
         else:
             ag_wait(a, 2 + k, k, gathered[a, 3, True])
         ag_send(a, 5 + k, k, gathered[a, 2, False], (p_f, z))
 
     def a_c(a, k):
-        ag_wait(a, 5 + k, k, gathered[a, 2, True])
+        if GATHERED[a][3] < 2:
+            a_arrive(a, k)
+        else:
+            ag_wait(a, 5 + k, k, gathered[a, 2, True])
         ag_send(a, 8 + k, k, gathered[a, 1, False], (p_c, z))
 
     def a_d(a, k):
         ag_wait(a, 8 + k, k, gathered[a, 1, True])
 
-    X_TOK, X_N, X_G, X_FG, X_A, X_DI, X_KA = 0, 1, 2, 3, 4, 8, 12
+    X_TOK, X_N, X_FG, X_A, X_DI, X_KA, X_G = 0, 1, 2, 4, 8, 12, 16
 
     def core_send(slot, pair):
         send(lambda: (*pair(), x_s.at[slot], x_r.at[slot], (p_c, z)))
@@ -303,12 +314,14 @@
         remote(dst, dst, *g_sem(p, slot), (dp, z1)).wait_recv()
 
     def add_into(dst, src, n):
+        m = 48 if n % 48 == 0 else (32 if n % 32 == 0 else 16)
+
         def blk(j, carry):
-            sl = pl.ds(pl.multiple_of(j * 48, 16), 48)
+            sl = pl.ds(pl.multiple_of(j * m, 16), m)
             dst[sl, :] = (dst[sl, :].astype(F32) + src[sl, :].astype(F32)).astype(BF)
             return carry
 
-        lax.fori_loop(0, n // 48, blk, 0)
+        lax.fori_loop(0, n // m, blk, 0)
 
     def chunk(p, k, depth, other=False):
         off, n = summed[p, depth, other]
@@ -317,6 +330,11 @@
     def final(p, depth, other=False):
         off, n = finals[p, depth, other]
         return whole.at[SUMMED[p][0], pl.ds(off, n)]
+
+    def final_across(p, side):
+        _, base, n, _ = SUMMED[p]
+        off = pl.multiple_of(c * half + base + (1 - f) * (n // 2) + side * (n // 4), 16)
+        return whole.at[SUMMED[p][0], pl.ds(off, n // 4)]
 
     def f_slot(p, k):
         piece, base, n, _ = SUMMED[p]
@@ -361,16 +379,14 @@
         depth = depth_at(p, "2")
         add_into(chunk(p, 0, depth), z_slot(p, 2), SUMMED[p][2] >> depth)
 
-    def write_out(p):
-        piece, base, n, _ = SUMMED[p]
-        return [
-            pltpu.make_async_copy(
-                whole.at[piece, pl.ds(side * half + base, n)],
-                grad_ref.at[piece, pl.ds(side * half + base, n)],
-                out_sem.at[p, side],
-            )
-            for side in range(2)
-        ]
+    def g_zs(p, k):
+        depth = depth_at(p, "Z")
+        g_send(p, 7 + k, lambda: (chunk(p, k, depth), z_slot(p, k - 1)), (dp, shard[k]))
+
+    def g_zr(p, k):
+        depth = depth_at(p, "Z")
+        g_wait(p, 7 + k, z_slot(p, k - 1))
+        add_into(chunk(p, 0, depth), z_slot(p, k - 1), SUMMED[p][2] >> depth)
 
     def g_s2s(p, _):
         piece, base, n, _ = SUMMED[p]
@@ -381,22 +397,32 @@
             cp.wait()
             add_into(chunk(p, 0, 2), slot, n // 4)
         mine, target = chunk(p, 0, 2), final(p, 2)
-        for lo in range(0, n // 4, 48):
-            target[pl.ds(lo, 48), :] = mine[pl.ds(lo, 48), :]
+        for lo in range(0, n // 4, 16):
+            target[pl.ds(lo, 16), :] = mine[pl.ds(lo, 16), :]
         g_send(p, 11, lambda: (final(p, 2),) * 2, (p_s, z))
+        if SUMMED[p][3].endswith("d"):
+            g_send(p, 12, lambda: (final(p, 2),) * 2, (p_f, z))
+            g_send(p, 14, lambda: (final(p, 2),) * 2, (p_x, z))
 
     def g_s2r(p, _):
         g_wait(p, 11, final(p, 2, True))
         g_send(p, 12, lambda: (final(p, 1),) * 2, (p_f, z))
 
+    def g_d2sr(p, _):
+        g_wait(p, 11, final(p, 2, True))
+
+    def g_d2fr(p, _):
+        g_wait(p, 12, final_across(p, s))
+
     def g_f2r(p, _):
-        g_wait(p, 12, final(p, 1, True))
+        if SUMMED[p][3].endswith("d"):
+            g_wait(p, 14, final_across(p, 1 - s))
+        else:
+            g_wait(p, 12, final(p, 1, True))
         g_send(p, 13, lambda: (final(p, 0),) * 2, (p_c, z))
 
     def g_c2r(p, _):
         g_wait(p, 13, final(p, "core", True))
-        for cp in write_out(p):
-            cp.start()
 
     partners = [(p_c, z), (p_f, z), (p_s, z), (dp, z1), (dp, z2)] + [(e, z) for e in extra]
 
@@ -413,7 +439,7 @@
     events = {
         "az1": a_z1, "az2": a_z2, "zf": a_zf, "s": a_s, "f": a_f, "c": a_c, "d": a_d,
         "gFs": g_fs, "gFr": g_fr, "gSs": g_ss, "gSr": g_sr, "g1s": g_1s, "g1r": g_1r, "g2s": g_2s, "g2r": g_2r,
-        "gS2s": g_s2s, "gS2r": g_s2r, "gF2r": g_f2r, "gC2r": g_c2r, "vs": v_send, "vr": v_recv,
+        "gZs": g_zs, "gZr": g_zr, "gd2Fr": g_d2fr, "gd2Sr": g_d2sr, "gS2s": g_s2s, "gS2r": g_s2r, "gF2r": g_f2r, "gC2r": g_c2r, "vs": v_send, "vr": v_recv,
     }
 
     def do(listed):
@@ -565,7 +591,7 @@
         normed = nh1[sl, :] * vrow(3) + vrow(4)
         hat, rs_ = norm_rows(acc[sl, :] + vrow(5) + normed)
         c_blk = cots[sl, :].astype(F32)
-        cots[sl, :] = (hat * vrow(6) + vrow(7)).astype(BF)
+        out_ref[sl, :] = (hat * vrow(6) + vrow(7)).astype(BF)
         back = norm_back(c_blk * vrow(6), hat, rs_)
         sg[sl, :] = back
         g[sl, :] = back.astype(BF)
@@ -575,10 +601,14 @@
         add_vec(V_EB, jnp.sum(back, 0, keepdims=True))
         return carry
 
-    lax.fori_loop(0, tl // rb, norm2, 0)
-    out_copy = pltpu.make_async_copy(cots, out_hbm, loc_sem.at[19])
-    core_send(X_G, lambda: (g.at[pl.ds(0, tl)], g.at[pl.ds(tl, tl)]))
-
+    def g_copy(j):
+        src = g.at[pl.ds(pl.multiple_of(j * rb, 16), rb)]
+        dst = g.at[pl.ds(pl.multiple_of(tl + j * rb, 16), rb)]
+        return remote(src, dst, x_s.at[X_G + j], x_r.at[X_G + j], (p_c, z))
+
+    for j in range(tl // rb):
+        norm2(j, 0)
+        g_copy(j).start()
     def order(i):
         return 3 - 2 * (i % 2) - i // 2
 
@@ -604,7 +634,8 @@
 
             @pl.when(i == 0)
             def _():
-                core_wait(X_G, g.at[pl.ds(tl, tl)])
+                for j in range(tl // rb):
+                    g_copy(j).wait_recv()
                 core_wait(X_N, nhalf.at[pl.ds(tl, tl)])
 
             core_wait(X_A + k, asib.at[t])
@@ -624,7 +655,6 @@
 
         return carry
 
-    out_copy.start()
     lax.fori_loop(0, 5, ffn_back, 0)
     once("l1b")
 
@@ -713,15 +743,11 @@
 
     lax.fori_loop(0, tl // rb, finish, 0)
 
-    dx_copy = pltpu.make_async_copy(dx_ref, dx_hbm, loc_sem.at[20])
-    dx_copy.start()
 
     once("end")
     for j in range(5, len(partners)):
         v_send(j, 0)
         v_recv(j, 0)
-    vec_copy = pltpu.make_async_copy(vec_ref, vec_hbm, loc_sem.at[21])
-    vec_copy.start()
 
     for make in pending:
         remote(*make()).wait_send()
@@ -736,57 +762,39 @@
         return carry
 
     lax.fori_loop(0, 4, sent, 0)
-    for p in range(len(SUMMED)):
-        for cp in write_out(p):
-            cp.wait()
-    out_copy.wait()
-    dx_copy.wait()
-    vec_copy.wait()
+    for j in range(tl // rb):
+        g_copy(j).wait_send()
 
 
 def spread_kernel(
     ml, grads, vec, out_in, dx_in,
     out_ref, dx_ref, gq, gk, gv, go, gi, ge, bq, bv, bo, g1, s1, bi, be, g2, s2,
-    grads_v, vec_v, wide_v, io_v, in_sem, out_sem,
+    wide_v, sem,
 ):
     z = lax.axis_index("mp")
     n = 2 * ml
+    outs = []
+
+    def put(src, dst):
+        cp = pltpu.make_async_copy(src, dst, sem.at[len(outs)])
+        cp.start()
+        outs.append(cp)
+
+    put(out_in, out_ref)
+    put(dx_in, dx_ref)
     steps = [(piece, lo, [(ref, lo, n)]) for piece, ref in ((1, gi), (2, ge)) for lo in (0, n)]
     steps += [(0, 0, [(gq, 0, ml), (gk, 0, ml)]), (0, n, [(gv, 0, ml), (go, 0, ml)])]
-    moves = [
-        pltpu.make_async_copy(grads.at[piece, pl.ds(lo, n)], grads_v.at[piece, pl.ds(lo, n)], in_sem.at[j])
-        for j, (piece, lo, _) in enumerate(steps)
-    ]
-    ins = [
-        pltpu.make_async_copy(vec, vec_v, in_sem.at[6]),
-        pltpu.make_async_copy(out_in, io_v.at[0], in_sem.at[7]),
-        pltpu.make_async_copy(dx_in, io_v.at[1], in_sem.at[8]),
-    ]
-    for cp in moves + ins:
-        cp.start()
-    outs = []
-
-    def put(src, dst):
-        cp = pltpu.make_async_copy(src, dst, out_sem.at[len(outs)])
-        cp.start()
-        outs.append(cp)
-
-    for j, (piece, lo, refs) in enumerate(steps):
-        moves[j].wait()
-        wide_v[piece, pl.ds(lo, n), :] = grads_v[piece, pl.ds(lo, n), :].astype(F32)
+    for piece, lo, refs in steps:
+        wide_v[piece, pl.ds(lo, n), :] = grads[piece, pl.ds(lo, n), :].astype(F32)
         at = lo
         for ref, row, m in refs:
             put(wide_v.at[piece, pl.ds(at, m)], ref.at[pl.ds(row, m)])
             at += m
-    ins[0].wait()
-    bq[...] = vec_v[pl.ds(z, 1), pl.ds(0, ml)].reshape(ml)
-    bv[...] = vec_v[pl.ds(z, 1), pl.ds(2 * ml, ml)].reshape(ml)
-    bi[...] = vec_v[pl.ds(4 + z, 1), :].reshape(4 * ml)
+    bq[...] = vec[pl.ds(z, 1), pl.ds(0, ml)].reshape(ml)
+    bv[...] = vec[pl.ds(z, 1), pl.ds(2 * ml, ml)].reshape(ml)
+    bi[...] = vec[pl.ds(4 + z, 1), :].reshape(4 * ml)
     for row, ref in ((V_OB, bo), (V_G1, g1), (V_S1, s1), (V_EB, be), (V_G2, g2), (V_S2, s2)):
-        ref[...] = vec_v[pl.ds(row, 1), :].reshape(4 * ml)
-    for j, ref in enumerate((out_ref, dx_ref)):
-        ins[1 + j].wait()
-        put(io_v.at[j], ref)
+        ref[...] = vec[pl.ds(row, 1), :].reshape(4 * ml)
     for cp in outs:
         cp.wait()
 
@@ -833,7 +841,6 @@
         pltpu.VMEM((tl, d), F32),
         pltpu.VMEM((4, 2 * tl, d), BF),
         pltpu.VMEM((2 * rows, seq, d), BF),
-        pltpu.VMEM((3, d, d), BF),
         pltpu.VMEM((3, 4, half, d), BF),
         pltpu.VMEM((3, 4, qtr, d), BF),
         pltpu.VMEM((sum(z_rows(len(SUMMED) - 1, 2)), d), BF),
@@ -841,30 +848,28 @@
         pltpu.VMEM((3, n_extra, eig, d), BF) if bits > 3 else pltpu.VMEM((1, 1, 16, 128), BF),
         pltpu.VMEM((n_vec, 16, d), F32),
         pltpu.VMEM((8, d), F32),
-        pltpu.VMEM((tl, d), BF),
-        pltpu.VMEM((16, d), F32),
         pltpu.VMEM((seq_rows, seq), jnp.int32),
         pltpu.VMEM((seq_rows, seq), jnp.int32),
     ]
     scratch += [pltpu.VMEM((n,), BF) for n in (ml, ml, ff, d, d, d, d, d, d)]
     scratch += [
         pltpu.SemaphoreType.DMA(shape)
-        for shape in [(24,)] + [(len(GATHERED), 12)] * 2 + [(len(SUMMED), 14)] * 2 + [(16,)] * 2 + [(3,)] * 2
-        + [(n_vec,)] * 2 + [(len(SUMMED), n_extra)] * 2 + [(len(SUMMED), 2)]
+        for shape in [(24,)] + [(len(GATHERED), 12)] * 2 + [(len(SUMMED), 15)] * 2 + [(16 + rows,)] * 2 + [(3,)] * 2
+        + [(n_vec,)] * 2 + [(len(SUMMED), n_extra)] * 2
     ]
     out, dx, grads, vec = pl.pallas_call(
         functools.partial(layer_kernel, cfg),
         out_shape=(
-            jax.ShapeDtypeStruct((tl, d), BF),
-            jax.ShapeDtypeStruct((tl, d), BF),
-            jax.ShapeDtypeStruct((3, d, d), BF),
-            jax.ShapeDtypeStruct((16, d), F32),
+            pltpu.VMEM((tl, d), BF),
+            pltpu.VMEM((tl, d), BF),
+            pltpu.VMEM((3, d, d), BF),
+            pltpu.VMEM((16, d), F32),
         ),
         in_specs=[hbm] * 19,
-        out_specs=(hbm,) * 4,
+        out_specs=(vmem,) * 4,
         scratch_shapes=scratch,
         compiler_params=pltpu.CompilerParams(
-            collective_id=0, has_side_effects=True, vmem_limit_bytes=62 * 1024 * 1024
+            collective_id=0, has_side_effects=True, vmem_limit_bytes=LIMIT
         ),
         name="layer",
     )(
@@ -882,19 +887,12 @@
             + [((ml,), F32)] * 2
             + [((d,), F32)] * 7
         ),
-        in_specs=[hbm] * 4,
+        in_specs=[vmem] * 4,
         out_specs=(hbm,) * 8 + (vmem,) * 9,
-        scratch_shapes=[
-            pltpu.VMEM((3, d, d), BF),
-            pltpu.VMEM((16, d), F32),
-            pltpu.VMEM((3, d, d), F32),
-            pltpu.VMEM((2, tl, d), BF),
-            pltpu.SemaphoreType.DMA((9,)),
-            pltpu.SemaphoreType.DMA((10,)),
-        ],
-        compiler_params=pltpu.CompilerParams(vmem_limit_bytes=60 * 1024 * 1024),
+        scratch_shapes=[pltpu.VMEM((3, d, d), F32), pltpu.SemaphoreType.DMA((10,))],
+        compiler_params=pltpu.CompilerParams(vmem_limit_bytes=24 * 1024 * 1024),
         name="spread",
-    )(grads, vec, out, dx)
+    )(*(pltpu.with_memory_space_constraint(x, pltpu.VMEM) for x in (grads, vec, out, dx)))
     return out, dx, gq.T, gk.T, gv.T, bq, bv, go, bo, g1, s1, gi, bi, ge, be, g2, s2
 
 

time: 142 us -> 134 us (0.944)
  Pallas kernels: 141 us -> 133 us
    pallas_call x1, Pallas kernels: 136 us -> 129 us  [per_device(): pl.pallas_call(functools.partial(layer_kernel, cfg), out_shape=(pltpu.VME...]
where the time goes in v5:
time: 134 us; the launch traced here: 133 us
  Pallas kernels  133 us (99%)
    pallas_call x1, Pallas kernels, per_device(): pl.pallas_call(functools.partial(layer_kernel, cfg), out_shape=(pltpu.VME...  129 us
    pallas_call x1, Pallas kernels, per_device(): pl.pallas_call(functools.partial(spread_kernel, ml), out_shape=tuple((jax...  3.9 us

profile of v5, /device:TPU:0, one launch (start us, length us, event | category | flops | bytes accessed | tf_op | source)
XLA Modules:
  0.0 133.5 jit_solution(5937602648221155777)
XLA Ops:
  0.7 128.9 %layer.1 = (bf16[320,768]{1,0:T(8,128)(2,1)S(1)}, bf16[320,768]{1,0:T(8,128)(2,1)S(1)}, bf16[3,768,768]{2,1,0:T(8,128)(2,1)S(1)}, f32[16,768]{1,0:T(8,128)S(1)}) custom-call(bf16[2,160,768]{2,1,0:T(8,128)(2,1)} %bitcast.7, bf16[320,768]{1,0:T(8,128)(2,1)} %cot.1, bf16[192,768]{1,0:T(8,128)(2,1)} %bitcast.8, bf16[192,768]{1,0:T(8,128)(2,1)} %bitcast.9, ...), custom_call_target="tpu_custom_call" | custom-call | tf_op jit(solution)/shard_map/layer/pallas_call | solution.py:860
  129.6 3.9 %spread.1 = (bf16[320,768]{1,0:T(8,128)(2,1)}, bf16[320,768]{1,0:T(8,128)(2,1)}, f32[192,768]{1,0:T(8,128)}, f32[192,768]{1,0:T(8,128)}, f32[192,768]{1,0:T(8,12...) custom-call(bf16[3,768,768]{2,1,0:T(8,128)(2,1)S(1)} %get-tuple-elem, ...), custom_call_target="tpu_custom_call" | custom-call | tf_op jit(solution)/shard_map/spread/pallas_call | solution.py:880

commit v6 on v5

--- a/solution.py
+++ b/solution.py
@@ -33,8 +33,7 @@
 )
 SUMMED = (
     (0, 0, 192, "FS12"),
-    (0, 192, 128, "FSZd"),
-    (0, 320, 64, "FSZd"),
+    (0, 192, 192, "FSZd"),
     (1, 0, 192, "F12S"),
     (1, 192, 192, "F12S"),
     (2, 0, 192, "1F2S"),
@@ -42,71 +41,73 @@
 )
 PLAN = {
     "x0": {
-        0: (("az1", 0, 0), ("az1", 1, 0), ("s", 0, 1), ("az2", 1, 0), ("az1", 4, 0), ("az2", 0, 0), ("az1", 2, 0), ("s", 1, 1), ("f", 0, 1), ("s", 4, 1), ("f", 1, 1), ("az2", 4, 0), ("zf", 0, 0), ("az2", 2, 0), ("zf", 1, 0), ("s", 0, 2), ("s", 1, 2),),
+        0: (("az2", 0, 0), ("az1", 0, 0), ("az1", 1, 0), ("az2", 1, 0), ("zf", 0, 0), ("s", 0, 2), ("az1", 4, 0),),
     },
     "att": {
-        0: (("f", 4, 1), ("s", 2, 1),),
-        1: (("f", 1, 2), ("az1", 5, 0), ("s", 0, 3), ("s", 1, 3), ("f", 0, 2), ("az2", 3, 0), ("c", 1, 1), ("zf", 4, 0), ("s", 4, 2), ("d", 1, 1), ("c", 4, 1), ("c", 0, 1), ("zf", 2, 0), ("f", 2, 1),),
-        2: (("s", 2, 2), ("f", 1, 3), ("d", 0, 1), ("f", 0, 3), ("az2", 5, 0),),
-        3: (("c", 1, 2), ("c", 2, 1), ("c", 0, 2), ("az1", 3, 0), ("zf", 3, 0), ("f", 3, 2), ("s", 2, 3), ("az2", 6, 0), ("d", 4, 1),),
-        4: (("f", 2, 2), ("s", 4, 3), ("d", 1, 2), ("d", 0, 2), ("f", 4, 2), ("c", 1, 3),),
-        5: (("zf", 5, 0), ("c", 0, 3), ("d", 1, 3), ("f", 2, 3),),
-        6: (("f", 3, 1), ("d", 0, 3),),
-        7: (("f", 3, 3), ("c", 2, 2), ("c", 3, 2), ("f", 5, 1), ("az1", 6, 0), ("f", 5, 2),),
+        0: (("s", 0, 1), ("az2", 2, 0), ("s", 1, 1), ("f", 0, 2), ("zf", 1, 0), ("s", 1, 2), ("s", 0, 3), ("az2", 4, 0), ("f", 0, 1), ("s", 4, 1), ("f", 1, 2), ("az1", 2, 0),),
+        1: (("f", 1, 1), ("az1", 3, 0), ("s", 1, 3), ("az2", 3, 0), ("zf", 2, 0), ("f", 0, 3), ("c", 0, 1),),
+        2: (("d", 0, 1), ("s", 2, 2), ("s", 2, 1), ("f", 4, 1), ("zf", 4, 0), ("c", 1, 1), ("c", 0, 2), ("az2", 5, 0), ("d", 1, 1), ("f", 1, 3),),
+        3: (("s", 4, 2), ("c", 0, 3), ("f", 2, 2), ("d", 0, 2), ("c", 1, 2), ("f", 2, 1),),
+        4: (("c", 1, 3), ("zf", 3, 0), ("s", 2, 3), ("s", 4, 3), ("d", 1, 2), ("f", 3, 1), ("az1", 5, 0),),
+        5: (("f", 4, 2), ("c", 2, 1), ("d", 1, 3), ("az2", 6, 0), ("f", 3, 2), ("c", 4, 1), ("c", 2, 2), ("d", 0, 3),),
+        6: (("zf", 5, 0), ("d", 4, 1), ("f", 2, 3), ("f", 3, 3),),
+        7: (("az1", 6, 0), ("d", 2, 1), ("c", 3, 1), ("f", 5, 2),),
     },
     "n1": {
-        0: (("d", 2, 1), ("f", 4, 3), ("c", 3, 1), ("c", 2, 3), ("c", 4, 2),),
+        0: (("d", 2, 2), ("f", 5, 1),),
     },
     "up": {
-        0: (("zf", 6, 0), ("d", 3, 2),),
-        1: (("c", 6, 2), ("d", 3, 1), ("d", 2, 2), ("f", 5, 3), ("c", 3, 3),),
-        2: (("c", 5, 1),),
-        3: (("c", 6, 1), ("d", 3, 3), ("c", 5, 2), ("d", 2, 3), ("d", 4, 2),),
+        0: (("c", 4, 2), ("d", 3, 1), ("f", 4, 3), ("c", 2, 3), ("c", 3, 2), ("zf", 6, 0),),
+        1: (("f", 5, 3), ("c", 3, 3), ("c", 6, 2),),
+        2: (("d", 3, 2),),
+        3: (("c", 5, 1), ("d", 2, 3), ("d", 3, 3), ("c", 5, 2),),
     },
     "dn": {
-        0: (("c", 4, 3),),
-        1: (("d", 5, 1), ("d", 6, 1), ("d", 6, 2), ("c", 6, 3), ("c", 5, 3),),
-        2: (("d", 5, 2),),
-        3: (("d", 6, 3), ("d", 5, 3), ("d", 4, 3),),
+        0: (("c", 6, 1), ("d", 6, 2), ("c", 4, 3),),
+        1: (("d", 5, 1), ("c", 6, 3), ("c", 5, 3), ("d", 5, 2), ("d", 6, 1), ("d", 4, 2),),
+        3: (("d", 4, 3), ("d", 5, 3), ("d", 6, 3),),
     },
     "l2": {
     },
     "da": {
-        2: (("gFs", 4, 3), ("gFr", 6, 3), ("gFs", 3, 3),),
+        1: (("gFs", 5, 3),),
+        2: (("gFs", 3, 3),),
         3: (("gFs", 3, 1),),
     },
     "gwo": {
-        2: (("g1s", 6, 3),),
-        3: (("gFs", 4, 1),),
+        2: (("gFs", 2, 3),),
+        3: (("g1s", 5, 3),),
     },
     "dn2": {
-        0: (("gFs", 6, 3), ("g1s", 5, 3),),
-        1: (("gFs", 6, 1),),
-        2: (("gFs", 6, 2),),
+        0: (("g1s", 4, 3),),
+        1: (("gFs", 5, 1), ("g1s", 4, 1),),
+        3: (("gFs", 5, 0), ("gFs", 2, 1),),
     },
     "gwi": {
-        1: (("g1s", 5, 1),),
-        2: (("gFr", 6, 1),),
-        3: (("g1s", 6, 1), ("gFr", 4, 3), ("gFs", 6, 0), ("g1r", 5, 2), ("gFr", 6, 2),),
+        1: (("gFr", 5, 3), ("gFs", 5, 2),),
+        2: (("g1r", 4, 2), ("gFr", 3, 3), ("gFs", 4, 2), ("g1s", 3, 3),),
+        3: (("gFs", 2, 2), ("gFs", 3, 2),),
     },
     "l1b": {
-        0: (("gFs", 4, 2), ("g1r", 6, 2), ("gFs", 3, 0),),
     },
     "ab": {
-        1: (("gFr", 3, 3), ("gFs", 5, 2),),
-        2: (("gFs", 3, 2), ("g2s", 6, 2), ("gFs", 4, 0),),
-        4: (("gFs", 0, 3), ("g1s", 3, 3), ("gFs", 1, 3), ("g1r", 5, 0), ("gFs", 2, 3), ("g1s", 4, 3), ("gFs", 5, 0),),
-        6: (("gFs", 0, 1), ("gFs", 1, 1), ("gFr", 5, 2), ("g2s", 5, 2), ("gFr", 6, 0),),
-        7: (("gFr", 0, 3), ("gFr", 4, 1), ("g1r", 6, 0), ("gFs", 2, 1), ("gFr", 2, 3), ("gFr", 1, 3), ("gSs", 1, 3), ("g1s", 4, 1), ("gSs", 0, 3), ("g2r", 6, 0), ("gSs", 6, 0),),
+        0: (("gFr", 3, 1), ("gFs", 2, 0), ("gFr", 2, 3),),
+        2: (("gFr", 4, 2), ("gFs", 3, 0), ("g2s", 4, 2),),
+        4: (("gFs", 0, 3),),
+        5: (("gFs", 1, 3), ("gFr", 5, 2), ("g1r", 5, 2), ("g2s", 5, 2),),
+        6: (("gFs", 1, 1), ("gFr", 4, 0), ("gFr", 5, 1), ("g2r", 4, 0), ("gFs", 0, 1), ("g1s", 2, 3),),
+        7: (("gSs", 4, 0), ("gFr", 0, 3), ("gFr", 1, 3), ("gSs", 0, 3),),
     },
     "gwa": {
-        2: (("gFr", 0, 1), ("gFr", 3, 1), ("gFr", 4, 2), ("gSs", 0, 1),),
-        3: (("gSs", 2, 3), ("gFs", 1, 2), ("g1r", 4, 2), ("g2s", 4, 2), ("gFr", 1, 1), ("gFs", 0, 2), ("gFs", 2, 2),),
+        0: (("g1s", 3, 1), ("g1r", 4, 0), ("gFs", 4, 0),),
+        2: (("gSs", 1, 3), ("gFr", 2, 1), ("g1s", 2, 1),),
+        3: (("gFs", 0, 2), ("gFr", 3, 2), ("g1r", 3, 2), ("g2s", 3, 2), ("gFr", 1, 1), ("gFr", 2, 0), ("gSr", 4, 0), ("gFr", 2, 2), ("gFs", 1, 2),),
     },
     "fin": {
+        0: (("gS2s", 4, 0),),
     },
     "end": {
-        0: (("gFs", 2, 0), ("g1s", 3, 1), ("gFr", 4, 0), ("gFr", 3, 2), ("gSs", 1, 1), ("gFr", 1, 2), ("gFr", 5, 0), ("g2r", 5, 0), ("gSr", 6, 0), ("g1r", 3, 2), ("gSs", 5, 0), ("gSs", 1, 2), ("gFs", 1, 0), ("gFr", 2, 2), ("g2s", 3, 2), ("gFr", 3, 0), ("gSr", 1, 3), ("gFr", 0, 2), ("gSr", 0, 1), ("gFr", 2, 1), ("gFs", 0, 0), ("gSr", 0, 3), ("g1s", 0, 3), ("vs", 0, 0), ("vr", 0, 0), ("gS2s", 6, 0), ("vs", 1, 0), ("gSs", 2, 1), ("gSr", 5, 0), ("gSr", 1, 2), ("gS2s", 5, 0), ("gSr", 1, 1), ("gFr", 1, 0), ("gSs", 2, 2), ("g1r", 4, 0), ("gSr", 2, 3), ("gSs", 0, 2), ("gZs", 1, 2), ("g1s", 0, 1), ("g2r", 4, 0), ("gFr", 0, 0), ("gSs", 4, 0), ("g1r", 3, 0), ("gSs", 1, 0), ("gSs", 0, 0), ("gFr", 2, 0), ("gS2r", 5, 0), ("g2r", 3, 0), ("gSr", 0, 2), ("gSs", 3, 0), ("g1r", 0, 2), ("vr", 1, 0), ("vs", 2, 0), ("g2s", 0, 2), ("gSr", 2, 1), ("gZs", 1, 1), ("gSr", 4, 0), ("gS2s", 4, 0), ("gSr", 0, 0), ("gZs", 2, 1), ("gS2r", 6, 0), ("gSr", 3, 0), ("gS2s", 3, 0), ("gZs", 1, 3), ("g1r", 0, 0), ("gSs", 2, 0), ("gS2r", 4, 0), ("gSr", 1, 0), ("g2r", 0, 0), ("gZr", 1, 1), ("gZr", 1, 2), ("gS2s", 0, 0), ("gF2r", 5, 0), ("gSr", 2, 2), ("gZs", 2, 3), ("gS2r", 3, 0), ("gSr", 2, 0), ("gZr", 1, 3), ("vr", 2, 0), ("gC2r", 5, 0), ("gZs", 2, 2), ("vs", 3, 0), ("gZr", 2, 1), ("gS2s", 1, 0), ("gS2r", 0, 0), ("gF2r", 3, 0), ("vr", 3, 0), ("gF2r", 4, 0), ("gZr", 2, 2), ("gZr", 2, 3), ("gS2s", 2, 0), ("vs", 4, 0), ("gF2r", 6, 0), ("gd2Fr", 1, 0), ("gC2r", 6, 0), ("gd2Sr", 1, 0), ("gF2r", 1, 0), ("gF2r", 0, 0), ("gd2Fr", 2, 0), ("gC2r", 4, 0), ("gd2Sr", 2, 0), ("gF2r", 2, 0), ("gC2r", 0, 0), ("vr", 4, 0), ("gC2r", 3, 0), ("gC2r", 1, 0), ("gC2r", 2, 0),),
+        0: (("gFr", 3, 0), ("gFs", 0, 0), ("g1r", 2, 2), ("gFr", 0, 1), ("g1s", 5, 1), ("gFs", 1, 0), ("vs", 0, 0), ("gSs", 0, 1), ("g1r", 3, 0), ("gFr", 5, 0), ("gFr", 1, 2), ("g2s", 2, 2), ("gSs", 1, 2), ("gSr", 0, 3), ("gS2r", 4, 0), ("gFr", 0, 2), ("g2r", 3, 0), ("vr", 0, 0), ("gSs", 3, 0), ("gFr", 0, 0), ("g1r", 5, 0), ("gSr", 0, 1), ("gSs", 0, 0), ("gSs", 0, 2), ("g2r", 5, 0), ("vs", 1, 0), ("gSr", 1, 2), ("gFr", 1, 0), ("g1s", 0, 3), ("gSs", 5, 0), ("gSr", 3, 0), ("gSr", 1, 3), ("gZs", 1, 2), ("g1r", 2, 0), ("gSs", 1, 1), ("g2r", 2, 0), ("gSs", 2, 0), ("g1s", 0, 1), ("gS2s", 3, 0), ("gSs", 1, 0), ("gSr", 0, 2), ("vr", 1, 0), ("g1r", 0, 2), ("gSr", 5, 0), ("gSr", 0, 0), ("gS2s", 5, 0), ("vs", 2, 0), ("g2s", 0, 2), ("gSr", 1, 1), ("gSr", 2, 0), ("gZs", 1, 1), ("gS2s", 2, 0), ("gF2r", 4, 0), ("g1r", 0, 0), ("gS2r", 3, 0), ("gZs", 1, 3), ("gSr", 1, 0), ("gS2r", 5, 0), ("gZr", 1, 1), ("g2r", 0, 0), ("gZr", 1, 2), ("gS2s", 0, 0), ("gS2r", 2, 0), ("gF2r", 3, 0), ("gZr", 1, 3), ("gS2s", 1, 0), ("gF2r", 5, 0), ("vr", 2, 0), ("vs", 3, 0), ("gS2r", 0, 0), ("vr", 3, 0), ("vs", 4, 0), ("gd2Fr", 1, 0), ("gF2r", 2, 0), ("gC2r", 5, 0), ("gd2Sr", 1, 0), ("gF2r", 1, 0), ("gF2r", 0, 0), ("gC2r", 2, 0), ("gC2r", 4, 0), ("vr", 4, 0), ("gC2r", 3, 0), ("gC2r", 1, 0), ("gC2r", 0, 0),),
     },
 }
 V_OB, V_G1, V_S1, V_EB, V_G2, V_S2 = 8, 9, 10, 11, 12, 13
@@ -135,7 +136,7 @@
     out_ref, dx_ref, whole, vec_ref,
     wbuf, bias, xs, cots, qkv, ka, ks, prob, mask, acc, tmp, nh1, r1,
     nb, nhalf, af, asib, al, gp, g, sg, di, fg,
-    gr, rf, rz, rs, rx, vrecv, vin,
+    gr, rf, rz, rs, rx, vrecv, vin, short,
     seg, live, *rest,
 ):
     n_dp, d, seq, rows = cfg["dp"], cfg["d"], cfg["seq"], cfg["rows"]
@@ -202,9 +203,14 @@
 
     pending = []
 
-    def send(make):
+    def send(make, group="early"):
         remote(*make()).start()
-        pending.append(make)
+        pending.append((group, make))
+
+    def flush(group):
+        for item in [item for item in pending if item[0] == group]:
+            remote(*item[1]()).wait_send()
+            pending.remove(item)
 
     small = rest[:9]
     loc_sem, ag_s, ag_r, gr_s, gr_r, x_s, x_r, b_s, b_r, v_s, v_r, e_s, e_r = rest[9:]
@@ -308,7 +314,7 @@
         return gr_s.at[p, slot], gr_r.at[p, slot]
 
     def g_send(p, slot, pair, dev):
-        send(lambda: (*pair(), *g_sem(p, slot), dev))
+        send(lambda: (*pair(), *g_sem(p, slot), dev), p if slot < 11 else "late")
 
     def g_wait(p, slot, dst):
         remote(dst, dst, *g_sem(p, slot), (dp, z1)).wait_recv()
@@ -420,21 +426,31 @@
         else:
             g_wait(p, 12, final(p, 1, True))
         g_send(p, 13, lambda: (final(p, 0),) * 2, (p_c, z))
+        flush(p)
 
     def g_c2r(p, _):
         g_wait(p, 13, final(p, "core", True))
 
     partners = [(p_c, z), (p_f, z), (p_s, z), (dp, z1), (dp, z2)] + [(e, z) for e in extra]
 
+    def v_half(mine):
+        return vec_ref.at[pl.ds(pl.multiple_of(8 * (c if mine else 1 - c), 8), 8)]
+
     def v_copy(j):
-        return remote(vec_ref, vrecv.at[j], v_s.at[j], v_r.at[j], partners[j])
+        return remote(v_half(j > 0), vrecv.at[j], v_s.at[j], v_r.at[j], partners[j])
 
     def v_send(j, _):
         v_copy(j).start()
 
+    def v_back():
+        return remote(v_half(True), v_half(True), v_s.at[len(partners)], v_r.at[len(partners)], (p_c, z))
+
     def v_recv(j, _):
         v_copy(j).wait()
-        vec_ref[...] += vrecv[j]
+        half_ref = v_half(True)
+        half_ref[...] = half_ref[...] + vrecv[j]
+        if j == len(partners) - 1:
+            v_back().start()
 
     events = {
         "az1": a_z1, "az2": a_z2, "zf": a_zf, "s": a_s, "f": a_f, "c": a_c, "d": a_d,
@@ -462,8 +478,14 @@
     for j, ref in enumerate(small[2:]):
         vin[pl.ds(j + 1, 1), :] = ref[...].astype(F32).reshape(1, d)
     bias[z] = vin[...]
+    third = d // 3
+    short[z] = jnp.zeros((8, third), F32)
+    short[z, pl.ds(0, 1), pl.ds(0, ml)] = vin[pl.ds(0, 1), pl.ds(0, ml)]
+    short[z, pl.ds(1, 1), pl.ds(0, ml)] = vin[pl.ds(0, 1), pl.ds(2 * ml, ml)]
+    for j in range(3):
+        short[z, pl.ds(2 + j, 1), :] = vin[pl.ds(1, 1), pl.ds(j * third, third)]
     for j, zz in enumerate((z1, z2, z3)):
-        send(lambda j=j, zz=zz: (vin, bias.at[z], b_s.at[j], b_r.at[j], (dp, zz)))
+        send(lambda j=j, zz=zz: (short.at[z], short.at[z], b_s.at[j], b_r.at[j], (dp, zz)))
     core_send(X_TOK, lambda: (tok, xs.at[pl.ds(rows, rows)]))
     for cp in seg_loads:
         cp.wait()
@@ -488,7 +510,12 @@
             @pl.when((i == 1) & (r == 0))
             def _():
                 for j, zz in enumerate((z1, z2, z3)):
-                    remote(vin, bias.at[zz], b_s.at[j], b_r.at[j], (dp, zz)).wait_recv()
+                    remote(short.at[zz], short.at[zz], b_s.at[j], b_r.at[j], (dp, zz)).wait_recv()
+                    bias[zz] = jnp.zeros((8, d), F32)
+                    bias[zz, pl.ds(0, 1), pl.ds(0, ml)] = short[zz, pl.ds(0, 1), pl.ds(0, ml)]
+                    bias[zz, pl.ds(0, 1), pl.ds(2 * ml, ml)] = short[zz, pl.ds(1, 1), pl.ds(0, ml)]
+                    for n in range(3):
+                        bias[zz, pl.ds(1, 1), pl.ds(n * third, third)] = short[zz, pl.ds(2 + n, 1), :]
 
             x_row = xs[r]
             bias_rows = bias[t].astype(BF)[:, : 3 * ml]
@@ -744,13 +771,7 @@
     lax.fori_loop(0, tl // rb, finish, 0)
 
 
-    once("end")
-    for j in range(5, len(partners)):
-        v_send(j, 0)
-        v_recv(j, 0)
-
-    for make in pending:
-        remote(*make()).wait_send()
+    flush("early")
 
     def sent(k, carry):
         t = shard_of(k)
@@ -765,15 +786,27 @@
     for j in range(tl // rb):
         g_copy(j).wait_send()
 
+    once("end")
+    for j in range(5, len(partners)):
+        v_send(j, 0)
+        v_recv(j, 0)
+    other_half = v_half(False)
+    remote(other_half, other_half, v_s.at[len(partners)], v_r.at[len(partners)], (p_c, z)).wait_recv()
+    v_back().wait_send()
+
+    flush("late")
+    assert not pending
+
 
 def spread_kernel(
     ml, grads, vec, out_in, dx_in,
     out_ref, dx_ref, gq, gk, gv, go, gi, ge, bq, bv, bo, g1, s1, bi, be, g2, s2,
-    wide_v, sem,
+    wide_v, *rest,
 ):
     z = lax.axis_index("mp")
     n = 2 * ml
     outs = []
+    small, sem = rest[:9], rest[9]
 
     def put(src, dst):
         cp = pltpu.make_async_copy(src, dst, sem.at[len(outs)])
@@ -782,6 +815,11 @@
 
     put(out_in, out_ref)
     put(dx_in, dx_ref)
+    picks = [(z, 0, ml, bq), (z, 2 * ml, ml, bv), (4 + z, 0, 4 * ml, bi)]
+    picks += [
+        (row, 0, 4 * ml, ref)
+        for row, ref in ((V_OB, bo), (V_G1, g1), (V_S1, s1), (V_EB, be), (V_G2, g2), (V_S2, s2))
+    ]
     steps = [(piece, lo, [(ref, lo, n)]) for piece, ref in ((1, gi), (2, ge)) for lo in (0, n)]
     steps += [(0, 0, [(gq, 0, ml), (gk, 0, ml)]), (0, n, [(gv, 0, ml), (go, 0, ml)])]
     for piece, lo, refs in steps:
@@ -790,11 +828,9 @@
         for ref, row, m in refs:
             put(wide_v.at[piece, pl.ds(at, m)], ref.at[pl.ds(row, m)])
             at += m
-    bq[...] = vec[pl.ds(z, 1), pl.ds(0, ml)].reshape(ml)
-    bv[...] = vec[pl.ds(z, 1), pl.ds(2 * ml, ml)].reshape(ml)
-    bi[...] = vec[pl.ds(4 + z, 1), :].reshape(4 * ml)
-    for row, ref in ((V_OB, bo), (V_G1, g1), (V_S1, s1), (V_EB, be), (V_G2, g2), (V_S2, s2)):
-        ref[...] = vec[pl.ds(row, 1), :].reshape(4 * ml)
+    for (row, lo, m, ref), buf in zip(picks, small):
+        buf[...] = vec[pl.ds(row, 1), pl.ds(lo, m)].reshape(m)
+        put(buf, ref)
     for cp in outs:
         cp.wait()
 
@@ -813,7 +849,7 @@
     half, qtr, eig = d // 2, d // 4, d // 8
     bits = n_dp.bit_length() - 1
     n_extra = max(bits - 3, 1)
-    n_vec = bits + 2
+    n_vec = bits + 3
     cfg = {"dp": n_dp, "d": d, "seq": seq, "rows": rows}
     vmem = pl.BlockSpec(memory_space=pltpu.VMEM)
     hbm = pl.BlockSpec(memory_space=pl.ANY)
@@ -846,8 +882,9 @@
         pltpu.VMEM((sum(z_rows(len(SUMMED) - 1, 2)), d), BF),
         pltpu.VMEM((3, 4, eig, d), BF),
         pltpu.VMEM((3, n_extra, eig, d), BF) if bits > 3 else pltpu.VMEM((1, 1, 16, 128), BF),
-        pltpu.VMEM((n_vec, 16, d), F32),
+        pltpu.VMEM((n_vec - 1, 8, d), F32),
         pltpu.VMEM((8, d), F32),
+        pltpu.VMEM((4, 8, d // 3), F32),
         pltpu.VMEM((seq_rows, seq), jnp.int32),
         pltpu.VMEM((seq_rows, seq), jnp.int32),
     ]
@@ -888,8 +925,10 @@
             + [((d,), F32)] * 7
         ),
         in_specs=[vmem] * 4,
-        out_specs=(hbm,) * 8 + (vmem,) * 9,
-        scratch_shapes=[pltpu.VMEM((3, d, d), F32), pltpu.SemaphoreType.DMA((10,))],
+        out_specs=(hbm,) * 17,
+        scratch_shapes=[pltpu.VMEM((3, d, d), F32)]
+        + [pltpu.VMEM((n,), F32) for n in (ml, ml, ff, d, d, d, d, d, d)]
+        + [pltpu.SemaphoreType.DMA((19,))],
         compiler_params=pltpu.CompilerParams(vmem_limit_bytes=24 * 1024 * 1024),
         name="spread",
     )(*(pltpu.with_memory_space_constraint(x, pltpu.VMEM) for x in (grads, vec, out, dx)))

time: 134 us -> 131 us (0.978)
  Pallas kernels: 133 us -> 130 us
    pallas_call x1, Pallas kernels: 129 us -> 127 us  [per_device(): pl.pallas_call(functools.partial(layer_kernel, cfg), out_shape=(pltpu.VME...]
where the time goes in v6:
time: 131 us
  Pallas kernels  130 us (99%)
    pallas_call x1, Pallas kernels, per_device(): pl.pallas_call(functools.partial(layer_kernel, cfg), out_shape=(pltpu.VME...  127 us
    pallas_call x1, Pallas kernels, per_device(): pl.pallas_call(functools.partial(spread_kernel, ml), out_shape=tuple((jax...  3.38 us

profile of v6, /device:TPU:0, one launch (start us, length us, event | category | flops | bytes accessed | tf_op | source)
XLA Modules:
  0.0 130.7 jit_solution(4352997247185392458)
XLA Ops:
  0.7 126.6 %layer.1 = (bf16[320,768]{1,0:T(8,128)(2,1)S(1)}, bf16[320,768]{1,0:T(8,128)(2,1)S(1)}, bf16[3,768,768]{2,1,0:T(8,128)(2,1)S(1)}, f32[16,768]{1,0:T(8,128)S(1)}) custom-call(bf16[2,160,768]{2,1,0:T(8,128)(2,1)} %bitcast.7, bf16[320,768]{1,0:T(8,128)(2,1)} %cot.1, bf16[192,768]{1,0:T(8,128)(2,1)} %bitcast.8, bf16[192,768]{1,0:T(8,128)(2,1)} %bitcast.9, ...), custom_call_target="tpu_custom_call" | custom-call | tf_op jit(solution)/shard_map/layer/pallas_call | solution.py:897
  127.3 3.4 %spread.1 = (bf16[320,768]{1,0:T(8,128)(2,1)}, bf16[320,768]{1,0:T(8,128)(2,1)}, f32[192,768]{1,0:T(8,128)}, f32[192,768]{1,0:T(8,128)}, f32[192,768]{1,0:T(8,12...) custom-call(bf16[3,768,768]{2,1,0:T(8,128)(2,1)S(1)} %get-tuple-elem, ...), custom_call_target="tpu_custom_call" | custom-call | tf_op jit(solution)/shard_map/spread/pallas_call | solution.py:917

commit v7 on v6

--- a/solution.py
+++ b/solution.py
@@ -33,7 +33,7 @@
 )
 SUMMED = (
     (0, 0, 192, "FS12"),
-    (0, 192, 192, "FSZd"),
+    (0, 192, 192, "FS12"),
     (1, 0, 192, "F12S"),
     (1, 192, 192, "F12S"),
     (2, 0, 192, "1F2S"),
@@ -51,63 +51,62 @@
         4: (("c", 1, 3), ("zf", 3, 0), ("s", 2, 3), ("s", 4, 3), ("d", 1, 2), ("f", 3, 1), ("az1", 5, 0),),
         5: (("f", 4, 2), ("c", 2, 1), ("d", 1, 3), ("az2", 6, 0), ("f", 3, 2), ("c", 4, 1), ("c", 2, 2), ("d", 0, 3),),
         6: (("zf", 5, 0), ("d", 4, 1), ("f", 2, 3), ("f", 3, 3),),
-        7: (("az1", 6, 0), ("d", 2, 1), ("c", 3, 1), ("f", 5, 2),),
+        7: (("d", 2, 1), ("c", 3, 1), ("f", 5, 2), ("az1", 6, 0),),
     },
     "n1": {
         0: (("d", 2, 2), ("f", 5, 1),),
     },
     "up": {
-        0: (("c", 4, 2), ("d", 3, 1), ("f", 4, 3), ("c", 2, 3), ("c", 3, 2), ("zf", 6, 0),),
-        1: (("f", 5, 3), ("c", 3, 3), ("c", 6, 2),),
+        0: (("c", 4, 2), ("d", 3, 1), ("f", 4, 3), ("c", 3, 2), ("zf", 6, 0),),
+        1: (("c", 2, 3), ("c", 3, 3), ("c", 6, 2), ("f", 5, 3),),
         2: (("d", 3, 2),),
-        3: (("c", 5, 1), ("d", 2, 3), ("d", 3, 3), ("c", 5, 2),),
+        3: (("d", 3, 3), ("c", 5, 1), ("d", 2, 3), ("c", 5, 2),),
     },
     "dn": {
         0: (("c", 6, 1), ("d", 6, 2), ("c", 4, 3),),
         1: (("d", 5, 1), ("c", 6, 3), ("c", 5, 3), ("d", 5, 2), ("d", 6, 1), ("d", 4, 2),),
-        3: (("d", 4, 3), ("d", 5, 3), ("d", 6, 3),),
+        3: (("d", 4, 3), ("d", 6, 3), ("d", 5, 3),),
     },
     "l2": {
     },
     "da": {
         1: (("gFs", 5, 3),),
-        2: (("gFs", 3, 3),),
+        2: (("gFs", 3, 3), ("gFr", 5, 3),),
         3: (("gFs", 3, 1),),
     },
     "gwo": {
-        2: (("gFs", 2, 3),),
-        3: (("g1s", 5, 3),),
+        2: (("gFs", 2, 3), ("g1s", 5, 3),),
+        3: (("gFr", 3, 3), ("g1r", 4, 2), ("gFs", 4, 2),),
     },
     "dn2": {
         0: (("g1s", 4, 3),),
         1: (("gFs", 5, 1), ("g1s", 4, 1),),
-        3: (("gFs", 5, 0), ("gFs", 2, 1),),
+        3: (("g1s", 3, 3), ("gFs", 5, 0),),
     },
     "gwi": {
-        1: (("gFr", 5, 3), ("gFs", 5, 2),),
-        2: (("g1r", 4, 2), ("gFr", 3, 3), ("gFs", 4, 2), ("g1s", 3, 3),),
-        3: (("gFs", 2, 2), ("gFs", 3, 2),),
     },
     "l1b": {
+        0: (("gFs", 3, 2), ("gFr", 5, 1), ("gFs", 5, 2), ("gFs", 2, 0),),
     },
     "ab": {
-        0: (("gFr", 3, 1), ("gFs", 2, 0), ("gFr", 2, 3),),
-        2: (("gFr", 4, 2), ("gFs", 3, 0), ("g2s", 4, 2),),
-        4: (("gFs", 0, 3),),
-        5: (("gFs", 1, 3), ("gFr", 5, 2), ("g1r", 5, 2), ("g2s", 5, 2),),
-        6: (("gFs", 1, 1), ("gFr", 4, 0), ("gFr", 5, 1), ("g2r", 4, 0), ("gFs", 0, 1), ("g1s", 2, 3),),
-        7: (("gSs", 4, 0), ("gFr", 0, 3), ("gFr", 1, 3), ("gSs", 0, 3),),
+        1: (("gFs", 2, 2), ("g1r", 4, 0), ("gFr", 4, 2),),
+        2: (("g2s", 4, 2),),
+        3: (("gFs", 3, 0), ("g1s", 5, 1),),
+        4: (("gFs", 2, 1), ("gFr", 3, 2),),
+        5: (("gFs", 1, 3), ("gFr", 2, 3), ("g1r", 3, 2),),
+        6: (("gFs", 1, 1),),
+        7: (("g1s", 2, 3), ("gFs", 0, 1), ("gFr", 4, 0),),
     },
     "gwa": {
-        0: (("g1s", 3, 1), ("g1r", 4, 0), ("gFs", 4, 0),),
-        2: (("gSs", 1, 3), ("gFr", 2, 1), ("g1s", 2, 1),),
-        3: (("gFs", 0, 2), ("gFr", 3, 2), ("g1r", 3, 2), ("g2s", 3, 2), ("gFr", 1, 1), ("gFr", 2, 0), ("gSr", 4, 0), ("gFr", 2, 2), ("gFs", 1, 2),),
+        0: (("gFs", 4, 0), ("gFr", 3, 1), ("g1s", 3, 1),),
+        1: (("gFs", 0, 3), ("g2s", 3, 2),),
+        2: (("g2r", 4, 0), ("gSs", 4, 0), ("gFr", 1, 3), ("gFr", 5, 2), ("g1r", 5, 2), ("g2s", 5, 2), ("gSs", 1, 3),),
+        3: (("gFs", 0, 2), ("gFr", 3, 0), ("gFr", 2, 1), ("gFs", 1, 2), ("gFr", 2, 2),),
     },
     "fin": {
-        0: (("gS2s", 4, 0),),
     },
     "end": {
-        0: (("gFr", 3, 0), ("gFs", 0, 0), ("g1r", 2, 2), ("gFr", 0, 1), ("g1s", 5, 1), ("gFs", 1, 0), ("vs", 0, 0), ("gSs", 0, 1), ("g1r", 3, 0), ("gFr", 5, 0), ("gFr", 1, 2), ("g2s", 2, 2), ("gSs", 1, 2), ("gSr", 0, 3), ("gS2r", 4, 0), ("gFr", 0, 2), ("g2r", 3, 0), ("vr", 0, 0), ("gSs", 3, 0), ("gFr", 0, 0), ("g1r", 5, 0), ("gSr", 0, 1), ("gSs", 0, 0), ("gSs", 0, 2), ("g2r", 5, 0), ("vs", 1, 0), ("gSr", 1, 2), ("gFr", 1, 0), ("g1s", 0, 3), ("gSs", 5, 0), ("gSr", 3, 0), ("gSr", 1, 3), ("gZs", 1, 2), ("g1r", 2, 0), ("gSs", 1, 1), ("g2r", 2, 0), ("gSs", 2, 0), ("g1s", 0, 1), ("gS2s", 3, 0), ("gSs", 1, 0), ("gSr", 0, 2), ("vr", 1, 0), ("g1r", 0, 2), ("gSr", 5, 0), ("gSr", 0, 0), ("gS2s", 5, 0), ("vs", 2, 0), ("g2s", 0, 2), ("gSr", 1, 1), ("gSr", 2, 0), ("gZs", 1, 1), ("gS2s", 2, 0), ("gF2r", 4, 0), ("g1r", 0, 0), ("gS2r", 3, 0), ("gZs", 1, 3), ("gSr", 1, 0), ("gS2r", 5, 0), ("gZr", 1, 1), ("g2r", 0, 0), ("gZr", 1, 2), ("gS2s", 0, 0), ("gS2r", 2, 0), ("gF2r", 3, 0), ("gZr", 1, 3), ("gS2s", 1, 0), ("gF2r", 5, 0), ("vr", 2, 0), ("vs", 3, 0), ("gS2r", 0, 0), ("vr", 3, 0), ("vs", 4, 0), ("gd2Fr", 1, 0), ("gF2r", 2, 0), ("gC2r", 5, 0), ("gd2Sr", 1, 0), ("gF2r", 1, 0), ("gF2r", 0, 0), ("gC2r", 2, 0), ("gC2r", 4, 0), ("vr", 4, 0), ("gC2r", 3, 0), ("gC2r", 1, 0), ("gC2r", 0, 0),),
+        0: (("g1r", 3, 0), ("gFs", 0, 0), ("vs", 0, 0), ("gFr", 5, 0), ("g2r", 3, 0), ("gFr", 0, 3), ("gSs", 3, 0), ("gSr", 1, 3), ("vr", 0, 0), ("g1s", 2, 1), ("gSr", 4, 0), ("gFr", 0, 1), ("gFs", 1, 0), ("gFr", 1, 1), ("gFr", 1, 2), ("gSs", 0, 3), ("gS2s", 4, 0), ("gSs", 1, 1), ("g1r", 2, 2), ("g2s", 2, 2), ("gSs", 0, 1), ("vs", 1, 0), ("gFr", 2, 0), ("g1r", 5, 0), ("gSs", 1, 2), ("gFr", 0, 0), ("g2r", 5, 0), ("gSs", 5, 0), ("gSr", 3, 0), ("gS2s", 3, 0), ("g1s", 1, 3), ("gFr", 0, 2), ("gSs", 0, 2), ("gSr", 1, 1), ("gFr", 1, 0), ("gSr", 0, 3), ("g1r", 2, 0), ("g1s", 0, 3), ("gSs", 1, 0), ("gSs", 0, 0), ("gS2r", 4, 0), ("g1s", 1, 1), ("gSr", 5, 0), ("g2r", 2, 0), ("vr", 1, 0), ("gSr", 1, 2), ("gSs", 2, 0), ("vs", 2, 0), ("g1r", 1, 2), ("g2s", 1, 2), ("gSr", 0, 1), ("gS2s", 5, 0), ("gSr", 0, 2), ("g1r", 0, 2), ("g1s", 0, 1), ("gS2r", 3, 0), ("g2s", 0, 2), ("gSr", 2, 0), ("gSr", 1, 0), ("gSr", 0, 0), ("g1r", 1, 0), ("gF2r", 4, 0), ("gS2s", 2, 0), ("gS2r", 5, 0), ("vr", 2, 0), ("g2r", 1, 0), ("gS2s", 1, 0), ("vs", 3, 0), ("gC2r", 4, 0), ("gF2r", 3, 0), ("gS2r", 2, 0), ("g1r", 0, 0), ("gC2r", 3, 0), ("g2r", 0, 0), ("gS2s", 0, 0), ("gF2r", 5, 0), ("gS2r", 1, 0), ("vr", 3, 0), ("vs", 4, 0), ("gS2r", 0, 0), ("gF2r", 2, 0), ("vr", 4, 0), ("gC2r", 5, 0), ("gC2r", 2, 0), ("gF2r", 1, 0), ("gF2r", 0, 0), ("gC2r", 1, 0), ("gC2r", 0, 0),),
     },
 }
 V_OB, V_G1, V_S1, V_EB, V_G2, V_S2 = 8, 9, 10, 11, 12, 13

time: 131 us -> 130 us (level)
  no operation moved by 1% of the time
where the time goes in v7:
time: 130 us
  Pallas kernels  129 us (99%)
    pallas_call x1, Pallas kernels, per_device(): pl.pallas_call(functools.partial(layer_kernel, cfg), out_shape=(pltpu.VME...  126 us
    pallas_call x1, Pallas kernels, per_device(): pl.pallas_call(functools.partial(spread_kernel, ml), out_shape=tuple((jax...  3.38 us

profile of v7, /device:TPU:0, one launch (start us, length us, event | category | flops | bytes accessed | tf_op | source)
XLA Modules:
  0.0 130.0 jit_solution(18143340118462065130)
XLA Ops:
  0.7 126.0 %layer.1 = (bf16[320,768]{1,0:T(8,128)(2,1)S(1)}, bf16[320,768]{1,0:T(8,128)(2,1)S(1)}, bf16[3,768,768]{2,1,0:T(8,128)(2,1)S(1)}, f32[16,768]{1,0:T(8,128)S(1)}) custom-call(bf16[2,160,768]{2,1,0:T(8,128)(2,1)} %bitcast.7, bf16[320,768]{1,0:T(8,128)(2,1)} %cot.1, bf16[192,768]{1,0:T(8,128)(2,1)} %bitcast.8, bf16[192,768]{1,0:T(8,128)(2,1)} %bitcast.9, ...), custom_call_target="tpu_custom_call" | custom-call | tf_op jit(solution)/shard_map/layer/pallas_call | solution.py:896
  126.6 3.4 %spread.1 = (bf16[320,768]{1,0:T(8,128)(2,1)}, bf16[320,768]{1,0:T(8,128)(2,1)}, f32[192,768]{1,0:T(8,128)}, f32[192,768]{1,0:T(8,128)}, f32[192,768]{1,0:T(8,12...) custom-call(bf16[3,768,768]{2,1,0:T(8,128)(2,1)S(1)} %get-tuple-elem, ...), custom_call_target="tpu_custom_call" | custom-call | tf_op jit(solution)/shard_map/spread/pallas_call | solution.py:916

commit v8 on v7

--- a/solution.py
+++ b/solution.py
@@ -319,7 +319,7 @@
         remote(dst, dst, *g_sem(p, slot), (dp, z1)).wait_recv()
 
     def add_into(dst, src, n):
-        m = 48 if n % 48 == 0 else (32 if n % 32 == 0 else 16)
+        m = 96 if n % 96 == 0 else (48 if n % 48 == 0 else (32 if n % 32 == 0 else 16))
 
         def blk(j, carry):
             sl = pl.ds(pl.multiple_of(j * m, 16), m)
@@ -819,17 +819,15 @@
         (row, 0, 4 * ml, ref)
         for row, ref in ((V_OB, bo), (V_G1, g1), (V_S1, s1), (V_EB, be), (V_G2, g2), (V_S2, s2))
     ]
-    steps = [(piece, lo, [(ref, lo, n)]) for piece, ref in ((1, gi), (2, ge)) for lo in (0, n)]
-    steps += [(0, 0, [(gq, 0, ml), (gk, 0, ml)]), (0, n, [(gv, 0, ml), (go, 0, ml)])]
-    for piece, lo, refs in steps:
-        wide_v[piece, pl.ds(lo, n), :] = grads[piece, pl.ds(lo, n), :].astype(F32)
-        at = lo
-        for ref, row, m in refs:
-            put(wide_v.at[piece, pl.ds(at, m)], ref.at[pl.ds(row, m)])
-            at += m
-    for (row, lo, m, ref), buf in zip(picks, small):
-        buf[...] = vec[pl.ds(row, 1), pl.ds(lo, m)].reshape(m)
-        put(buf, ref)
+    steps = [(0, j * ml, ref, 0, ml) for j, ref in enumerate((gq, gk, gv, go))]
+    steps += [(piece, lo, ref, lo, n) for piece, ref in ((1, gi), (2, ge)) for lo in (0, n)]
+    for count, (piece, lo, ref, row, m) in enumerate(steps):
+        wide_v[piece, pl.ds(lo, m), :] = grads[piece, pl.ds(lo, m), :].astype(F32)
+        put(wide_v.at[piece, pl.ds(lo, m)], ref.at[pl.ds(row, m)])
+        if count == 3:
+            for (src_row, src_lo, width, dst), buf in zip(picks, small):
+                buf[...] = vec[pl.ds(src_row, 1), pl.ds(src_lo, width)].reshape(width)
+                put(buf, dst)
     for cp in outs:
         cp.wait()
 

time: 130 us -> 130 us (level)
  no operation moved by 1% of the time
where the time goes in v8:
time: 130 us
  Pallas kernels  129 us (99%)
    pallas_call x1, Pallas kernels, per_device(): pl.pallas_call(functools.partial(layer_kernel, cfg), out_shape=(pltpu.VME...  126 us
    pallas_call x1, Pallas kernels, per_device(): pl.pallas_call(functools.partial(spread_kernel, ml), out_shape=tuple((jax...  3.42 us

profile of v8, /device:TPU:0, one launch (start us, length us, event | category | flops | bytes accessed | tf_op | source)
XLA Modules:
  0.0 130.1 jit_solution(2903128360794944174)
XLA Ops:
  0.7 126.0 %layer.1 = (bf16[320,768]{1,0:T(8,128)(2,1)S(1)}, bf16[320,768]{1,0:T(8,128)(2,1)S(1)}, bf16[3,768,768]{2,1,0:T(8,128)(2,1)S(1)}, f32[16,768]{1,0:T(8,128)S(1)}) custom-call(bf16[2,160,768]{2,1,0:T(8,128)(2,1)} %bitcast.7, bf16[320,768]{1,0:T(8,128)(2,1)} %cot.1, bf16[192,768]{1,0:T(8,128)(2,1)} %bitcast.8, bf16[192,768]{1,0:T(8,128)(2,1)} %bitcast.9, ...), custom_call_target="tpu_custom_call" | custom-call | tf_op jit(solution)/shard_map/layer/pallas_call | solution.py:894
  126.6 3.4 %spread.1 = (bf16[320,768]{1,0:T(8,128)(2,1)}, bf16[320,768]{1,0:T(8,128)(2,1)}, f32[192,768]{1,0:T(8,128)}, f32[192,768]{1,0:T(8,128)}, f32[192,768]{1,0:T(8,12...) custom-call(bf16[3,768,768]{2,1,0:T(8,128)(2,1)S(1)} %get-tuple-elem, ...), custom_call_target="tpu_custom_call" | custom-call | tf_op jit(solution)/shard_map/spread/pallas_call | solution.py:914
